TPU v7x, 32 devices: a whole 2x2x4 slice. The times are simulated.
32 devices in a mesh: dp: 4 (over x, core), seq: 2 (over y), tap: 4 (over z).
Axes of the slice: x: 2, y: 2, z: 4, core: 2. Of those that a mesh axis runs over, the one named last changes fastest.
Arguments:
- inputs: bfloat16 [64, 512, 512], P(('dp', 'tap'), 'seq'), may hold values from -6 to 6
- targets: int32 [64, 512], P(('dp', 'tap'), 'seq'), may hold values from 0 to 3
- masked: int32 [64, 512], P(('dp', 'tap'), 'seq'), may hold values from 0 to 1, as said below
- conv_weight: bfloat16 [2, 9, 512, 512], P(None, None, 'tap'), may hold values from -0.09375 to 0.09375
- conv_bias: float32 [2, 512], replicated, may hold values from -3 to 3
- gains: float32 [2, 2, 512], replicated, may hold values from 0.5 to 1.5
- shifts: float32 [2, 2, 512], replicated, may hold values from -2 to 2
- in_weight: bfloat16 [2, 512, 2048], P(None, None, ('dp', 'seq', 'tap')), may hold values from -0.25 to 0.25
- in_bias: float32 [2, 2048], replicated, may hold values from -3 to 3
- out_weight: bfloat16 [2, 2048, 512], P(None, ('dp', 'seq', 'tap')), may hold values from -0.125 to 0.125
- out_bias: float32 [2, 512], replicated, may hold values from -2 to 2
- head_weight: float32 [512, 4], replicated, may hold values from -0.25 to 0.25
Outputs:
- final_state: bfloat16 [64, 512, 512], P(('dp', 'tap'), 'seq')
- grad_inputs: bfloat16 [64, 512, 512], P(('dp', 'tap'), 'seq')
- grad_conv_weight: float32 [2, 9, 512, 512], P(None, None, 'tap')
- grad_conv_bias: float32 [2, 512], replicated
- grad_gains: float32 [2, 2, 512], replicated
- grad_shifts: float32 [2, 2, 512], replicated
- grad_in_weight: float32 [2, 512, 2048], P(None, None, ('dp', 'seq', 'tap'))
- grad_in_bias: float32 [2, 2048], replicated
- grad_out_weight: float32 [2, 2048, 512], P(None, ('dp', 'seq', 'tap'))
- grad_out_bias: float32 [2, 512], replicated
- grad_head_weight: float32 [512, 4], replicated
- loss: float32 [], replicated
Inputs may be any that keep to these rules, and one draw needn't show every extreme that they name: Every window has at least one masked position; the masked share of a window varies from window to window, from 5 up to 50 percent.
All inputs are finite; a program needn't handle non-finite values.
Results may differ from a plain program's by a relative error of at most 0.013.
Values may be sent and summed in bfloat16 or wider, within the bound.
No kernel may reach another device: no remote copies, remote signals or barrier semaphores. Data moves between devices by JAX's collectives and lax.ppermute only.
A program may use at most 192 MiB of HBM per device.

v0:
```python
import functools

import jax
import jax.numpy as jnp
import numpy as np
from jax import lax
from jax.experimental import pallas as pl
from jax.experimental.pallas import tpu as pltpu
from jax.sharding import PartitionSpec as P

FIRST_DILATION = 4
SECOND_DILATION = 32
EPSILON = 1e-05
HIGHEST_PRECISION = lax.Precision.HIGHEST
CORES = 2
ROW_TILE = 16
MIB = 1024 * 1024
VMEM_BYTES = 20 * MIB
ANYWHERE = pl.BlockSpec(memory_space=pl.ANY)
SCALARS = pl.BlockSpec(memory_space=pltpu.SMEM)


TOKEN = jax.ShapeDtypeStruct((8, 128), jnp.float32)


def cost(microseconds):
    size = int(microseconds * 3.5e6)
    return pl.CostEstimate(flops=int(microseconds * 1.1e9), bytes_accessed=size, transcendentals=0)


WHOLE = pl.BlockSpec(memory_space=pltpu.VMEM)
TOKEN_SPEC = pl.BlockSpec(TOKEN.shape, lambda *_: (0, 0))


def tokens(after):
    return [TOKEN_SPEC] * len(after)


def in_hbm(array):
    return pltpu.with_memory_space_constraint(array, pltpu.HBM)


def low(values):
    return values.astype(jnp.bfloat16)


def wide(values):
    return values.astype(jnp.float32)


def gelu_parts(values):
    phi = 0.5 * (1.0 + lax.erf(values * 0.7071067811865476))
    return (
        values * phi,
        phi + values * jnp.exp(-0.5 * values * values) * 0.3989422804014327,
    )


def normalize(values):
    center = values - jnp.mean(values, -1, keepdims=True)
    scale = lax.rsqrt(jnp.mean(center * center, -1, keepdims=True) + EPSILON)
    return (center * scale, scale)


def norm_back(upstream, normed, scale):
    return scale * (
        upstream
        - jnp.mean(upstream, -1, keepdims=True)
        - normed * jnp.mean(upstream * normed, -1, keepdims=True)
    )


def tap_groups(taps):
    return 3 if taps % 3 == 0 else 1


def row_chunks(rows, most):
    size = min(rows, most)
    return [(first, size) for first in range(0, rows, size)]


def conv_forward(extended, weight, stream, bias, gain, shift, step, after=(), reads=()):
    taps, inner, width = weight.shape
    rows = stream.shape[0]
    group = tap_groups(taps)
    steps = taps // group

    def kernel(extended_ref, weight_ref, stream_ref, bias_ref, gain_ref, shift_ref, *refs):
        normed_ref, slope_ref, next_ref, lowered_ref, token_ref, total_ref = refs[-6:]
        token_ref[...] = jnp.zeros(TOKEN.shape, TOKEN.dtype)
        first = pl.program_id(0) * group
        total = None
        for j in range(group):
            start = pl.multiple_of((first + j) * step, ROW_TILE)
            term = jnp.dot(
                extended_ref[pl.ds(start, rows), :],
                weight_ref[j],
                preferred_element_type=jnp.float32,
            )
            total = term if total is None else total + term

        @pl.when(pl.program_id(0) == 0)
        def _():
            total_ref[...] = total

        @pl.when(pl.program_id(0) > 0)
        def _():
            total_ref[...] += total

        @pl.when(pl.program_id(0) == steps - 1)
        def _():
            for at, size in row_chunks(rows, 128):
                some = pl.ds(at, size)
                value, slope = gelu_parts(total_ref[some, :] + bias_ref[...])
                normed, scale = normalize(value)
                mid = wide(stream_ref[some, :]) + normed * gain_ref[...] + shift_ref[...]
                normed_ref[some, :] = low(normed)
                slope_ref[some, :] = low(scale * slope)
                next_ref[some, :] = mid
                lowered_ref[some, :] = low(mid)

    whole = pl.BlockSpec((rows, width), lambda g: (0, 0))
    row = pl.BlockSpec((1, width), lambda g: (0, 0))
    found = pl.pallas_call(
        kernel,
        grid=(steps,),
        in_specs=[
            pl.BlockSpec(extended.shape, lambda g: (0, 0)),
            pl.BlockSpec((group, inner, width), lambda g: (g, 0, 0)),
            whole,
            row,
            row,
            row,
        ]
        + tokens(after)
        + [ANYWHERE] * len(reads),
        out_specs=[whole] * 4 + [TOKEN_SPEC],
        out_shape=[
            pltpu.HBM((rows, width), jnp.bfloat16),
            pltpu.HBM((rows, width), jnp.bfloat16),
            pltpu.HBM((rows, width), jnp.float32),
            jax.ShapeDtypeStruct((rows, width), jnp.bfloat16),
            TOKEN,
        ],
        scratch_shapes=[pltpu.VMEM((rows, width), jnp.float32)],
        compiler_params=pltpu.CompilerParams(vmem_limit_bytes=VMEM_BYTES),
        cost_estimate=cost(9),
        name="conv_forward",
    )(extended, in_hbm(weight), in_hbm(stream) if stream.dtype == jnp.float32 else stream, bias[None], gain[None], shift[None], *after, *reads)
    return found[:4], (found[4],)


def ffn_forward(
    lowered,
    stream,
    ins,
    outs,
    in_biases,
    out_bias,
    gain,
    shift,
    seq_index,
    reach,
    last_block,
    after=(),
    reads=(),
):
    rows, width = lowered.shape
    cores = len(ins)
    units = ins[0].shape[0]
    block = min(units, 256)
    steps = units // block

    rims_out = 1 if reach else 0

    def kernel(place_ref, lowered_ref, stream_ref, out_bias_ref, gain_ref, shift_ref, *refs):
        in_refs, out_refs, bias_refs = (refs[i * cores : (i + 1) * cores] for i in range(3))
        found_refs = refs[-6 - 2 * cores - rims_out :]
        active_ref, slope_refs = found_refs[0], found_refs[1 : 1 + cores]
        normed_ref, scale_ref, next_ref, rounded_ref = found_refs[1 + cores : 5 + cores]
        packet_refs = found_refs[5 + cores : 4 + 2 * cores]
        token_ref, total_ref = found_refs[-2:]
        token_ref[...] = jnp.zeros(TOKEN.shape, TOKEN.dtype)
        lane = pl.multiple_of(width + pl.program_id(0) * block, block)

        @pl.when(pl.program_id(0) == 0)
        def _():
            total_ref[...] = jnp.zeros(total_ref.shape, jnp.float32)
            for packet_ref in packet_refs:
                packet_ref[:, :width] = lowered_ref[...]

        for at, size in row_chunks(rows, 512):
            some = pl.ds(at, size)
            term = None
            for c in range(cores):
                hidden = lax.dot_general(
                    lowered_ref[some, :],
                    in_refs[c][...],
                    (((1,), (1,)), ((), ())),
                    preferred_element_type=jnp.float32,
                )
                active, slope = gelu_parts(hidden + bias_refs[c][...])
                active = low(active)
                if c == 0:
                    active_ref[some, :] = active
                else:
                    packet_refs[c - 1][some, pl.ds(lane, block)] = active
                slope_refs[c][some, :] = low(slope)
                found = jnp.dot(active, out_refs[c][...], preferred_element_type=jnp.float32)
                term = found if term is None else term + found
            total_ref[some, :] += term

        @pl.when(pl.program_id(0) == steps - 1)
        def _():
            for at, size in row_chunks(rows, 128):
                some = pl.ds(at, size)
                normed, scale = normalize(total_ref[some, :] + out_bias_ref[...])
                after_ffn = stream_ref[some, :] + normed * gain_ref[...] + shift_ref[...]
                normed_ref[some, :] = low(normed)
                scale_ref[some, :] = jnp.broadcast_to(scale, (size, 128))
                next_ref[some, :] = after_ffn
                rounded_ref[some, :] = low(after_ffn)
            if reach:
                first = pl.multiple_of((1 - place_ref[0]) * (rows - reach), ROW_TILE)
                found_refs[-3][...] = rounded_ref[pl.ds(first, reach), :]

    whole = pl.BlockSpec((rows, width), lambda g: (0, 0))
    row = pl.BlockSpec((1, width), lambda g: (0, 0))
    piece = pl.BlockSpec((block, width), lambda g: (g, 0))
    columns = pl.BlockSpec((rows, block), lambda g: (0, g))
    hidden_shape = pltpu.HBM((rows, units), jnp.bfloat16)
    found = pl.pallas_call(
        kernel,
        grid=(steps,),
        in_specs=[SCALARS, whole, whole, row, row, row]
        + [piece] * (2 * cores)
        + [pl.BlockSpec((1, block), lambda g: (0, g))] * cores
        + tokens(after)
        + [ANYWHERE] * len(reads),
        out_specs=[columns] * (1 + cores)
        + [whole, pl.BlockSpec((rows, 128), lambda g: (0, 0)), whole, whole]
        + [pl.BlockSpec((rows, width + units), lambda g: (0, 0))] * (cores - 1)
        + [pl.BlockSpec((reach, width), lambda g: (0, 0))] * rims_out
        + [TOKEN_SPEC],
        out_shape=[hidden_shape] * (1 + cores)
        + [
            pltpu.HBM((rows, width), jnp.bfloat16),
            pltpu.HBM((rows, 128), jnp.float32),
            (jax.ShapeDtypeStruct if last_block else pltpu.HBM)((rows, width), jnp.float32),
            jax.ShapeDtypeStruct((rows, width), jnp.bfloat16),
        ]
        + [jax.ShapeDtypeStruct((rows, width + units), jnp.bfloat16)] * (cores - 1)
        + [jax.ShapeDtypeStruct((reach, width), jnp.bfloat16)] * rims_out
        + [TOKEN],
        scratch_shapes=[pltpu.VMEM((rows, width), jnp.float32)],
        compiler_params=pltpu.CompilerParams(vmem_limit_bytes=VMEM_BYTES),
        cost_estimate=cost(11),
        name="ffn_forward",
    )(
        seq_index.astype(jnp.int32)[None],
        lowered,
        in_hbm(stream),
        out_bias[None],
        gain[None],
        shift[None],
        *[in_hbm(each) for each in ins],
        *[in_hbm(each) for each in outs],
        *[each[None] for each in in_biases],
        *after,
        *reads,
    )
    return (
        found[0],
        found[1 : 1 + cores],
        found[1 + cores : 5 + cores],
        found[5 + cores : 4 + 2 * cores],
        found[4 + 2 * cores] if reach else None,
        (found[-1],),
    )


def head_and_loss(stream, head_weight, codes, after=()):
    rows, width = stream.shape
    classes = head_weight.shape[1]
    padded = jnp.pad(head_weight, ((0, 0), (0, 128 - classes)))
    cuts = row_chunks(rows, 256)

    def kernel(stream_ref, head_ref, code_ref, *refs):
        grad_ref, head_grad_ref, sums_ref, token_ref = refs[-4:]
        token_ref[...] = jnp.zeros(TOKEN.shape, TOKEN.dtype)
        head_grad = jnp.zeros((128, width), jnp.float32)
        objective = jnp.zeros((1, 1), jnp.float32)
        scored = jnp.zeros((1, 1), jnp.float32)
        for at, size in cuts:
            some = pl.ds(at, size)
            value = stream_ref[some, :]
            code = code_ref[some, :]
            mask = jnp.where(code[:, :1] >= classes, 1.0, 0.0)
            logits = jnp.dot(
                value, head_ref[...], precision=HIGHEST_PRECISION, preferred_element_type=jnp.float32
            )
            lane = lax.broadcasted_iota(jnp.int32, logits.shape, 1)
            valid = lane < classes
            peak = jnp.max(jnp.where(valid, logits, -jnp.inf), -1, keepdims=True)
            exponent = jnp.where(valid, jnp.exp(jnp.where(valid, logits - peak, 0.0)), 0.0)
            denominator = jnp.sum(exponent, -1, keepdims=True)
            chosen = lane == jnp.where(code >= classes, code - classes, code)
            picked = jnp.sum(jnp.where(chosen, logits, 0.0), -1, keepdims=True)
            terms = mask * (peak + jnp.log(denominator) - picked)
            objective = objective + jnp.sum(terms, 0, keepdims=True)
            scored = scored + jnp.sum(mask, 0, keepdims=True)
            logit_grad = mask * (exponent / denominator - jnp.where(chosen, 1.0, 0.0))
            grad_ref[some, :] = lax.dot_general(
                logit_grad,
                head_ref[...],
                (((1,), (1,)), ((), ())),
                precision=HIGHEST_PRECISION,
                preferred_element_type=jnp.float32,
            )
            head_grad = head_grad + lax.dot_general(
                logit_grad,
                value,
                (((0,), (0,)), ((), ())),
                precision=HIGHEST_PRECISION,
                preferred_element_type=jnp.float32,
            )
        head_grad_ref[...] = head_grad[: head_grad_ref.shape[0]]
        at_row = lax.broadcasted_iota(jnp.int32, sums_ref.shape, 0)
        sums_ref[...] = jnp.where(at_row == 0, objective, scored)

    found = pl.pallas_call(
        kernel,
        out_shape=[
            jax.ShapeDtypeStruct((rows, width), jnp.float32),
            jax.ShapeDtypeStruct((-(-classes // 8) * 8, width), jnp.float32),
            jax.ShapeDtypeStruct((8, 128), jnp.float32),
            TOKEN,
        ],
        compiler_params=pltpu.CompilerParams(vmem_limit_bytes=VMEM_BYTES),
        cost_estimate=cost(6),
        name="head_and_loss",
    )(stream, padded, codes, *after)
    return found[:3], (found[3],)


def ffn_back_hidden(upstream, normed, scale, gain, outs, slopes, after=()):
    rows, width = upstream.shape
    cores = len(outs)
    units = outs[0].shape[0]
    block = min(units, 256)

    def kernel(upstream_ref, normed_ref, scale_ref, gain_ref, *refs):
        out_refs, slope_refs = refs[:cores], refs[cores : 2 * cores]
        found_refs = refs[-3 - 2 * cores :]
        output_grad_ref, hidden_ref = found_refs[:2]
        bias_refs, packet_refs = found_refs[2 : 2 + cores], found_refs[2 + cores : -2]
        sums_ref, token_ref = found_refs[-2:]
        token_ref[...] = jnp.zeros(TOKEN.shape, TOKEN.dtype)
        lane = pl.multiple_of(width + pl.program_id(0) * block, block)

        @pl.when(pl.program_id(0) == 0)
        def _():
            totals = [jnp.zeros((1, width), jnp.float32)] * 3
            for at, size in row_chunks(rows, 128):
                some = pl.ds(at, size)
                grad, value = upstream_ref[some, :], wide(normed_ref[some, :])
                output_grad = low(norm_back(grad * gain_ref[...], value, scale_ref[some, :1]))
                output_grad_ref[some, :] = output_grad
                for packet_ref in packet_refs:
                    packet_ref[some, :width] = output_grad
                for i, each in enumerate((grad * value, grad, wide(output_grad))):
                    totals[i] = totals[i] + jnp.sum(each, 0, keepdims=True)
            sums_ref[...] = jnp.zeros(sums_ref.shape, jnp.float32)
            for i in range(3):
                sums_ref[i : i + 1, :] = totals[i]

        for c in range(cores):
            total = jnp.zeros((1, block), jnp.float32)
            for at, size in row_chunks(rows, 512):
                some = pl.ds(at, size)
                active_grad = lax.dot_general(
                    output_grad_ref[some, :],
                    out_refs[c][...],
                    (((1,), (1,)), ((), ())),
                    preferred_element_type=jnp.float32,
                )
                hidden_grad = low(active_grad * wide(slope_refs[c][some, :]))
                if c == 0:
                    hidden_ref[some, :] = hidden_grad
                else:
                    packet_refs[c - 1][some, pl.ds(lane, block)] = hidden_grad
                total = total + jnp.sum(wide(hidden_grad), 0, keepdims=True)
            bias_refs[c][...] = total

    whole = pl.BlockSpec((rows, width), lambda g: (0, 0))
    columns = pl.BlockSpec((rows, block), lambda g: (0, g))
    found = pl.pallas_call(
        kernel,
        grid=(units // block,),
        in_specs=[
            whole,
            whole,
            pl.BlockSpec((rows, 128), lambda g: (0, 0)),
            pl.BlockSpec((1, width), lambda g: (0, 0)),
        ]
        + [pl.BlockSpec((block, width), lambda g: (g, 0))] * cores
        + [columns] * cores
        + tokens(after),
        out_specs=[whole, columns]
        + [pl.BlockSpec((1, block), lambda g: (0, g))] * cores
        + [pl.BlockSpec((rows, width + units), lambda g: (0, 0))] * (cores - 1)
        + [pl.BlockSpec((8, width), lambda g: (0, 0)), TOKEN_SPEC],
        out_shape=[
            jax.ShapeDtypeStruct((rows, width), jnp.bfloat16),
            pltpu.HBM((rows, units), jnp.bfloat16),
        ]
        + [jax.ShapeDtypeStruct((1, units), jnp.float32)] * cores
        + [jax.ShapeDtypeStruct((rows, width + units), jnp.bfloat16)] * (cores - 1)
        + [jax.ShapeDtypeStruct((8, width), jnp.float32), TOKEN],
        compiler_params=pltpu.CompilerParams(vmem_limit_bytes=VMEM_BYTES),
        cost_estimate=cost(6),
        name="ffn_back_hidden",
    )(
        upstream,
        in_hbm(normed),
        in_hbm(scale),
        gain[None],
        *[in_hbm(each) for each in outs],
        *[in_hbm(each) for each in slopes],
        *after,
    )
    return (
        found[0],
        found[1],
        found[2 : 2 + cores],
        found[2 + cores : -2],
        found[-2],
        (found[-1],),
    )


def ffn_back_stream(
    upstream, hidden, packets, ins, normed, slope, gain, places, reach, after=(), reads=(), relay=False
):
    rows, width = upstream.shape
    cores = len(ins)
    units = ins[0].shape[0]
    block = min(units, 256)
    steps = units // block
    lanes = width // cores
    relays = cores - 1 if relay else 0
    rims_out = 1 if reach else 0

    def kernel(core_ref, upstream_ref, normed_ref, slope_ref, gain_ref, *refs):
        hidden_refs, in_refs = refs[:cores], refs[cores : 2 * cores]
        found_refs = refs[-4 - cores - relays - rims_out :]
        mid_ref, conv_grad_ref = found_refs[:2]
        cut_refs = found_refs[2 : 1 + cores]
        sums_ref, token_ref, total_ref = found_refs[-3:]
        token_ref[...] = jnp.zeros(TOKEN.shape, TOKEN.dtype)
        for i in range(relays):
            relay_ref = found_refs[1 + cores + i]
            lane = pl.multiple_of(width + pl.program_id(0) * block, block)
            relay_ref[:, pl.ds(lane, block)] = hidden_refs[1 + i][...]

            @pl.when(pl.program_id(0) == 0)
            def _(i=i, relay_ref=relay_ref):
                relay_ref[:, :width] = refs[2 * cores + i][...]

        @pl.when(pl.program_id(0) == 0)
        def _():
            total_ref[...] = upstream_ref[...]

        for at, size in row_chunks(rows, 512):
            some = pl.ds(at, size)
            total_ref[some, :] += sum(
                jnp.dot(
                    hidden_refs[c][some, :], in_refs[c][...], preferred_element_type=jnp.float32
                )
                for c in range(cores)
            )

        @pl.when(pl.program_id(0) == steps - 1)
        def _():
            totals = [jnp.zeros((1, width), jnp.float32)] * 3
            for at, size in row_chunks(rows, 128):
                some = pl.ds(at, size)
                grad, value = total_ref[some, :], wide(normed_ref[some, :])
                conv_grad = low(norm_back(grad * gain_ref[...], value, wide(slope_ref[some, :])))
                mid_ref[some, :] = grad
                conv_grad_ref[some, :] = conv_grad
                for i, each in enumerate((grad * value, grad, wide(conv_grad))):
                    totals[i] = totals[i] + jnp.sum(each, 0, keepdims=True)
            sums_ref[...] = jnp.zeros(sums_ref.shape, jnp.float32)
            for i in range(3):
                sums_ref[i : i + 1, :] = totals[i]
            for c in range(1, cores):
                first = lax.rem(core_ref[0] - c + cores, cores) * lanes
                cut_refs[c - 1][...] = conv_grad_ref[:, pl.ds(pl.multiple_of(first, lanes), lanes)]
            if reach:
                first = pl.multiple_of((1 - core_ref[1]) * (rows - reach), ROW_TILE)
                found_refs[-4][...] = conv_grad_ref[pl.ds(first, reach), :]

    whole = pl.BlockSpec((rows, width), lambda g, core: (0, 0))
    found = pl.pallas_call(
        kernel,
        grid_spec=pltpu.PrefetchScalarGridSpec(
            num_scalar_prefetch=1,
            grid=(steps,),
            in_specs=[whole, whole, whole, pl.BlockSpec((1, width), lambda g, core: (0, 0))]
            + [pl.BlockSpec((rows, block), lambda g, core: (0, g))]
            + [pl.BlockSpec((rows, block), lambda g, core: (0, width // block + g))] * (cores - 1)
            + [pl.BlockSpec((block, width), lambda g, core: (g, 0))] * cores
            + [whole] * relays
            + tokens(after)
            + [ANYWHERE] * len(reads),
            out_specs=[whole, whole]
            + [pl.BlockSpec((rows, lanes), lambda g, core: (0, 0))] * (cores - 1)
            + [pl.BlockSpec((rows, width + units), lambda g, core: (0, 0))] * relays
            + [pl.BlockSpec((reach, width), lambda g, core: (0, 0))] * rims_out
            + [pl.BlockSpec((8, width), lambda g, core: (0, 0)), TOKEN_SPEC],
            scratch_shapes=[pltpu.VMEM((rows, width), jnp.float32)],
        ),
        out_shape=[
            jax.ShapeDtypeStruct((rows, width), jnp.float32),
            jax.ShapeDtypeStruct((rows, width), jnp.bfloat16),
        ]
        + [jax.ShapeDtypeStruct((rows, lanes), jnp.bfloat16)] * (cores - 1)
        + [jax.ShapeDtypeStruct((rows, width + units), jnp.bfloat16)] * relays
        + [jax.ShapeDtypeStruct((reach, width), jnp.bfloat16)] * rims_out
        + [jax.ShapeDtypeStruct((8, width), jnp.float32), TOKEN],
        compiler_params=pltpu.CompilerParams(vmem_limit_bytes=VMEM_BYTES),
        cost_estimate=cost(5),
        name="ffn_back_stream",
    )(
        jnp.stack(places[:2]).astype(jnp.int32),
        upstream,
        in_hbm(normed),
        in_hbm(slope),
        gain[None],
        in_hbm(hidden),
        *packets,
        *[in_hbm(each) for each in ins],
        *packets[:relays],
        *after,
        *reads,
    )
    return (
        found[0],
        found[1],
        found[2 : 1 + cores],
        found[1 + cores : 1 + cores + relays],
        found[1 + cores + relays] if reach else None,
        found[-2],
        (found[-1],),
    )


def conv_data_grad(extended, weight, upstream, step, kind, after=()):
    taps, inner, width = weight.shape
    rows = upstream.shape[0]
    group = tap_groups(taps)
    steps = taps // group

    def kernel(extended_ref, weight_ref, upstream_ref, *refs):
        out_ref, token_ref, total_ref = refs[-3:]
        token_ref[...] = jnp.zeros(TOKEN.shape, TOKEN.dtype)
        first = pl.program_id(0) * group
        total = None
        for j in range(group):
            start = pl.multiple_of((taps - 1 - first - j) * step, ROW_TILE)
            term = lax.dot_general(
                extended_ref[pl.ds(start, rows), :],
                weight_ref[j],
                (((1,), (1,)), ((), ())),
                preferred_element_type=jnp.float32,
            )
            total = term if total is None else total + term

        @pl.when(pl.program_id(0) == 0)
        def _():
            total_ref[...] = total

        @pl.when(pl.program_id(0) > 0)
        def _():
            total_ref[...] += total

        @pl.when(pl.program_id(0) == steps - 1)
        def _():
            out_ref[...] = (upstream_ref[...] + wide(low(total_ref[...]))).astype(kind)

    whole = pl.BlockSpec((rows, inner), lambda g: (0, 0))
    found = pl.pallas_call(
        kernel,
        grid=(steps,),
        in_specs=[
            pl.BlockSpec(extended.shape, lambda g: (0, 0)),
            pl.BlockSpec((group, inner, width), lambda g: (g, 0, 0)),
            whole,
        ]
        + tokens(after),
        out_specs=(whole, TOKEN_SPEC),
        out_shape=(jax.ShapeDtypeStruct((rows, inner), kind), TOKEN),
        scratch_shapes=[pltpu.VMEM((rows, inner), jnp.float32)],
        compiler_params=pltpu.CompilerParams(vmem_limit_bytes=VMEM_BYTES),
        cost_estimate=cost(6),
        name="conv_data_grad",
    )(extended, in_hbm(weight), upstream, *after)
    return found[0], (found[1],)


def hold(arrays, after, reads=()):
    count = len(arrays)
    if count == 0:
        return [], after

    def kernel(*refs):
        refs[-1][...] = jnp.zeros(TOKEN.shape, TOKEN.dtype)

    found = pl.pallas_call(
        kernel,
        in_specs=[ANYWHERE] * (count + len(reads)) + [WHOLE] * len(after),
        out_specs=[ANYWHERE] * count + [WHOLE],
        out_shape=[jax.ShapeDtypeStruct(each.shape, each.dtype) for each in arrays] + [TOKEN],
        input_output_aliases={i: i for i in range(count)},
        compiler_params=pltpu.CompilerParams(vmem_limit_bytes=1 * MIB),
        cost_estimate=cost(0.5),
        name="hold",
    )(*arrays, *reads, *after)
    return list(found[:-1]), (found[-1],)


def join_rows(parts, after=(), reads=()):
    def kernel(*refs):
        out_ref, token_ref = refs[-2:]
        token_ref[...] = jnp.zeros(TOKEN.shape, TOKEN.dtype)
        first = 0
        for i, part in enumerate(parts):
            out_ref[first : first + part.shape[0]] = refs[i][...]
            first += part.shape[0]

    shape = (sum(part.shape[0] for part in parts), parts[0].shape[1])
    found = pl.pallas_call(
        kernel,
        in_specs=[WHOLE] * len(parts) + [ANYWHERE] * len(reads) + [WHOLE] * len(after),
        out_specs=[WHOLE] * 2,
        out_shape=[jax.ShapeDtypeStruct(shape, parts[0].dtype), TOKEN],
        compiler_params=pltpu.CompilerParams(vmem_limit_bytes=10 * MIB),
        cost_estimate=cost(1.5),
        name="join_rows",
    )(*parts, *reads, *after)
    return found[0], (found[1],)


def restack(groups, reads=(), after=()):
    cuts = [cut for _, each in groups for cut in each]
    if any(last is not None and (first % ROW_TILE or last % ROW_TILE) for first, last, _ in cuts):
        return [
            jnp.stack([array[first:last].reshape(shape) for array in arrays])
            for arrays, each in groups
            for first, last, shape in each
        ], after
    flat = [array for arrays, _ in groups for array in arrays]
    plan = []
    shapes = []
    at = 0
    for arrays, each in groups:
        for first, last, shape in each:
            for slot in range(len(arrays)):
                plan.append((at + slot, first, last, len(shapes), slot))
            held = shape if last is None else (last - first,) + arrays[0].shape[1:]
            shapes.append(jax.ShapeDtypeStruct((len(arrays),) + held, arrays[0].dtype))
        at += len(arrays)

    def kernel(*refs):
        out_refs = refs[-2 - len(shapes) : -2]
        token_ref, sem_ref = refs[-2:]
        token_ref[...] = jnp.zeros(TOKEN.shape, TOKEN.dtype)
        copies = []
        for source, first, last, target, slot in plan:
            ref = refs[source]
            copies.append(
                pltpu.make_async_copy(
                    ref if last is None else ref.at[pl.ds(first, last - first)],
                    out_refs[target].at[slot],
                    sem_ref.at[len(copies)],
                )
            )
        copy_all(copies)

    found = pl.pallas_call(
        kernel,
        in_specs=[ANYWHERE] * (len(flat) + len(reads)) + [WHOLE] * len(after),
        out_specs=[WHOLE] * (len(shapes) + 1),
        out_shape=shapes + [TOKEN],
        scratch_shapes=[pltpu.SemaphoreType.DMA((len(plan),))],
        compiler_params=pltpu.CompilerParams(vmem_limit_bytes=10 * MIB),
        cost_estimate=cost(1.5),
        name="restack",
    )(*flat, *reads, *after)
    return [
        each.reshape((each.shape[0],) + shape) for each, (_, _, shape) in zip(found, cuts)
    ], (found[-1],)


def conv_weight_grad(
    extendeds, upstream, arrived, places, sizes, taps, step, after=(), reads=()
):
    cores, seqs, acrosses, tap_peers = sizes
    rows = upstream.shape[0]
    inner = extendeds[0].shape[1]
    lanes = upstream.shape[1] // cores
    slab = inner // (seqs * acrosses * tap_peers)
    direct = slab % ROW_TILE == 0
    half = (tap_peers + 1) // 2
    rest = tap_peers - half
    seconds = acrosses if rest else 0
    outs = seqs + seconds if direct else 1

    def kernel(place_ref, *refs):
        out_refs = refs[-2 - outs : -2]
        token_ref, found_ref = refs[-2:]
        token_ref[...] = jnp.zeros(TOKEN.shape, TOKEN.dtype)
        start = pl.multiple_of(pl.program_id(0) * step, ROW_TILE)
        found = low(
            sum(
                lax.dot_general(
                    refs[c][pl.ds(start, rows), :],
                    refs[cores + c][...],
                    (((0,), (0,)), ((), ())),
                    preferred_element_type=jnp.float32,
                )
                for c in range(cores)
            )
        )
        if not direct:
            out_refs[0][0] = found
            return
        found_ref[...] = found

        def chunk(slot_t, slot_s, slot_a):
            t = lax.rem(place_ref[3] - slot_t + tap_peers, tap_peers)
            at = lax.rem(place_ref[1] - slot_s + seqs, seqs)
            a = lax.rem(place_ref[2] - slot_a + acrosses, acrosses)
            first = pl.multiple_of(((t * seqs + at) * acrosses + a) * slab, slab)
            return found_ref[pl.ds(first, slab), :]

        for s in range(seqs):
            for a in range(acrosses):
                for t in range(half):
                    out_refs[s][a, t, 0] = chunk(t, s, a)
                for t in range(half, tap_peers):
                    out_refs[seqs + a][s, t - half, 0] = chunk(t, s, a)

    if direct:
        shapes = [(acrosses, half, taps, slab, lanes)] * seqs
        shapes += [(seqs, rest, taps, slab, lanes)] * seconds
        specs = [
            pl.BlockSpec(shape[:2] + (1, slab, lanes), lambda k, place: (0, 0, k, 0, 0))
            for shape in shapes
        ]
    else:
        shapes = [(taps, inner, lanes)]
        specs = [pl.BlockSpec((1, inner, lanes), lambda k, place: (k, 0, 0))]
    found = pl.pallas_call(
        kernel,
        grid_spec=pltpu.PrefetchScalarGridSpec(
            num_scalar_prefetch=1,
            grid=(taps,),
            in_specs=[pl.BlockSpec(extendeds[0].shape, lambda k, place: (0, 0))] * cores
            + [pl.BlockSpec((rows, lanes), lambda k, place: (0, place[0]))]
            + [pl.BlockSpec((rows, lanes), lambda k, place: (0, 0))] * (cores - 1)
            + tokens(after)
            + [ANYWHERE] * len(reads),
            out_specs=specs + [TOKEN_SPEC],
            scratch_shapes=[pltpu.VMEM((inner, lanes), jnp.bfloat16)],
        ),
        out_shape=[jax.ShapeDtypeStruct(shape, jnp.bfloat16) for shape in shapes] + [TOKEN],
        compiler_params=pltpu.CompilerParams(vmem_limit_bytes=VMEM_BYTES),
        cost_estimate=cost(9),
        name="conv_weight_grad",
    )(jnp.stack(places).astype(jnp.int32), *extendeds, upstream, *arrived, *after, *reads)
    token = found[-1]
    if not direct:
        found = found[0].reshape(taps, tap_peers, seqs, acrosses, slab, lanes)
        for axis, which in ((1, 3), (2, 1), (3, 2)):
            found = relative(found, axis, places[which], sizes[which])
        found = found.transpose(2, 3, 1, 0, 4, 5)
        found = [found[s, :, :half] for s in range(seqs)] + [
            found[:, a, half:] for a in range(seconds)
        ]
    flat = [each.reshape(-1, lanes) for each in found[: seqs + seconds]]
    return flat[:seqs], flat[seqs:], token


def ffn_weight_grad(pairs, sizes, ffn_rows, after=()):
    cores, seqs, acrosses, tap_peers = sizes
    rows, width = pairs[0][1].shape
    block = tap_peers * ffn_rows
    half = (tap_peers + 1) // 2
    rest = tap_peers - half
    seconds = seqs if rest else 0
    transposed = (((0,), (0,)), ((), ()))
    if ffn_rows % ROW_TILE:
        found = jnp.stack(
            [
                low(
                    sum(
                        lax.dot_general(a, b, transposed, preferred_element_type=jnp.float32)
                        for a, b in [(left, right)]
                        + [(ends[:, width:], starts[:, :width]) for ends, starts in packets]
                    )
                ).reshape(acrosses, seqs, tap_peers, ffn_rows, width)
                for left, right, packets in pairs
            ],
            3,
        )
        token = jnp.zeros(TOKEN.shape, TOKEN.dtype)
        return (
            [found[a, :, :half].reshape(-1, width) for a in range(acrosses)],
            [found[:, s, half:].reshape(-1, width) for s in range(seconds)],
            token,
        )
    outs = acrosses + seconds

    def kernel(*refs):
        out_refs, token_ref = refs[-1 - outs : -1], refs[-1]
        token_ref[...] = jnp.zeros(TOKEN.shape, TOKEN.dtype)
        step = pl.program_id(0)
        for which in range(2):
            base = 2 * cores * which
            found = low(
                sum(
                    lax.dot_general(
                        refs[base + 2 * c][...],
                        refs[base + 2 * c + 1][...],
                        transposed,
                        preferred_element_type=jnp.float32,
                    )
                    for c in range(cores)
                )
            ).reshape(tap_peers, ffn_rows, width)
            for a in range(acrosses):

                @pl.when(step // seqs == a)
                def _(a=a):
                    out_refs[a][0, :, which] = found[:half]

            for s in range(seconds):

                @pl.when(lax.rem(step, seqs) == s)
                def _(s=s):
                    out_refs[acrosses + s][0, :, which] = found[half:]

    right_spec = pl.BlockSpec((rows, width), lambda g: (0, 0))
    left_spec = pl.BlockSpec((rows, block), lambda g: (0, g))
    late_spec = pl.BlockSpec((rows, block), lambda g: (0, width // block + g))

    def first_spec(a):
        return pl.BlockSpec(
            (1, half, 2, ffn_rows, width),
            lambda g: (jnp.clip(g - a * seqs, 0, seqs - 1), 0, 0, 0, 0),
        )

    second_spec = pl.BlockSpec(
        (1, rest, 2, ffn_rows, width), lambda g: (g // seqs, 0, 0, 0, 0)
    )
    operands = []
    for left, right, packets in pairs:
        operands += [in_hbm(left), right]
        for ends, starts in packets:
            operands += [ends, starts]
    found = pl.pallas_call(
        kernel,
        grid=(acrosses * seqs,),
        in_specs=([left_spec, right_spec] + [late_spec, right_spec] * (cores - 1)) * 2
        + tokens(after),
        out_specs=[first_spec(a) for a in range(acrosses)]
        + [second_spec] * seconds
        + [TOKEN_SPEC],
        out_shape=[jax.ShapeDtypeStruct((seqs, half, 2, ffn_rows, width), jnp.bfloat16)] * acrosses
        + [jax.ShapeDtypeStruct((acrosses, rest, 2, ffn_rows, width), jnp.bfloat16)] * seconds
        + [TOKEN],
        compiler_params=pltpu.CompilerParams(vmem_limit_bytes=VMEM_BYTES),
        cost_estimate=cost(8),
        name="ffn_weight_grad",
    )(*operands, *after)
    flat = [each.reshape(-1, width) for each in found[:-1]]
    return flat[:acrosses], flat[acrosses:], found[-1]


def group_slots(groups, lanes):
    flat, where = [], []
    rows = groups[0][0][0].size // (groups[0][1] * lanes)
    for parts, slots in groups:
        where += [(len(flat), len(parts), slot) for slot in range(slots)]
        flat += [part.reshape(slots, rows, lanes) for part in parts]
    return flat, where, rows


def slot_sum(refs, place, first=0):
    start, count, at = place
    return low(sum(wide(refs[first + start + i][at]) for i in range(count)))


def merge_slots(conv_groups, ffn_groups, after=()):
    lanes, width = conv_groups[0][0][0].shape[-1], ffn_groups[0][0][0].shape[-1]
    cuts = width // lanes
    conv_parts, conv_where, conv_rows = group_slots(conv_groups, lanes)
    ffn_parts, ffn_where, ffn_rows = group_slots(ffn_groups, width)
    slots = len(conv_where)
    if conv_rows % ROW_TILE or ffn_rows % ROW_TILE:
        merged = []
        for slot in range(slots):
            ffn = slot_sum(ffn_parts, ffn_where[slot])
            merged.append(
                jnp.concatenate(
                    [slot_sum(conv_parts, conv_where[slot])]
                    + [ffn[:, i * lanes : (i + 1) * lanes] for i in range(cuts)]
                )
            )
        return merged, after

    def kernel(*refs):
        out_refs, token_ref = refs[-1 - slots : -1], refs[-1]
        token_ref[...] = jnp.zeros(TOKEN.shape, TOKEN.dtype)
        for slot in range(slots):
            out_refs[slot][:conv_rows] = slot_sum(refs, conv_where[slot])
            ffn = slot_sum(refs, ffn_where[slot], len(conv_parts))
            for i in range(cuts):
                first = conv_rows + i * ffn_rows
                out_refs[slot][first : first + ffn_rows] = ffn[:, i * lanes : (i + 1) * lanes]

    found = pl.pallas_call(
        kernel,
        in_specs=[WHOLE] * (len(conv_parts) + len(ffn_parts) + len(after)),
        out_specs=[WHOLE] * (slots + 1),
        out_shape=[jax.ShapeDtypeStruct((conv_rows + cuts * ffn_rows, lanes), jnp.bfloat16)] * slots
        + [TOKEN],
        compiler_params=pltpu.CompilerParams(vmem_limit_bytes=10 * MIB),
        cost_estimate=cost(1.5),
        name="merge_slots",
    )(*conv_parts, *ffn_parts, *after)
    return found[:slots], (found[slots],)


def append_slots(groups, packed, after=(), reads=()):
    lanes = groups[0][0][0].shape[-1]
    parts, where, rows = group_slots(groups, lanes)
    slots = len(where)
    if rows % ROW_TILE:
        return [
            jnp.concatenate([slot_sum(parts, where[slot])] + packed) for slot in range(slots)
        ], after

    def kernel(*refs):
        out_refs, token_ref = refs[-1 - slots : -1], refs[-1]
        token_ref[...] = jnp.zeros(TOKEN.shape, TOKEN.dtype)
        for slot in range(slots):
            out_refs[slot][:rows] = slot_sum(refs, where[slot])
            if packed:
                out_refs[slot][rows:] = refs[len(parts)][...]

    shape = jax.ShapeDtypeStruct((rows + sum(each.shape[0] for each in packed), lanes), jnp.bfloat16)
    found = pl.pallas_call(
        kernel,
        in_specs=[WHOLE] * (len(packed) + len(parts) + len(after)) + [ANYWHERE] * len(reads),
        out_specs=[WHOLE] * (slots + 1),
        out_shape=[shape] * slots + [TOKEN],
        compiler_params=pltpu.CompilerParams(vmem_limit_bytes=8 * MIB),
        cost_estimate=cost(1),
        name="append_slots",
    )(*parts, *packed, *after, *reads)
    return found[:slots], (found[slots],)


def pack_small(row_groups, biases, losses, places, sizes, ffn_rows, after=()):
    cores, seqs, acrosses, tap_peers = sizes
    width = row_groups[0][0].shape[1]
    head_rows = sum(count for _, count in row_groups)
    hidden = cores * biases[0][0].shape[1]
    bias_rows = hidden // width
    used = head_rows + len(biases) * bias_rows + 2
    rows = -(-used // ROW_TILE) * ROW_TILE
    lanes = width // 2
    per_row = width // ffn_rows
    if ffn_rows % 64:
        terms = jnp.stack([losses[0, 0], losses[1, 0]])
        terms = jnp.stack([terms, terms - wide(low(terms))])
        pieces = [array[:count] for array, count in row_groups]
        for each in biases:
            bias = jnp.stack(each).reshape(cores, acrosses, seqs, tap_peers, ffn_rows)
            for axis, which in enumerate((0, 2, 1, 3)):
                bias = relative(bias, axis, places[which], sizes[which])
            pieces.append(bias.transpose(1, 0, 2, 3, 4).reshape(-1, width))
        pieces.append(jnp.pad(terms, ((0, rows - used), (0, width - 2))))
        packed = low(jnp.concatenate(pieces))
        return jnp.concatenate([packed[:, :lanes], packed[:, lanes:]]), after

    def kernel(place_ref, *refs):
        packed_ref, token_ref, rows_ref = refs[-3:]
        token_ref[...] = jnp.zeros(TOKEN.shape, TOKEN.dtype)
        rows_ref[...] = jnp.zeros(rows_ref.shape, jnp.float32)
        at = 0
        for i, (_, count) in enumerate(row_groups):
            rows_ref[at : at + count, :] = refs[i][:count, :]
            at += count
        shape = (cores, acrosses, seqs, tap_peers)
        owners = (0, 2, 1, 3)
        for b in range(len(biases)):
            blocks = {}
            for slot in np.ndindex(*shape):
                first = ((slot[1] * seqs + slot[2]) * tap_peers + slot[3]) * ffn_rows
                ref = refs[len(row_groups) + b * cores + slot[0]]
                blocks[slot] = ref[:, first : first + ffn_rows]
            for axis, size in enumerate(shape):
                turned = {}
                for slot in blocks:
                    place = lax.rem(place_ref[owners[axis]] - slot[axis] + size, size)
                    value = blocks[slot[:axis] + (0,) + slot[axis + 1 :]]
                    for other in range(1, size):
                        candidate = blocks[slot[:axis] + (other,) + slot[axis + 1 :]]
                        value = jnp.where(place == other, candidate, value)
                    turned[slot] = value
                blocks = turned
            ordered = [
                blocks[(c, a, s, t)]
                for a in range(acrosses)
                for c in range(cores)
                for s in range(seqs)
                for t in range(tap_peers)
            ]
            for row in range(bias_rows):
                line = ordered[row * per_row : (row + 1) * per_row]
                rows_ref[at : at + 1, :] = jnp.concatenate(line, 1)
                at += 1
        losses_ref = refs[len(row_groups) + len(biases) * cores]
        lane = lax.broadcasted_iota(jnp.int32, (1, width), 1)
        objective = jnp.broadcast_to(losses_ref[0:1, 0:1], (1, width))
        scored = jnp.broadcast_to(losses_ref[1:2, 0:1], (1, width))
        line = jnp.where(lane == 0, objective, jnp.where(lane == 1, scored, 0.0))
        rows_ref[at : at + 1, :] = line
        rows_ref[at + 1 : at + 2, :] = line - wide(low(line))
        packed_ref[:rows, :] = low(rows_ref[:, :lanes])
        packed_ref[rows:, :] = low(rows_ref[:, lanes:])

    flat = [array for array, _ in row_groups] + [each for some in biases for each in some]
    found = pl.pallas_call(
        kernel,
        in_specs=[SCALARS] + [WHOLE] * (len(flat) + 1 + len(after)),
        out_specs=[WHOLE] * 2,
        out_shape=[jax.ShapeDtypeStruct((2 * rows, lanes), jnp.bfloat16), TOKEN],
        scratch_shapes=[pltpu.VMEM((rows, width), jnp.float32)],
        compiler_params=pltpu.CompilerParams(vmem_limit_bytes=8 * MIB),
        cost_estimate=cost(2),
        name="pack_small",
    )(jnp.stack(places).astype(jnp.int32), *flat, losses, *after)
    return found[0], (found[1],)


def paired(values):
    while len(values) > 1:
        half = len(values) // 2
        if len(values) % 2:
            return sum(values[1:], values[0])
        values = [values[i] + values[i + half] for i in range(half)]
    return values[0]


def finish_small(stacks, first, width, classes, hidden, places, sizes):
    cores, seqs, acrosses = sizes[:3]
    peers, rows, lanes = stacks[0].shape
    count = rows - first
    bias_rows = hidden // width
    at_bias = 12 + classes
    at_loss = at_bias + 2 * bias_rows

    def pick(row):
        return (
            [row(2), row(5)],
            [[row(0), row(6)], [row(3), row(9)]],
            [[row(1), row(7)], [row(4), row(10)]],
            [[row(at_bias + b * bias_rows + i) for i in range(bias_rows)] for b in range(2)],
            [row(8), row(11)],
        )

    if max(cores, seqs, acrosses) > 2 or first % count or count % ROW_TILE:
        full = jnp.stack(
            [wide(each[:, first:]).reshape(seqs, acrosses, count, lanes) for each in stacks]
        )
        for axis, (place, size) in enumerate(zip(places[:3], sizes[:3])):
            full = relative(full, axis, place, size)
        total = jnp.sum(full, (0, 1, 2))
        total = jnp.concatenate([total[: count // 2], total[count // 2 :]], 1)
        conv_bias, gains, shifts, in_bias, out_bias = pick(lambda i: total[i])
        terms = total[at_loss] + total[at_loss + 1]
        return (
            jnp.stack(conv_bias),
            jnp.stack([jnp.stack(each) for each in gains]),
            jnp.stack([jnp.stack(each) for each in shifts]),
            jnp.stack([jnp.concatenate(each) for each in in_bias]),
            jnp.stack(out_bias),
            total[12:at_bias].T,
            (terms[0] / terms[1]).reshape(1, 1),
        )

    def kernel(*refs):
        conv_ref, gain_ref, shift_ref, in_ref, out_ref, head_ref, loss_ref, rows_ref = refs[cores:]
        total = paired(
            [
                paired(
                    [
                        paired([wide(refs[c][s * acrosses + a]) for a in range(acrosses)])
                        for s in range(seqs)
                    ]
                )
                for c in range(cores)
            ]
        )
        rows_ref[:, :lanes] = total[: count // 2]
        rows_ref[:, lanes:] = total[count // 2 :]
        conv_bias, gains, shifts, in_bias, out_bias = pick(lambda i: rows_ref[i : i + 1, :])
        for b in range(2):
            conv_ref[b : b + 1, :] = conv_bias[b]
            out_ref[b : b + 1, :] = out_bias[b]
            for i in range(2):
                gain_ref[b, i : i + 1, :] = gains[b][i]
                shift_ref[b, i : i + 1, :] = shifts[b][i]
            for i in range(bias_rows):
                in_ref[b : b + 1, i * width : (i + 1) * width] = in_bias[b][i]
        head_ref[...] = rows_ref[12 : 12 + 8 * (-(-classes // 8)), :].T[:, :classes]
        terms = rows_ref[at_loss : at_loss + 1, :128] + rows_ref[at_loss + 1 : at_loss + 2, :128]
        loss_ref[...] = terms[:, 0:1] / terms[:, 1:2]

    return pl.pallas_call(
        kernel,
        grid=(1,),
        in_specs=[pl.BlockSpec((peers, count, lanes), lambda g: (0, first // count, 0))] * cores,
        out_shape=(
            jax.ShapeDtypeStruct((2, width), jnp.float32),
            jax.ShapeDtypeStruct((2, 2, width), jnp.float32),
            jax.ShapeDtypeStruct((2, 2, width), jnp.float32),
            jax.ShapeDtypeStruct((2, hidden), jnp.float32),
            jax.ShapeDtypeStruct((2, width), jnp.float32),
            jax.ShapeDtypeStruct((width, classes), jnp.float32),
            jax.ShapeDtypeStruct((1, 1), jnp.float32),
        ),
        out_specs=[
            pl.BlockSpec((2, width), lambda g: (0, 0)),
            pl.BlockSpec((2, 2, width), lambda g: (0, 0, 0)),
            pl.BlockSpec((2, 2, width), lambda g: (0, 0, 0)),
            pl.BlockSpec((2, hidden), lambda g: (0, 0)),
            pl.BlockSpec((2, width), lambda g: (0, 0)),
            pl.BlockSpec((width, classes), lambda g: (0, 0)),
            pl.BlockSpec((1, 1), lambda g: (0, 0)),
        ],
        scratch_shapes=[pltpu.VMEM((count // 2, 2 * lanes), jnp.float32)],
        compiler_params=pltpu.CompilerParams(vmem_limit_bytes=4 * MIB),
        cost_estimate=cost(1.5),
        name="finish_small",
    )(*stacks)


def finish_conv(parts, conv_rows, small_rows, after=()):
    blocks, count = len(parts), len(parts[0])
    lanes = parts[0][0].shape[-1]
    flat = [part for block in parts for part in block]
    if conv_rows % ROW_TILE:
        sums = [sum(wide(part[:conv_rows]) for part in block) for block in parts]
        sums.append(paired([wide(part[conv_rows:]) for part in parts[0]]))
        return jnp.concatenate([low(total) for total in sums]), after

    def kernel(*refs):
        shard_ref, token_ref = refs[-2:]
        token_ref[...] = jnp.zeros(TOKEN.shape, TOKEN.dtype)
        shard_ref[blocks * conv_rows :] = low(
            paired([wide(refs[i][conv_rows:]) for i in range(count)])
        )
        for b in range(blocks):
            total = sum(wide(refs[b * count + i][:conv_rows]) for i in range(count))
            shard_ref[b * conv_rows : (b + 1) * conv_rows] = low(total)

    found = pl.pallas_call(
        kernel,
        in_specs=[WHOLE] * (len(flat) + len(after)),
        out_specs=[WHOLE] * 2,
        out_shape=[
            jax.ShapeDtypeStruct((blocks * conv_rows + small_rows, lanes), jnp.bfloat16),
            TOKEN,
        ],
        compiler_params=pltpu.CompilerParams(vmem_limit_bytes=8 * MIB),
        cost_estimate=cost(1.2),
        name="finish_conv",
    )(*flat, *after)
    return found[0], (found[1],)


def finish_ffn(merged, plain, conv_rows, ffn_rows, after=()):
    lanes, width = merged[0].shape[-1], plain[0].shape[-1]

    def cut_back(total):
        size = 2 * ffn_rows
        return jnp.concatenate(
            [total[i * size : (i + 1) * size] for i in range(width // lanes)], 1
        )

    if conv_rows % ROW_TILE or ffn_rows % ROW_TILE:
        sums = [sum(wide(part) for part in plain)]
        sums.append(cut_back(sum(wide(part[conv_rows:]) for part in merged)))
        return jnp.stack([each[:ffn_rows].T for each in sums]), jnp.stack(
            [each[ffn_rows:] for each in sums]
        ), after

    def kernel(*refs):
        in_ref, out_ref, token_ref = refs[-3:]
        token_ref[...] = jnp.zeros(TOKEN.shape, TOKEN.dtype)
        late = sum(wide(refs[i][conv_rows:]) for i in range(len(merged)))
        sums = [sum(wide(refs[len(merged) + i][...]) for i in range(len(plain))), cut_back(late)]
        for b in range(2):
            in_ref[b] = sums[b][:ffn_rows].T
            out_ref[b] = sums[b][ffn_rows:]

    found = pl.pallas_call(
        kernel,
        in_specs=[WHOLE] * (len(merged) + len(plain) + len(after)),
        out_specs=[WHOLE] * 3,
        out_shape=(
            jax.ShapeDtypeStruct((2, width, ffn_rows), jnp.float32),
            jax.ShapeDtypeStruct((2, ffn_rows, width), jnp.float32),
            TOKEN,
        ),
        compiler_params=pltpu.CompilerParams(vmem_limit_bytes=8 * MIB),
        cost_estimate=cost(1),
        name="finish_ffn",
    )(*merged, *plain, *after)
    return found[0], found[1], (found[2],)


def add_slots(parts, slots, after=(), reads=()):
    lanes = parts[0].shape[-1]
    rows = parts[0].size // (slots * lanes)
    parts = [part.reshape(slots, rows, lanes) for part in parts]
    block = rows // 4 if rows % (4 * ROW_TILE) == 0 else rows

    def kernel(*refs):
        out_refs, token_ref = refs[-1 - slots : -1], refs[-1]
        token_ref[...] = jnp.zeros(TOKEN.shape, TOKEN.dtype)
        for slot in range(slots):
            out_refs[slot][...] = low(sum(wide(refs[i][slot]) for i in range(len(parts))))

    found = pl.pallas_call(
        kernel,
        grid=(rows // block,),
        in_specs=[pl.BlockSpec((slots, block, lanes), lambda g: (0, g, 0))] * len(parts)
        + tokens(after)
        + [ANYWHERE] * len(reads),
        out_specs=[pl.BlockSpec((block, lanes), lambda g: (g, 0))] * slots + [TOKEN_SPEC],
        out_shape=[jax.ShapeDtypeStruct((rows, lanes), jnp.bfloat16)] * slots + [TOKEN],
        compiler_params=pltpu.CompilerParams(vmem_limit_bytes=8 * MIB),
        cost_estimate=cost(2),
        name="add_slots",
    )(*parts, *after, *reads)
    return found[:slots], found[slots]


def place_conv_grads(stacks, blocks, taps, slab, places, sizes):
    cores, seqs, acrosses = sizes[:3]
    peers, rows, lanes = stacks[0].shape
    channels = slab * seqs * acrosses
    if slab % ROW_TILE or rows % slab:
        full = jnp.stack([each[:, : blocks * taps * slab] for each in stacks])
        full = full.reshape(cores, seqs, acrosses, blocks, taps, slab, lanes)
        for axis, (place, size) in enumerate(zip(places[:3], sizes[:3])):
            full = relative(full, axis, place, size)
        return wide(
            full.transpose(3, 4, 1, 2, 5, 0, 6).reshape(blocks, taps, channels, cores * lanes)
        )
    stacks = [each.reshape(peers, rows // slab, slab, lanes) for each in stacks]

    def kernel(place_ref, *refs):
        out_ref = refs[-1]
        for c in range(cores):
            lane = pl.multiple_of(lax.rem(place_ref[0] - c + cores, cores) * lanes, lanes)
            for s in range(seqs):
                at_s = lax.rem(place_ref[1] - s + seqs, seqs)
                for a in range(acrosses):
                    at_a = lax.rem(place_ref[2] - a + acrosses, acrosses)
                    row = pl.multiple_of((at_s * acrosses + at_a) * slab, slab)
                    for b in range(blocks):
                        piece = wide(refs[c * blocks + b][s * acrosses + a, 0])
                        out_ref[b, 0, pl.ds(row, slab), pl.ds(lane, lanes)] = piece

    specs = [
        pl.BlockSpec((peers, 1, slab, lanes), lambda k, place, b=b: (0, b * taps + k, 0, 0))
        for b in range(blocks)
    ]
    return pl.pallas_call(
        kernel,
        grid_spec=pltpu.PrefetchScalarGridSpec(
            num_scalar_prefetch=1,
            grid=(taps,),
            in_specs=specs * cores,
            out_specs=pl.BlockSpec(
                (blocks, 1, channels, cores * lanes), lambda k, place: (0, k, 0, 0)
            ),
        ),
        out_shape=jax.ShapeDtypeStruct((blocks, taps, channels, cores * lanes), jnp.float32),
        compiler_params=pltpu.CompilerParams(vmem_limit_bytes=10 * MIB),
        cost_estimate=cost(5),
        name="place_conv_grads",
    )(
        jnp.stack(places[:3]).astype(jnp.int32),
        *[each for stack in stacks for each in [stack] * blocks],
    )


def copy_all(copies):
    for copy in copies:
        copy.start()
    for copy in copies:
        copy.wait()


def place_conv(pieces, places, sizes, after=(), reads=()):
    cores, seqs, acrosses, tap_peers = sizes
    taps, slab, lanes = pieces[0][0].shape[2:]
    inner = slab * seqs * acrosses * tap_peers
    if slab % ROW_TILE:
        full = jnp.stack([jnp.stack(row) for row in pieces])
        for axis, (place, size) in enumerate(zip(places, sizes)):
            full = relative(full, axis, place, size)
        return full.transpose(4, 3, 1, 2, 5, 0, 6).reshape(taps, inner, cores * lanes), after
    flat = [piece for row in pieces for piece in row]

    def kernel(place_ref, *refs):
        out_ref, token_ref, sem_ref = refs[-3:]
        token_ref[...] = jnp.zeros(TOKEN.shape, TOKEN.dtype)
        copies = []
        for c in range(cores):
            lane = lax.rem(place_ref[0] - c + cores, cores) * lanes
            for s in range(seqs):
                at_s = lax.rem(place_ref[1] - s + seqs, seqs)
                for a in range(acrosses):
                    at_a = lax.rem(place_ref[2] - a + acrosses, acrosses)
                    for t in range(tap_peers):
                        at_t = lax.rem(place_ref[3] - t + tap_peers, tap_peers)
                        row = ((at_t * seqs + at_s) * acrosses + at_a) * slab
                        copies.append(
                            pltpu.make_async_copy(
                                refs[c * seqs + s].at[a, t],
                                out_ref.at[
                                    :,
                                    pl.ds(pl.multiple_of(row, slab), slab),
                                    pl.ds(pl.multiple_of(lane, lanes), lanes),
                                ],
                                sem_ref.at[len(copies)],
                            )
                        )
        copy_all(copies)

    found = pl.pallas_call(
        kernel,
        in_specs=[SCALARS] + [ANYWHERE] * (len(flat) + len(reads)) + [WHOLE] * len(after),
        out_specs=[WHOLE] * 2,
        out_shape=[pltpu.HBM((taps, inner, cores * lanes), jnp.bfloat16), TOKEN],
        scratch_shapes=[pltpu.SemaphoreType.DMA((cores * seqs * acrosses * tap_peers,))],
        compiler_params=pltpu.CompilerParams(vmem_limit_bytes=12 * MIB),
        cost_estimate=cost(3),
        name="place_conv",
    )(jnp.stack(places).astype(jnp.int32), *flat, *reads, *after)
    return found[0], (found[1],)


def place_ffn(pieces, sizes, after=(), reads=()):
    cores, seqs, acrosses, tap_peers = sizes
    cuts, ffn_rows, lanes = pieces[0][0].shape[2:]
    cuts //= 2
    width = cuts * lanes
    units = seqs * acrosses * tap_peers * ffn_rows
    if ffn_rows % ROW_TILE:
        full = jnp.stack([jnp.stack(row) for row in pieces])
        full = full.reshape(cores, acrosses, seqs, tap_peers, 2, cuts, ffn_rows, lanes)
        full = full.transpose(4, 0, 1, 2, 3, 6, 5, 7).reshape(2, cores, units, width)
        return [full[0, c] for c in range(cores)], [full[1, c] for c in range(cores)], after
    flat = [piece for row in pieces for piece in row]

    def kernel(*refs):
        out_refs = refs[-2 - 2 * cores : -2]
        token_ref, sem_ref = refs[-2:]
        token_ref[...] = jnp.zeros(TOKEN.shape, TOKEN.dtype)
        copies = []
        for c in range(cores):
            for a in range(acrosses):
                for which in range(2):
                    for cut in range(cuts):
                        copies.append(
                            pltpu.make_async_copy(
                                refs[c * acrosses + a].at[:, :, which * cuts + cut],
                                out_refs[which * cores + c].at[
                                    a, :, :, :, pl.ds(cut * lanes, lanes)
                                ],
                                sem_ref.at[len(copies)],
                            )
                        )
        copy_all(copies)

    shape = pltpu.HBM((acrosses, seqs, tap_peers, ffn_rows, width), jnp.bfloat16)
    found = pl.pallas_call(
        kernel,
        in_specs=[ANYWHERE] * (len(flat) + len(reads)) + [WHOLE] * len(after),
        out_specs=[WHOLE] * (2 * cores + 1),
        out_shape=[shape] * (2 * cores) + [TOKEN],
        scratch_shapes=[pltpu.SemaphoreType.DMA((2 * cores * acrosses * cuts,))],
        compiler_params=pltpu.CompilerParams(vmem_limit_bytes=12 * MIB),
        cost_estimate=cost(2),
        name="place_ffn",
    )(*flat, *reads, *after)
    token = found[-1]
    found = [each.reshape(units, width) for each in found[:-1]]
    return found[:cores], found[cores:], (token,)


class Ring:
    def __init__(self, axis, size, index, pairs):
        self.axis, self.size, self.index, self.pairs = axis, size, index, pairs

    def shifted(self, value, by):
        return lax.ppermute(value, self.axis, self.pairs(lambda i: (i + by) % self.size))

    def swapped(self, value, bit):
        return lax.ppermute(value, self.axis, self.pairs(lambda i: i ^ bit))

    def gather(self, value):
        return [value] + [self.shifted(value, by) for by in range(1, self.size)]

    def swap(self, values):
        return [values[0]] + [self.shifted(values[by], -by) for by in range(1, self.size)]


def relative(value, axis, place, size):
    if size == 1:
        return value
    return jnp.stack(
        [
            lax.dynamic_index_in_dim(value, (place - slot) % size, axis, False)
            for slot in range(size)
        ],
        axis,
    )


def rings():
    peers = lax.axis_size("dp")
    cores = CORES if peers % CORES == 0 else 1
    columns = peers // cores
    place = lax.axis_index("dp")

    def plain(axis):
        size = lax.axis_size(axis)
        return Ring(
            axis, size, lax.axis_index(axis), lambda move: [(i, move(i)) for i in range(size)]
        )

    across = Ring(
        "dp",
        columns,
        place // cores,
        lambda move: [(i, move(i // cores) * cores + i % cores) for i in range(peers)],
    )
    core = Ring(
        "dp",
        cores,
        place % cores,
        lambda move: [(i, i // cores * cores + move(i % cores)) for i in range(peers)],
    )
    return core, across, plain("seq"), plain("tap")


class Reduce:
    def __init__(self, terms, order):
        self.order = order
        self.parts = [terms[0]] + [order[0].shifted(terms[s], -s) for s in range(1, order[0].size)]

    def step(self, level, after, reads=()):
        ring = self.order[level]
        found, token = add_slots(self.parts, ring.size, after, reads)
        self.parts = [found[0]] + [ring.shifted(found[s], -s) for s in range(1, ring.size)]
        return (token,)


def shared_copies(value, across, seq):
    peers, spans = lax.axis_size("dp"), lax.axis_size("seq")
    cores = peers // across.size

    def target(place, by_a, by_s):
        dp, at = place // spans, place % spans
        moved = (dp // cores + by_a) % across.size * cores + dp % cores
        return moved * spans + (at + by_s) % spans

    return [
        [
            value
            if by_a == by_s == 0
            else lax.ppermute(
                value,
                ("dp", "seq"),
                [(place, target(place, by_a, by_s)) for place in range(peers * spans)],
            )
            for by_a in range(across.size)
        ]
        for by_s in range(seq.size)
    ]


def passed_along(value, axis, by):
    peers = lax.axis_size(axis)
    pairs = [(i, i + by) for i in range(peers) if 0 <= i + by < peers]
    return lax.ppermute(value, axis, pairs)


def rims(source, reach_rows, seq, rim=None):
    span_rows = source.shape[0]
    if seq.size == 2 and reach_rows <= span_rows:
        if rim is None:
            first = (1 - seq.index) * (span_rows - reach_rows)
            rim = lax.dynamic_slice_in_dim(source, first, reach_rows, 0)
        return seq.shifted(rim, 1)
    left_parts = []
    right_parts = []
    distances = -(-reach_rows // span_rows)
    for distance in range(1, distances + 1):
        rim_count = min(span_rows, reach_rows - (distance - 1) * span_rows)
        left_parts.insert(0, passed_along(source[span_rows - rim_count :], "seq", distance))
        right_parts.append(passed_along(source[:rim_count], "seq", -distance))
    return left_parts, right_parts


def extend(source, found, seq, after=()):
    if isinstance(found, tuple):
        return join_rows(found[0] + [source] + found[1], after)
    reach, span = found.shape[0], source.shape[0]

    def kernel(place_ref, found_ref, source_ref, *refs):
        out_ref, token_ref = refs[-2:]
        token_ref[...] = jnp.zeros(TOKEN.shape, TOKEN.dtype)
        out_ref[reach : reach + span] = source_ref[...]
        zeros = jnp.zeros(found.shape, found.dtype)

        @pl.when(place_ref[0] == 0)
        def _():
            out_ref[:reach] = zeros
            out_ref[reach + span :] = found_ref[...]

        @pl.when(place_ref[0] != 0)
        def _():
            out_ref[:reach] = found_ref[...]
            out_ref[reach + span :] = zeros

    shape = jax.ShapeDtypeStruct((span + 2 * reach, source.shape[1]), source.dtype)
    extended, token = pl.pallas_call(
        kernel,
        in_specs=[SCALARS] + [WHOLE] * (2 + len(after)),
        out_specs=[WHOLE] * 2,
        out_shape=[shape, TOKEN],
        compiler_params=pltpu.CompilerParams(vmem_limit_bytes=10 * MIB),
        cost_estimate=cost(1.5),
        name="extend",
    )(seq.index.astype(jnp.int32)[None], found, source, *after)
    return extended, (token,)


def to_rows(values):
    windows, positions = values.shape[:2]
    cut = values.reshape((windows, positions // FIRST_DILATION, FIRST_DILATION) + values.shape[2:])
    return jnp.swapaxes(cut, 0, 1).reshape((windows * positions,) + values.shape[2:])


def from_rows(values, windows):
    cut = values.reshape((-1, windows, FIRST_DILATION) + values.shape[1:])
    return jnp.swapaxes(cut, 0, 1).reshape((windows, -1) + values.shape[1:])


def on_device(
    inputs,
    targets,
    masked,
    conv_weight,
    conv_bias,
    gains,
    shifts,
    in_weight,
    in_bias,
    out_weight,
    out_bias,
    head_weight,
):
    core, across, seq, tap = rings()
    taps = conv_weight.shape[1]
    channels = conv_weight.shape[2]
    width = conv_weight.shape[3]
    slab = channels // (seq.size * across.size)
    lanes = width // core.size
    hidden_width = in_bias.shape[1]
    ffn_rows = in_weight.shape[2]
    windows = inputs.shape[0]
    rows = windows * inputs.shape[1]
    steps = (FIRST_DILATION * windows, SECOND_DILATION * windows)
    units = hidden_width // core.size
    places = (core.index, seq.index, across.index, tap.index)
    sizes = (core.size, seq.size, across.size, tap.size)

    in_bias_placed = []
    for b in range(2):
        bias = in_bias[b].reshape(across.size, core.size, seq.size, tap.size, ffn_rows)
        for axis, ring in enumerate((across, core, seq, tap)):
            bias = relative(bias, axis, ring.index, ring.size)
        in_bias_placed.append(bias.transpose(1, 0, 2, 3, 4).reshape(core.size, units))

    def cut_ffn(piece):
        return piece.reshape(ffn_rows, core.size, lanes).swapaxes(0, 1).reshape(-1, lanes)

    def bundle(b):
        conv_piece = lax.dynamic_slice(
            conv_weight[b],
            (0, (seq.index * across.size + across.index) * slab, core.index * lanes),
            (taps, slab, lanes),
        )
        pieces = [
            conv_piece.reshape(taps * slab, lanes),
            cut_ffn(in_weight[b].T),
            cut_ffn(out_weight[b]),
        ]
        return jnp.concatenate(pieces)

    cuts = (
        (0, taps * slab, (taps, slab, lanes)),
        (taps * slab, taps * slab + 2 * core.size * ffn_rows, (2 * core.size, ffn_rows, lanes)),
    )

    def straight(arrays):
        return (arrays, ((0, None, arrays[0].shape),))

    conv_input = to_rows(inputs)
    stream = conv_input
    codes = to_rows(targets + masked * head_weight.shape[1])
    codes = jnp.broadcast_to(codes[:, None], (rows, 128))

    tap_parts = tap.gather(bundle(0))
    behind = bundle(1)
    (conv_part, ffn_part), last = restack([(tap_parts, cuts)], reads=[conv_input, behind])
    split = (tap.size + 1) // 2
    (behind,), last = hold([behind], last)
    late_parts = tap.gather(behind)
    extended, last = extend(conv_input, rims(conv_input, taps // 2 * steps[0], seq), seq, last)
    extended_parts = [extended] + [core.shifted(extended, -c) for c in range(1, core.size)]
    conv_parts, ffn_parts = across.gather(conv_part), seq.gather(ffn_part)
    (conv_part, ffn_part), last = restack(
        [straight(conv_parts), straight(ffn_parts)],
        reads=[late_parts[by] for by in range(1, tap.size) if by != split],
        after=last,
    )
    conv_parts, ffn_parts = seq.gather(conv_part), across.gather(ffn_part)
    conv_slots = [core.gather(conv_part)]
    ffn_slots = [core.gather(ffn_part)]
    held, last = hold(
        conv_parts[1:] + ffn_parts[1:],
        last,
        conv_slots[0][1:] + ffn_slots[0][1:] + late_parts[1:],
    )
    conv_slots += [core.gather(each) for each in held[: seq.size - 1]]
    ffn_slots += [core.gather(each) for each in held[seq.size - 1 :]]
    (late_conv, late_ffn), last = restack([(late_parts, cuts)], after=last)
    late_conv_parts, late_ffn_parts = across.gather(late_conv), seq.gather(late_ffn)

    def turned(slots):
        return [[each[c] for each in slots] for c in range(core.size)]

    conv_full, in_full, out_full = [None, None], [None, None], [None, None]
    conv_full[0], last = place_conv(
        turned(conv_slots), places, sizes, last, [part for each in ffn_slots for part in each[1:]]
    )
    (late_conv, late_ffn), last = restack(
        [straight(late_conv_parts), straight(late_ffn_parts)], after=last
    )
    late_conv_parts, late_ffn_parts = seq.gather(late_conv), across.gather(late_ffn)
    late_conv_slots = [core.gather(late_conv)]
    late_ffn_slots = [core.gather(late_ffn)]
    reaches = [taps // 2 * step for step in steps]
    rim_reaches = [reach if seq.size == 2 and reach <= rows else 0 for reach in reaches]
    saved = []
    reads = []
    rim = None
    for b in range(2):
        if b == 1:
            found = rims(conv_input, reaches[1], seq, rim)
            held, last = hold(late_conv_parts[1:] + late_ffn_parts[1:], last)
            late_conv_slots += [core.gather(each) for each in held[: seq.size - 1]]
            late_ffn_slots += [core.gather(each) for each in held[seq.size - 1 :]]
            conv_full[1], last = place_conv(turned(late_conv_slots), places, sizes, last)
            in_full[1], out_full[1], last = place_ffn(turned(late_ffn_slots), sizes, last)
            extended, last = extend(conv_input, found, seq, last)
            extended_parts = [extended] + [core.shifted(extended, -c) for c in range(1, core.size)]
        (normed_conv, conv_slope, stream, lowered), last = conv_forward(
            extended,
            conv_full[b],
            stream,
            conv_bias[b],
            gains[b, 0],
            shifts[b, 0],
            steps[b],
            last,
            reads,
        )
        reads = extended_parts[1:]
        if b == 0:
            in_full[0], out_full[0], last = place_ffn(turned(ffn_slots), sizes, last)
            reads = reads + late_conv_slots[0][1:] + late_ffn_slots[0][1:]
        active, hidden_slopes, (normed_ffn, scale_ffn, stream, conv_input), packets, rim, last = (
            ffn_forward(
                lowered,
                stream,
                in_full[b],
                out_full[b],
                [in_bias_placed[b][c] for c in range(core.size)],
                out_bias[b],
                gains[b, 1],
                shifts[b, 1],
                seq.index,
                rim_reaches[1] if b == 0 else 0,
                b == 1,
                last,
                reads,
            )
        )
        packets = [core.shifted(packet, -1 - c) for c, packet in enumerate(packets)]
        reads = packets
        saved.append(
            (
                extended_parts,
                conv_slope,
                normed_conv,
                (active, lowered, packets),
                hidden_slopes,
                normed_ffn,
                scale_ffn,
            )
        )

    final_state = from_rows(conv_input, windows)
    (stream_grad, head_grad, loss_rows), last = head_and_loss(stream, head_weight, codes, last)

    ffn_rows_of_sums = [None, None]
    conv_rows_of_sums = [None, None]
    in_bias_grads = [None, None]
    ffn_sums = [None, None]
    conv_sums = [None, None]
    merged = [None, None]

    def groups(halves):
        half = (tap.size + 1) // 2
        return [(each.parts, slots) for each, slots in zip(halves, (half, tap.size - half))]

    for b in (1, 0):
        (
            extended_parts,
            conv_slope,
            normed_conv,
            active_pair,
            hidden_slopes,
            normed_ffn,
            scale_ffn,
        ) = saved[b]
        output_grad, hidden_grad, biases, packets, ffn_rows_of_sums[b], last = ffn_back_hidden(
            stream_grad, normed_ffn, scale_ffn, gains[b, 1], out_full[b], hidden_slopes, last
        )
        if b == 1:
            arrived_packets = [core.shifted(packet, -1 - c) for c, packet in enumerate(packets)]
        if b == 0:
            for each in ffn_sums[1]:
                last = each.step(1, last)
            for each in conv_sums[1]:
                last = each.step(1, last)
        stream_grad, conv_grad, conv_cuts, relayed, rim, conv_rows_of_sums[b], last = ffn_back_stream(
            stream_grad,
            hidden_grad,
            packets,
            in_full[b],
            normed_conv,
            conv_slope,
            gains[b, 0],
            places,
            rim_reaches[b],
            last,
            reads,
            relay=b == 0,
        )
        reads = []
        if b == 0:
            merged[1], last = merge_slots(
                groups(conv_sums[1]), groups(ffn_sums[1]), last
            )
            sent = [rim] if rim is not None else []
            held, last = hold(list(conv_cuts) + list(relayed) + sent, last)
            conv_cuts, relayed = held[: core.size - 1], held[core.size - 1 : 2 * core.size - 2]
            rim = held[-1] if sent else None
            merged[1] = tap.swap(merged[1])
            arrived_packets = [core.shifted(packet, -1 - c) for c, packet in enumerate(relayed)]
        arrived = [core.shifted(conv_cuts[c - 1], -c) for c in range(1, core.size)]
        in_bias_grads[b] = list(biases)
        found_rims = rims(conv_grad, reaches[b], seq, rim)

        def ffn_grads(last):
            active, lowered, packets = active_pair
            if core.size == 1:
                packets = []
            first, second, token = ffn_weight_grad(
                (
                    (hidden_grad, lowered, [(g, p) for g, p in zip(arrived_packets, packets)]),
                    (active, output_grad, [(p, g) for g, p in zip(arrived_packets, packets)]),
                ),
                sizes,
                ffn_rows,
                last,
            )
            found = [Reduce(first, (across, seq))]
            if second:
                found.append(Reduce(second, (seq, across)))
            return found, (token,)

        def conv_grads(last, reads=()):
            first, second, token = conv_weight_grad(
                extended_parts, conv_grad, arrived, places, sizes, taps, steps[b], last, reads
            )
            found = [Reduce(first, (seq, across))]
            if second:
                found.append(Reduce(second, (across, seq)))
            return found, (token,)

        if b == 1:
            ffn_sums[1], last = ffn_grads(last)
            extended_grad, last = extend(conv_grad, found_rims, seq, last)
            conv_sums[1], last = conv_grads(last)
        else:
            conv_sums[0], last = conv_grads(last, arrived_packets)
            extended_grad, last = extend(conv_grad, found_rims, seq, last)
            ffn_sums[0], last = ffn_grads(last)
            for each in conv_sums[0]:
                last = each.step(1, last, merged[1][1:])
        stream_grad, last = conv_data_grad(
            extended_grad,
            conv_full[b],
            stream_grad,
            steps[b],
            jnp.float32 if b == 1 else jnp.bfloat16,
            last,
        )

    grad_inputs = from_rows(stream_grad, windows)

    row_groups = [(each, 3) for each in conv_rows_of_sums + ffn_rows_of_sums]
    row_groups.append((head_grad, head_weight.shape[1]))
    packed, last = pack_small(row_groups, in_bias_grads, loss_rows, places, sizes, ffn_rows, last)

    conv_rows = taps * slab
    merged[0], last = append_slots(groups(conv_sums[0]), [packed], last, [final_state])
    merged[0] = tap.swap(merged[0])
    for each in ffn_sums[0]:
        last = each.step(1, last)
    shards, last = finish_conv([merged[0], merged[1]], conv_rows, packed.shape[0], last)
    ffn_late, last = append_slots(groups(ffn_sums[0]), [], last, [grad_inputs])
    ffn_late = tap.swap(ffn_late)
    copies = [each for row in shared_copies(shards, across, seq) for each in row]
    grad_in, grad_out, last = finish_ffn(merged[1], ffn_late, conv_rows, ffn_rows, last)
    (stack,), last = restack([straight(copies)], after=last)
    stacks = core.gather(stack)
    (
        grad_conv_bias,
        grad_gains,
        grad_shifts,
        grad_in_bias,
        grad_out_bias,
        grad_head_weight,
        loss,
    ) = finish_small(
        stacks, 2 * conv_rows, width, head_weight.shape[1], hidden_width, places, sizes
    )
    grad_conv = place_conv_grads(stacks, 2, taps, slab, places, sizes)
    return (
        final_state,
        grad_inputs,
        grad_conv,
        grad_conv_bias,
        grad_gains,
        grad_shifts,
        grad_in,
        grad_in_bias,
        grad_out,
        grad_out_bias,
        grad_head_weight,
        loss.reshape(()),
    )


def solution(mesh):
    placed = (
        P(("dp", "tap"), "seq", None),
        P(("dp", "tap"), "seq"),
        P(("dp", "tap"), "seq"),
        P(None, None, "tap", None),
        P(),
        P(),
        P(),
        P(None, None, ("dp", "seq", "tap")),
        P(),
        P(None, ("dp", "seq", "tap"), None),
        P(),
        P(),
    )
    return jax.shard_map(
        on_device,
        mesh=mesh,
        in_specs=placed,
        out_specs=(
            P(("dp", "tap"), "seq", None),
            P(("dp", "tap"), "seq", None),
            P(None, None, "tap", None),
            P(),
            P(),
            P(),
            P(None, None, ("dp", "seq", "tap")),
            P(),
            P(None, ("dp", "seq", "tap"), None),
            P(),
            P(),
            P(),
        ),
        check_vma=False,
    )
```

profile of v0, /device:TPU:0, one launch (start us, length us, event | category | flops | bytes accessed | tf_op | source)
XLA Modules:
  0.0 378.6 jit_solution(1735351679738933336)
XLA Ops:
  4.4 5.1 %collective-permute-start.3 = (bf16[544,256]{1,0:T(8,128)(2,1)S(1)}, bf16[544,256]{1,0:T(8,128)(2,1)S(1)}, u32[]{:S(2)}, u32[]{:S(2)}) collective-permute-start(bf16[544,256]{1,0:T(8,128)(2,1)S(1)} %pad_maximum_fusion.1.refs_0_), channel_id=1, source_target_pairs={{0,3},{1,0},{2,1},{3,2},{4,7},{5,4},{6,5},{7,6},{8,11},{9,8},{10,9... | collective-permute-start | bytes 835592 | tf_op jit(solution)/shard_map/ppermute | solution.py:1428
  16.6 16.6 %collective-permute-done.2.refs_2_ = bf16[544,256]{1,0:T(8,128)(2,1)S(1)} collective-permute-done((bf16[544,256]{1,0:T(8,128)(2,1)S(1)}, bf16[544,256]{1,0:T(8,128)(2,1)S(1)}, u32[]{:S(2)}, u32[]{:S(2)}) %collective-permute-start.2) | collective-permute-done | bytes 278560 | tf_op jit(solution)/shard_map/ppermute | solution.py:1428
  42.0 9.9 %collective-permute-done.found_ref = bf16[64,512]{1,0:T(8,128)(2,1)S(1)} collective-permute-done((bf16[64,512]{1,0:T(8,128)(2,1)S(1)}, bf16[64,512]{1,0:T(8,128)(2,1)S(1)}, u32[]{:S(2)}, u32[]{:S(2)}) %collective-permute-start) | collective-permute-done | bytes 65568 | tf_op jit(solution)/shard_map/ppermute | solution.py:1428
  55.0 2.7 restack.6
  61.5 13.3 %collective-permute-done.12.refs_5_.refs_2_ = bf16[544,256]{1,0:T(8,128)(2,1)} collective-permute-done((bf16[544,256]{1,0:T(8,128)(2,1)}, bf16[544,256]{1,0:T(8,128)(2,1)}, u32[]{:S(2)}, u32[]{:S(2)}) %collective-permute-start.12) | collective-permute-done | bytes 278560 | tf_op jit(solution)/shard_map/ppermute | solution.py:1428
  74.8 9.4 %collective-permute-done.9.refs_1_ = bf16[2,4,4,64,256]{4,3,2,1,0:T(8,128)(2,1)} collective-permute-done((bf16[2,4,4,64,256]{4,3,2,1,0:T(8,128)(2,1)}, bf16[2,4,4,64,256]{4,3,2,1,0:T(8,128)(2,1)}, u32[]{:S(2)}, u32[]{:S(2)}) %collective-permute-start.9) | collective-permute-done | bytes 1048608 | tf_op jit(solution)/shard_map/ppermute | solution.py:1428
  95.2 4.8 %place_conv.2 = (bf16[9,512,512]{2,1,0:T(8,128)(2,1)}, f32[8,128]{1,0:T(8,128)S(1)}) custom-call(s32[4]{0:T(128)S(1)} %pad_add_fusion.place_ref, bf16[2,4,9,32,256]{4,3,2,1,0:T(8,128)(2,1)} %get-tuple-element.203.refs_0_, bf16[2,4,9,32,256]{4,3,2,1,0:T(8,128)(2,1)S(1)} %get-tuple-element.206.refs_1_, ...), custom_call_target="tpu_custom_call" | custom-call | flops 3300000000 | bytes 10500000 | tf_op jit(solution)/shard_map/place_conv/pallas_call | solution.py:1361
  100.0 8.1 %collective-permute-done.16.refs_3_ = bf16[4,4,64,256]{3,2,1,0:T(8,128)(2,1)S(1)} collective-permute-done((bf16[4,4,64,256]{3,2,1,0:T(8,128)(2,1)S(1)}, bf16[4,4,64,256]{3,2,1,0:T(8,128)(2,1)S(1)}, u32[]{:S(2)}, u32[]{:S(2)}) %collective-permute-start.16) | collective-permute-done | bytes 524320 | tf_op jit(solution)/shard_map/ppermute | solution.py:1428
  111.1 11.6 %conv_forward.2 = (bf16[1024,512]{1,0:T(8,128)(2,1)}, bf16[1024,512]{1,0:T(8,128)(2,1)}, f32[1024,512]{1,0:T(8,128)}, bf16[1024,512]{1,0:T(8,128)(2,1)S(1)}, f32[8,128]{1,0:T(8,128)S(1)}) custom-call(bf16[1152,512]{1,0:T(8,128)(2,1)} %get-tuple-element.198.extended_ref.refs_0_, bf16[9,512,512]{2,1,0:T(8,128)(2,1)} %get-tuple-element.210.weight_ref, ...), custom_call_target="tpu_custom_call" | custom-call | flops 9900000256 | bytes 31500000 | tf_op jit(solution)/shard_map/conv_forward/pallas_call | solution.py:124
  122.7 4.3 %place_ffn.2 = (bf16[2,2,4,64,512]{4,3,2,1,0:T(8,128)(2,1)}, bf16[2,2,4,64,512]{4,3,2,1,0:T(8,128)(2,1)}, bf16[2,2,4,64,512]{4,3,2,1,0:T(8,128)(2,1)}, bf16[2,2,4,64,512]{4,3,2,1,0:T(8,128)(2,1)}, f32[8,128]{1,0:T(8,128)S(1)}) custom-call(bf16[2,4,4,64,256]{4,3,2,1,0:T(8,128)(2,1)} %get-tuple-element.204.refs_0_, ...), custom_call_target="tpu_custom_call" | custom-call | flops 2200000000 | bytes 7000000 | tf_op jit(solution)/shard_map/place_ffn/pallas_call | solution.py:1408
  127.0 13.9 %ffn_forward.2 = (bf16[1024,1024]{1,0:T(8,128)(2,1)}, bf16[1024,1024]{1,0:T(8,128)(2,1)}, bf16[1024,1024]{1,0:T(8,128)(2,1)}, bf16[1024,512]{1,0:T(8,128)(2,1)},...) custom-call(s32[1]{0:T(128)} %bitcast.place_ref, ...), custom_call_target="tpu_custom_call" | custom-call | flops 12099999744 | bytes 38500000 | tf_op jit(solution)/shard_map/ffn_forward/pallas_call | solution.py:232
  143.3 5.0 %collective-permute-done.24.refs_3_ = bf16[2,4,9,32,256]{4,3,2,1,0:T(8,128)(2,1)S(1)} collective-permute-done((bf16[2,4,9,32,256]{4,3,2,1,0:T(8,128)(2,1)S(1)}, bf16[2,4,9,32,256]{4,3,2,1,0:T(8,128)(2,1)S(1)}, u32[]{:S(2)}, u32[]{:S(2)}) %collective-permute-start.24) | collective-permute-done | bytes 1179680 | tf_op jit(solution)/shard_map/ppermute | solution.py:1428
  148.3 4.6 %place_conv.3 = (bf16[9,512,512]{2,1,0:T(8,128)(2,1)}, f32[8,128]{1,0:T(8,128)S(1)}) custom-call(s32[4]{0:T(128)S(1)} %pad_add_fusion.place_ref, bf16[2,4,9,32,256]{4,3,2,1,0:T(8,128)(2,1)S(1)} %get-tuple-element.223.refs_0_, bf16[2,4,9,32,256]{4,3,2,1,0:T(8,128)(2,1)S(1)} %get-tuple-element.229.refs_1_, ...), custom_call_target="tpu_custom_call" | custom-call | flops 3300000000 | bytes 10500000 | tf_op jit(solution)/shard_map/place_conv/pallas_call | solution.py:1361
  157.3 11.7 %conv_forward.3 = (bf16[1024,512]{1,0:T(8,128)(2,1)}, bf16[1024,512]{1,0:T(8,128)(2,1)}, f32[1024,512]{1,0:T(8,128)}, bf16[1024,512]{1,0:T(8,128)(2,1)S(1)}, f32[8,128]{1,0:T(8,128)S(1)}) custom-call(bf16[2048,512]{1,0:T(8,128)(2,1)S(1)} %get-tuple-element.233.extended_ref.refs_0_, bf16[9,512,512]{2,1,0:T(8,128)(2,1)} %get-tuple-element.234.weight_ref, ...), custom_call_target="tpu_custom_call" | custom-call | flops 9900000256 | bytes 31500000 | tf_op jit(solution)/shard_map/conv_forward/pallas_call | solution.py:124
  169.0 12.1 %ffn_forward.3 = (bf16[1024,1024]{1,0:T(8,128)(2,1)}, bf16[1024,1024]{1,0:T(8,128)(2,1)}, bf16[1024,1024]{1,0:T(8,128)(2,1)}, bf16[1024,512]{1,0:T(8,128)(2,1)},...) custom-call(s32[1]{0:T(128)} %bitcast.place_ref, ...), custom_call_target="tpu_custom_call" | custom-call | flops 12099999744 | bytes 38500000 | tf_op jit(solution)/shard_map/ffn_forward/pallas_call | solution.py:232
  181.8 6.0 %head_and_loss.1 = (f32[1024,512]{1,0:T(8,128)S(1)}, f32[8,512]{1,0:T(8,128)S(1)}, f32[8,128]{1,0:T(8,128)S(1)}, f32[8,128]{1,0:T(8,128)S(1)}) custom-call(f32[1024,512]{1,0:T(8,128)S(1)} %get-tuple-element.246.stream_ref, f32[512,128]{1,0:T(8,128)S(1)} %pad.4.head_ref, s32[1024,128]{1,0:T(8,128)S(1)} %broadcast_in_dim.8.code_ref, ...), custom_call_target="tpu_custom_call" | custom-call | flops 6600000000 | bytes 21000000 | tf_op jit(solution)/shard_map/head_and_loss/pallas_call | solution.py:331
  187.9 19.3 %ffn_back_hidden.2 = (bf16[1024,512]{1,0:T(8,128)(2,1)S(1)}, bf16[1024,1024]{1,0:T(8,128)(2,1)}, f32[1,1024]{1,0:T(1,128)S(1)}, f32[1,1024]{1,0:T(1,128)S(1)}, b...) custom-call(f32[1024,512]{1,0:T(8,128)S(1)} %get-tuple-element.248.upstream_ref, ...), custom_call_target="tpu_custom_call" | custom-call | flops 6600000000 | bytes 21000000 | tf_op jit(solution)/shard_map/ffn_back_hidden/pallas_call | solution.py:397
  207.3 7.5 %ffn_back_stream.2 = (f32[1024,512]{1,0:T(8,128)S(1)}, bf16[1024,512]{1,0:T(8,128)(2,1)S(1)}, bf16[1024,256]{1,0:T(8,128)(2,1)S(1)}, bf16[512,512]{1,0:T(8,128)(...) custom-call(s32[2]{0:T(128)S(1)} %pad_add_fusion.1.core_ref, f32[1024,512]{1,0:T(8,128)S(1)} %get-tuple-element.248.upstream_ref, ...), custom_call_target="tpu_custom_call" | custom-call | flops 5500000256 | bytes 17500000 | tf_op jit(solution)/shard_map/ffn_back_stream/pallas_call | solution.py:505
  216.6 7.6 %ffn_weight_grad.2 = (bf16[2,2,2,64,512]{4,3,2,1,0:T(8,128)(2,1)S(1)}, bf16[2,2,2,64,512]{4,3,2,1,0:T(8,128)(2,1)S(1)}, bf16[2,2,2,64,512]{4,3,2,1,0:T(8,128)(2,...) custom-call(bf16[1024,1024]{1,0:T(8,128)(2,1)} %get-tuple-element.256.refs_0_, ...), custom_call_target="tpu_custom_call" | custom-call | flops 8800000000 | bytes 28000000 | tf_op jit(solution)/shard_map/ffn_weight_grad/pallas_call | solution.py:873
  226.2 3.3 collective-permute-done.28.found_ref
  229.7 9.6 %conv_weight_grad.2 = (bf16[2,2,9,32,256]{4,3,2,1,0:T(8,128)(2,1)S(1)}, bf16[2,2,9,32,256]{4,3,2,1,0:T(8,128)(2,1)S(1)}, bf16[2,2,9,32,256]{4,3,2,1,0:T(8,128)(2...) custom-call(s32[4]{0:T(128)S(1)} %pad_add_fusion.place_ref, ...), custom_call_target="tpu_custom_call" | custom-call | flops 9900000256 | bytes 31500000 | tf_op jit(solution)/shard_map/conv_weight_grad/pallas_call | solution.py:765
  242.4 7.6 %conv_data_grad.2 = (f32[1024,512]{1,0:T(8,128)S(1)}, f32[8,128]{1,0:T(8,128)S(1)}) custom-call(bf16[2048,512]{1,0:T(8,128)(2,1)S(1)} %get-tuple-element.266.extended_ref, bf16[9,512,512]{2,1,0:T(8,128)(2,1)} %get-tuple-element.234.weight_ref, f32[1024,512]{1,0:T(8,128)S(1)} %get-tuple-element.267.upstream_ref, f32[8,128]{1,0:T(8,128)S(1)} %get-tuple-element.270.refs_0_), custom_call_target="tpu_custom_call" | custom-call | flops 6600000000 | bytes 21000000 | tf_op jit(solution)/shard_map/conv_data_grad/pallas_call | solution.py:593
  250.0 8.1 %ffn_back_hidden.3 = (bf16[1024,512]{1,0:T(8,128)(2,1)S(1)}, bf16[1024,1024]{1,0:T(8,128)(2,1)}, f32[1,1024]{1,0:T(1,128)S(1)}, f32[1,1024]{1,0:T(1,128)S(1)}, b...) custom-call(f32[1024,512]{1,0:T(8,128)S(1)} %get-tuple-element.271.upstream_ref, ...), custom_call_target="tpu_custom_call" | custom-call | flops 6600000000 | bytes 21000000 | tf_op jit(solution)/shard_map/ffn_back_hidden/pallas_call | solution.py:397
  264.6 8.5 %ffn_back_stream.3 = (f32[1024,512]{1,0:T(8,128)S(1)}, bf16[1024,512]{1,0:T(8,128)(2,1)S(1)}, bf16[1024,256]{1,0:T(8,128)(2,1)}, bf16[1024,1536]{1,0:T(8,128)(2,...) custom-call(s32[2]{0:T(128)S(1)} %pad_add_fusion.1.core_ref, ...), custom_call_target="tpu_custom_call" | custom-call | flops 5500000256 | bytes 17500000 | tf_op jit(solution)/shard_map/ffn_back_stream/pallas_call | solution.py:505
  288.5 9.8 %conv_weight_grad.3 = (bf16[2,2,9,32,256]{4,3,2,1,0:T(8,128)(2,1)S(1)}, bf16[2,2,9,32,256]{4,3,2,1,0:T(8,128)(2,1)S(1)}, bf16[2,2,9,32,256]{4,3,2,1,0:T(8,128)(2...) custom-call(s32[4]{0:T(128)S(1)} %pad_add_fusion.place_ref, ...), custom_call_target="tpu_custom_call" | custom-call | flops 9900000256 | bytes 31500000 | tf_op jit(solution)/shard_map/conv_weight_grad/pallas_call | solution.py:765
  300.9 8.8 %ffn_weight_grad.3 = (bf16[2,2,2,64,512]{4,3,2,1,0:T(8,128)(2,1)S(1)}, bf16[2,2,2,64,512]{4,3,2,1,0:T(8,128)(2,1)S(1)}, bf16[2,2,2,64,512]{4,3,2,1,0:T(8,128)(2,...) custom-call(bf16[1024,1024]{1,0:T(8,128)(2,1)} %get-tuple-element.279.refs_0_, ...), custom_call_target="tpu_custom_call" | custom-call | flops 8800000000 | bytes 28000000 | tf_op jit(solution)/shard_map/ffn_weight_grad/pallas_call | solution.py:873
  317.3 7.6 %conv_data_grad.3 = (bf16[1024,512]{1,0:T(8,128)(2,1)S(1)}, f32[8,128]{1,0:T(8,128)S(1)}) custom-call(bf16[1152,512]{1,0:T(8,128)(2,1)S(1)} %get-tuple-element.313.extended_ref, bf16[9,512,512]{2,1,0:T(8,128)(2,1)} %get-tuple-element.210.weight_ref, f32[1024,512]{1,0:T(8,128)S(1)} %copy-done.29, f32[8,128]{1,0:T(8,128)S(1)} %get-tuple-element.327.refs_0_), custom_call_target="tpu_custom_call" | custom-call | flops 6600000000 | bytes 21000000 | tf_op jit(solution)/shard_map/conv_data_grad/pallas_call | solution.py:593
  325.9 4.7 %collective-permute-done.48 = bf16[576,256]{1,0:T(8,128)(2,1)S(1)} collective-permute-done((bf16[576,256]{1,0:T(8,128)(2,1)S(1)}, bf16[576,256]{1,0:T(8,128)(2,1)S(1)}, u32[]{:S(2)}, u32[]{:S(2)}) %collective-permute-start.48) | collective-permute-done | bytes 294944 | tf_op jit(solution)/shard_map/ppermute | solution.py:1428
  340.0 2.6 copy.72
  344.0 4.5 %collective-permute-done.50.refs_2_ = bf16[352,256]{1,0:T(8,128)(2,1)} collective-permute-done((bf16[352,256]{1,0:T(8,128)(2,1)S(1)}, bf16[352,256]{1,0:T(8,128)(2,1)}, u32[]{:S(2)}, u32[]{:S(2)}) %collective-permute-start.50) | collective-permute-done | bytes 180256 | tf_op jit(solution)/shard_map/ppermute | solution.py:1428
  359.2 6.1 %collective-permute-done.60.refs_6_ = bf16[128,512]{1,0:T(8,128)(2,1)S(1)} collective-permute-done((bf16[128,512]{1,0:T(8,128)(2,1)S(1)}, bf16[128,512]{1,0:T(8,128)(2,1)S(1)}, u32[]{:S(2)}, u32[]{:S(2)}) %collective-permute-start.60) | collective-permute-done | bytes 131104 | tf_op jit(solution)/shard_map/ppermute | solution.py:1428
  373.4 5.0 %place_conv_grads.1 = f32[2,9,128,512]{3,2,1,0:T(8,128)} custom-call(s32[3]{0:T(128)S(1)} %pad_add_fusion.2.place_ref, bf16[4,20,32,256]{3,2,1,0:T(8,128)(2,1)S(1)} %bitcast.125, bf16[4,20,32,256]{3,2,1,0:T(8,128)(2,1)S(1)} %bitcast.126, bf16[4,20,32,256]{3,2,1,0:T(8,128)(2,1)S(1)} %bitcast.127, bf16[4,20,32,256]{3,2,1,0:T(8,128)(2,1)S(1)} %bitcast.128), custom_call_target="tpu_custom_call" | custom-call | flops 5500000256 | bytes 17500000 | tf_op jit(solution)/shard_map/place_conv_grads/pallas_call | solution.py:1297
  (293 shorter events, 116.8 us)
Async XLA Ops:
  9.5 23.7 %collective-permute-start.2 = (bf16[544,256]{1,0:T(8,128)(2,1)S(1)}, bf16[544,256]{1,0:T(8,128)(2,1)S(1)}, u32[]{:S(2)}, u32[]{:S(2)}) collective-permute-start(bf16[544,256]{1,0:T(8,128)(2,1)S(1)} %pad_maximum_fusion.1.refs_0_), channel_id=1, source_target_pairs={{0,2},{1,3},{2,0},{3,1},{4,6},{5,7},{6,4},{7,5},{8,10},{9,11},{10,... | collective-permute-start | bytes 835592 | tf_op jit(solution)/shard_map/ppermute | solution.py:1428
  9.5 23.7 %collective-permute-start.1 = (bf16[544,256]{1,0:T(8,128)(2,1)S(1)}, bf16[544,256]{1,0:T(8,128)(2,1)S(1)}, u32[]{:S(2)}, u32[]{:S(2)}) collective-permute-start(bf16[544,256]{1,0:T(8,128)(2,1)S(1)} %pad_maximum_fusion.1.refs_0_), channel_id=1, source_target_pairs={{0,1},{1,2},{2,3},{3,0},{4,5},{5,6},{6,7},{7,4},{8,9},{9,10},{10,1... | collective-permute-start | bytes 835592 | tf_op jit(solution)/shard_map/ppermute | solution.py:1428
  36.4 18.5 %collective-permute-start.4 = (bf16[4,9,32,256]{3,2,1,0:T(8,128)(2,1)S(1)}, bf16[4,9,32,256]{3,2,1,0:T(8,128)(2,1)S(1)}, u32[]{:S(2)}, u32[]{:S(2)}) collective-permute-start(bf16[4,9,32,256]{3,2,1,0:T(8,128)(2,1)S(1)} %bitcast.132), channel_id=1, source_target_pairs={{0,16},{8,24},{16,0},{24,8},{1,17},{9,25},{17,1},{25,9},{2,18},{10... | collective-permute-start | bytes 1769480 | tf_op jit(solution)/shard_map/ppermute | solution.py:1428
  38.0 17.0 %collective-permute-start.5 = (bf16[4,4,64,256]{3,2,1,0:T(8,128)(2,1)S(1)}, bf16[4,4,64,256]{3,2,1,0:T(8,128)(2,1)}, u32[]{:S(2)}, u32[]{:S(2)}) collective-permute-start(bf16[4,4,64,256]{3,2,1,0:T(8,128)(2,1)S(1)} %bitcast.148), channel_id=1, source_target_pairs={{0,4},{4,0},{1,5},{5,1},{2,6},{6,2},{3,7},{7,3},{8,12},{12,8},{9,1... | collective-permute-start | bytes 1572872 | tf_op jit(solution)/shard_map/ppermute | solution.py:1428
  39.5 15.4 %collective-permute-start.6 = (bf16[544,256]{1,0:T(8,128)(2,1)S(1)}, bf16[544,256]{1,0:T(8,128)(2,1)S(1)}, u32[]{:S(2)}, u32[]{:S(2)}) collective-permute-start(bf16[544,256]{1,0:T(8,128)(2,1)S(1)} %get-tuple-element.201.refs_0_), channel_id=1, source_target_pairs={{0,1},{1,2},{2,3},{3,0},{4,5},{5,6},{6,7},{7,4},{8,9},{9,10},{10,1... | collective-permute-start | bytes 835592 | tf_op jit(solution)/shard_map/ppermute | solution.py:1428
  57.7 26.5 %collective-permute-start.10 = (bf16[2,4,9,32,256]{4,3,2,1,0:T(8,128)(2,1)}, bf16[2,4,9,32,256]{4,3,2,1,0:T(8,128)(2,1)S(1)}, u32[]{:S(2)}, u32[]{:S(2)}) collective-permute-start(bf16[2,4,9,32,256]{4,3,2,1,0:T(8,128)(2,1)} %get-tuple-element.203.refs_0_), channel_id=1, source_target_pairs={{0,8},{8,0},{16,24},{24,16},{1,9},{9,1},{17,25},{25,17},{2,10},{10... | collective-permute-start | bytes 3538952 | tf_op jit(solution)/shard_map/ppermute | solution.py:1428
  57.8 28.6 %collective-permute-start.8 = (bf16[2,4,9,32,256]{4,3,2,1,0:T(8,128)(2,1)}, bf16[2,4,9,32,256]{4,3,2,1,0:T(8,128)(2,1)S(1)}, u32[]{:S(2)}, u32[]{:S(2)}) collective-permute-start(bf16[2,4,9,32,256]{4,3,2,1,0:T(8,128)(2,1)} %get-tuple-element.203.refs_0_), channel_id=1, source_target_pairs={{0,4},{4,0},{1,5},{5,1},{2,6},{6,2},{3,7},{7,3},{8,12},{12,8},{9,1... | collective-permute-start | bytes 3538952 | tf_op jit(solution)/shard_map/ppermute | solution.py:1428
  58.3 16.5 %collective-permute-start.11 = (bf16[2,4,4,64,256]{4,3,2,1,0:T(8,128)(2,1)}, bf16[2,4,4,64,256]{4,3,2,1,0:T(8,128)(2,1)}, u32[]{:S(2)}, u32[]{:S(2)}) collective-permute-start(bf16[2,4,4,64,256]{4,3,2,1,0:T(8,128)(2,1)} %get-tuple-element.204.refs_0_), channel_id=1, source_target_pairs={{0,8},{8,0},{16,24},{24,16},{1,9},{9,1},{17,25},{25,17},{2,10},{10... | collective-permute-start | bytes 3145736 | tf_op jit(solution)/shard_map/ppermute | solution.py:1428
  58.5 25.7 %collective-permute-start.9 = (bf16[2,4,4,64,256]{4,3,2,1,0:T(8,128)(2,1)}, bf16[2,4,4,64,256]{4,3,2,1,0:T(8,128)(2,1)}, u32[]{:S(2)}, u32[]{:S(2)}) collective-permute-start(bf16[2,4,4,64,256]{4,3,2,1,0:T(8,128)(2,1)} %get-tuple-element.204.refs_0_), channel_id=1, source_target_pairs={{0,16},{8,24},{16,0},{24,8},{1,17},{9,25},{17,1},{25,9},{2,18},{10... | collective-permute-start | bytes 3145736 | tf_op jit(solution)/shard_map/ppermute | solution.py:1428
  59.3 15.6 %collective-permute-start.12 = (bf16[544,256]{1,0:T(8,128)(2,1)}, bf16[544,256]{1,0:T(8,128)(2,1)}, u32[]{:S(2)}, u32[]{:S(2)}) collective-permute-start(bf16[544,256]{1,0:T(8,128)(2,1)} %copy-done.9), channel_id=1, source_target_pairs={{0,2},{1,3},{2,0},{3,1},{4,6},{5,7},{6,4},{7,5},{8,10},{9,11},{10,... | collective-permute-start | bytes 835592 | tf_op jit(solution)/shard_map/ppermute | solution.py:1428
  93.9 15.3 %collective-permute-start.15 = (bf16[4,9,32,256]{3,2,1,0:T(8,128)(2,1)S(1)}, bf16[4,9,32,256]{3,2,1,0:T(8,128)(2,1)S(1)}, u32[]{:S(2)}, u32[]{:S(2)}) collective-permute-start(bf16[4,9,32,256]{3,2,1,0:T(8,128)(2,1)S(1)} %bitcast.138), channel_id=1, source_target_pairs={{0,16},{8,24},{16,0},{24,8},{1,17},{9,25},{17,1},{25,9},{2,18},{10... | collective-permute-start | bytes 1769480 | tf_op jit(solution)/shard_map/ppermute | solution.py:1428
  95.0 31.9 %collective-permute-start.17 = (bf16[1152,512]{1,0:T(8,128)(2,1)}, bf16[1152,512]{1,0:T(8,128)(2,1)}, u32[]{:S(2)}, u32[]{:S(2)}) collective-permute-start(bf16[1152,512]{1,0:T(8,128)(2,1)} %get-tuple-element.198.extended_ref.refs_0_), channel_id=1, source_target_pairs={{0,8},{8,0},{16,24},{24,16},{1,9},{9,1},{17,25},{25,17},{2,10},{10... | collective-permute-start | bytes 3538952 | tf_op jit(solution)/shard_map/ppermute | solution.py:1428
  109.5 17.5 %collective-permute-start.18 = (bf16[2,4,9,32,256]{4,3,2,1,0:T(8,128)(2,1)S(1)}, bf16[2,4,9,32,256]{4,3,2,1,0:T(8,128)(2,1)}, u32[]{:S(2)}, u32[]{:S(2)}) collective-permute-start(bf16[2,4,9,32,256]{4,3,2,1,0:T(8,128)(2,1)S(1)} %get-tuple-element.223.refs_0_), channel_id=1, source_target_pairs={{0,8},{8,0},{16,24},{24,16},{1,9},{9,1},{17,25},{25,17},{2,10},{10... | collective-permute-start | bytes 3538952 | tf_op jit(solution)/shard_map/ppermute | solution.py:1428
  110.0 31.2 %collective-permute-start.22 = (bf16[2,4,4,64,256]{4,3,2,1,0:T(8,128)(2,1)S(1)}, bf16[2,4,4,64,256]{4,3,2,1,0:T(8,128)(2,1)S(1)}, u32[]{:S(2)}, u32[]{:S(2)}) collective-permute-start(bf16[2,4,4,64,256]{4,3,2,1,0:T(8,128)(2,1)S(1)} %get-tuple-element.224.refs_0_), channel_id=1, source_target_pairs={{0,16},{8,24},{16,0},{24,8},{1,17},{9,25},{17,1},{25,9},{2,18},{10... | collective-permute-start | bytes 3145736 | tf_op jit(solution)/shard_map/ppermute | solution.py:1428
  110.6 16.4 %collective-permute-start.19 = (bf16[2,4,4,64,256]{4,3,2,1,0:T(8,128)(2,1)S(1)}, bf16[2,4,4,64,256]{4,3,2,1,0:T(8,128)(2,1)S(1)}, u32[]{:S(2)}, u32[]{:S(2)}) collective-permute-start(bf16[2,4,4,64,256]{4,3,2,1,0:T(8,128)(2,1)S(1)} %get-tuple-element.224.refs_0_), channel_id=1, source_target_pairs={{0,8},{8,0},{16,24},{24,16},{1,9},{9,1},{17,25},{25,17},{2,10},{10... | collective-permute-start | bytes 3145736 | tf_op jit(solution)/shard_map/ppermute | solution.py:1428
  110.6 30.7 %collective-permute-start.21 = (bf16[2,4,9,32,256]{4,3,2,1,0:T(8,128)(2,1)S(1)}, bf16[2,4,9,32,256]{4,3,2,1,0:T(8,128)(2,1)S(1)}, u32[]{:S(2)}, u32[]{:S(2)}) collective-permute-start(bf16[2,4,9,32,256]{4,3,2,1,0:T(8,128)(2,1)S(1)} %get-tuple-element.223.refs_0_), channel_id=1, source_target_pairs={{0,4},{4,0},{1,5},{5,1},{2,6},{6,2},{3,7},{7,3},{8,12},{12,8},{9,1... | collective-permute-start | bytes 3538952 | tf_op jit(solution)/shard_map/ppermute | solution.py:1428
  140.9 16.3 %collective-permute-start.25 = (bf16[1024,1536]{1,0:T(8,128)(2,1)}, bf16[1024,1536]{1,0:T(8,128)(2,1)}, u32[]{:S(2)}, u32[]{:S(2)}) collective-permute-start(bf16[1024,1536]{1,0:T(8,128)(2,1)} %get-tuple-element.237), channel_id=1, source_target_pairs={{0,8},{8,0},{16,24},{24,16},{1,9},{9,1},{17,25},{25,17},{2,10},{10... | collective-permute-start | bytes 9437192 | tf_op jit(solution)/shard_map/ppermute | solution.py:1428
  181.1 26.2 %collective-permute-start.27 = (bf16[1024,1536]{1,0:T(8,128)(2,1)S(1)}, bf16[1024,1536]{1,0:T(8,128)(2,1)S(1)}, u32[]{:S(2)}, u32[]{:S(2)}) collective-permute-start(bf16[1024,1536]{1,0:T(8,128)(2,1)S(1)} %get-tuple-element.259), channel_id=1, source_target_pairs={{0,8},{8,0},{16,24},{24,16},{1,9},{9,1},{17,25},{25,17},{2,10},{10... | collective-permute-start | bytes 9437192 | tf_op jit(solution)/shard_map/ppermute | solution.py:1428
  224.2 35.2 %collective-permute-start.33 = (bf16[512,512]{1,0:T(8,128)(2,1)S(1)}, bf16[512,512]{1,0:T(8,128)(2,1)S(1)}, u32[]{:S(2)}, u32[]{:S(2)}) collective-permute-start(bf16[512,512]{1,0:T(8,128)(2,1)S(1)} %bitcast.145), channel_id=1, source_target_pairs={{0,4},{4,0},{1,5},{5,1},{2,6},{6,2},{3,7},{7,3},{8,12},{12,8},{9,1... | collective-permute-start | bytes 1572872 | tf_op jit(solution)/shard_map/ppermute | solution.py:1428
  224.7 34.4 %collective-permute-start.34 = (bf16[512,512]{1,0:T(8,128)(2,1)S(1)}, bf16[512,512]{1,0:T(8,128)(2,1)S(1)}, u32[]{:S(2)}, u32[]{:S(2)}) collective-permute-start(bf16[512,512]{1,0:T(8,128)(2,1)S(1)} %bitcast.147), channel_id=1, source_target_pairs={{0,16},{8,24},{16,0},{24,8},{1,17},{9,25},{17,1},{25,9},{2,18},{10... | collective-permute-start | bytes 1572872 | tf_op jit(solution)/shard_map/ppermute | solution.py:1428
  239.4 21.8 %collective-permute-start.31 = (bf16[1152,256]{1,0:T(8,128)(2,1)S(1)}, bf16[1152,256]{1,0:T(8,128)(2,1)S(1)}, u32[]{:S(2)}, u32[]{:S(2)}) collective-permute-start(bf16[1152,256]{1,0:T(8,128)(2,1)S(1)} %bitcast.129), channel_id=1, source_target_pairs={{0,16},{8,24},{16,0},{24,8},{1,17},{9,25},{17,1},{25,9},{2,18},{10... | collective-permute-start | bytes 1769480 | tf_op jit(solution)/shard_map/ppermute | solution.py:1428
  240.9 19.9 %collective-permute-start.32 = (bf16[1152,256]{1,0:T(8,128)(2,1)S(1)}, bf16[1152,256]{1,0:T(8,128)(2,1)S(1)}, u32[]{:S(2)}, u32[]{:S(2)}) collective-permute-start(bf16[1152,256]{1,0:T(8,128)(2,1)S(1)} %bitcast.131), channel_id=1, source_target_pairs={{0,4},{4,0},{1,5},{5,1},{2,6},{6,2},{3,7},{7,3},{8,12},{12,8},{9,1... | collective-permute-start | bytes 1769480 | tf_op jit(solution)/shard_map/ppermute | solution.py:1428
  282.5 16.4 %collective-permute-start.39 = (bf16[64,512]{1,0:T(8,128)(2,1)S(1)}, bf16[64,512]{1,0:T(8,128)(2,1)S(1)}, u32[]{:S(2)}, u32[]{:S(2)}) collective-permute-start(bf16[64,512]{1,0:T(8,128)(2,1)S(1)} %get-tuple-element.307), channel_id=1, source_target_pairs={{0,4},{4,0},{1,5},{5,1},{2,6},{6,2},{3,7},{7,3},{8,12},{12,8},{9,1... | collective-permute-start | bytes 196616 | tf_op jit(solution)/shard_map/ppermute | solution.py:1428
  283.1 26.7 %collective-permute-start.44 = (bf16[544,256]{1,0:T(8,128)(2,1)}, bf16[544,256]{1,0:T(8,128)(2,1)S(1)}, u32[]{:S(2)}, u32[]{:S(2)}) collective-permute-start(bf16[544,256]{1,0:T(8,128)(2,1)} %copy-done.21), channel_id=1, source_target_pairs={{0,3},{1,0},{2,1},{3,2},{4,7},{5,4},{6,5},{7,6},{8,11},{9,8},{10,9... | collective-permute-start | bytes 835592 | tf_op jit(solution)/shard_map/ppermute | solution.py:1428
  283.1 28.3 %collective-permute-start.45 = (bf16[544,256]{1,0:T(8,128)(2,1)}, bf16[544,256]{1,0:T(8,128)(2,1)S(1)}, u32[]{:S(2)}, u32[]{:S(2)}) collective-permute-start(bf16[544,256]{1,0:T(8,128)(2,1)} %copy-done.20), channel_id=1, source_target_pairs={{0,2},{1,3},{2,0},{3,1},{4,6},{5,7},{6,4},{7,5},{8,10},{9,11},{10,... | collective-permute-start | bytes 835592 | tf_op jit(solution)/shard_map/ppermute | solution.py:1428
  285.2 27.7 %collective-permute-start.46 = (bf16[544,256]{1,0:T(8,128)(2,1)}, bf16[544,256]{1,0:T(8,128)(2,1)S(1)}, u32[]{:S(2)}, u32[]{:S(2)}) collective-permute-start(bf16[544,256]{1,0:T(8,128)(2,1)} %copy-done.19), channel_id=1, source_target_pairs={{0,1},{1,2},{2,3},{3,0},{4,5},{5,6},{6,7},{7,4},{8,9},{9,10},{10,1... | collective-permute-start | bytes 835592 | tf_op jit(solution)/shard_map/ppermute | solution.py:1428
  298.3 17.0 %collective-permute-start.42 = (bf16[1152,256]{1,0:T(8,128)(2,1)S(1)}, bf16[1152,256]{1,0:T(8,128)(2,1)S(1)}, u32[]{:S(2)}, u32[]{:S(2)}) collective-permute-start(bf16[1152,256]{1,0:T(8,128)(2,1)S(1)} %bitcast.134), channel_id=1, source_target_pairs={{0,16},{8,24},{16,0},{24,8},{1,17},{9,25},{17,1},{25,9},{2,18},{10... | collective-permute-start | bytes 1769480 | tf_op jit(solution)/shard_map/ppermute | solution.py:1428
  298.9 16.0 %collective-permute-start.43 = (bf16[1152,256]{1,0:T(8,128)(2,1)S(1)}, bf16[1152,256]{1,0:T(8,128)(2,1)S(1)}, u32[]{:S(2)}, u32[]{:S(2)}) collective-permute-start(bf16[1152,256]{1,0:T(8,128)(2,1)S(1)} %bitcast.137), channel_id=1, source_target_pairs={{0,4},{4,0},{1,5},{5,1},{2,6},{6,2},{3,7},{7,3},{8,12},{12,8},{9,1... | collective-permute-start | bytes 1769480 | tf_op jit(solution)/shard_map/ppermute | solution.py:1428
  309.8 24.7 %collective-permute-start.52 = (bf16[512,512]{1,0:T(8,128)(2,1)S(1)}, bf16[512,512]{1,0:T(8,128)(2,1)S(1)}, u32[]{:S(2)}, u32[]{:S(2)}) collective-permute-start(bf16[512,512]{1,0:T(8,128)(2,1)S(1)} %bitcast.141), channel_id=1, source_target_pairs={{0,4},{4,0},{1,5},{5,1},{2,6},{6,2},{3,7},{7,3},{8,12},{12,8},{9,1... | collective-permute-start | bytes 1572872 | tf_op jit(solution)/shard_map/ppermute | solution.py:1428
  311.4 22.8 %collective-permute-start.53 = (bf16[512,512]{1,0:T(8,128)(2,1)S(1)}, bf16[512,512]{1,0:T(8,128)(2,1)S(1)}, u32[]{:S(2)}, u32[]{:S(2)}) collective-permute-start(bf16[512,512]{1,0:T(8,128)(2,1)S(1)} %bitcast.143), channel_id=1, source_target_pairs={{0,16},{8,24},{16,0},{24,8},{1,17},{9,25},{17,1},{25,9},{2,18},{10... | collective-permute-start | bytes 1572872 | tf_op jit(solution)/shard_map/ppermute | solution.py:1428
  333.5 15.0 %collective-permute-start.51 = (bf16[352,256]{1,0:T(8,128)(2,1)S(1)}, bf16[352,256]{1,0:T(8,128)(2,1)}, u32[]{:S(2)}, u32[]{:S(2)}) collective-permute-start(bf16[352,256]{1,0:T(8,128)(2,1)S(1)} %get-tuple-element.349), channel_id=1, source_target_pairs={{0,1},{1,2},{2,3},{3,0},{4,5},{5,6},{6,7},{7,4},{8,9},{9,10},{10,1... | collective-permute-start | bytes 540680 | tf_op jit(solution)/shard_map/ppermute | solution.py:1428
  335.9 15.8 %collective-permute-start.58 = (bf16[256,512]{1,0:T(8,128)(2,1)S(1)}, bf16[256,512]{1,0:T(8,128)(2,1)S(1)}, u32[]{:S(2)}, u32[]{:S(2)}) collective-permute-start(bf16[256,512]{1,0:T(8,128)(2,1)S(1)} %get-tuple-element.362), channel_id=1, source_target_pairs={{0,16},{8,24},{16,0},{24,8},{1,17},{9,25},{17,1},{25,9},{2,18},{10... | collective-permute-start | bytes 786440 | tf_op jit(solution)/shard_map/ppermute | solution.py:1428
  (79 other events, 495.7 us)
where the time goes:
time: 383 us; the launch traced here: 379 us
  Pallas kernels  187 us (49%)
  waiting for transfers between devices  95.1 us (25%)
  starting transfers between devices  55.3 us (14%)
  local copies, waits for them, and re-layouts  38.2 us (10%)
    ppermute x60, waiting for transfers between devices, shifted(): lax.ppermute(value, self.axis, self.pairs(lambda i: (i + by) % self.size))  93.5 us
    ppermute x60, starting transfers between devices, shifted(): lax.ppermute(value, self.axis, self.pairs(lambda i: (i + by) % self.size))  51.8 us
    pallas_call x2, Pallas kernels, ffn_back_hidden(): pl.pallas_call(kernel, grid=(units // block,), in_specs=[whole, whole, pl...  27.4 us
    pallas_call x2, Pallas kernels, ffn_forward(): pl.pallas_call(kernel, grid=(steps,), in_specs=[SCALARS, whole, whole, ro...  26 us
    pallas_call x2, Pallas kernels, conv_forward(): pl.pallas_call(kernel, grid=(steps,), in_specs=[pl.BlockSpec(extended.sha...  23.3 us
    pallas_call x2, Pallas kernels, conv_weight_grad(): pl.pallas_call(kernel, grid_spec=pltpu.PrefetchScalarGridSpec(num_scalar_...  19.4 us
    unnamed x101, local copies, waits for them, and re-layouts  17.3 us
    pallas_call x2, Pallas kernels, ffn_weight_grad(): pl.pallas_call(kernel, grid=(acrosses * seqs,), in_specs=([left_spec, rig...  16.5 us
  transfers between devices with their start and end apart: 63, of which 20 were waited for; matrix products, arithmetic and copies ran while one was open for 5% of the time, Pallas kernels for 43%

commit v1 on v0

--- a/solution.py
+++ b/solution.py
@@ -189,7 +189,7 @@
             for packet_ref in packet_refs:
                 packet_ref[:, :width] = lowered_ref[...]
 
-        for at, size in row_chunks(rows, 512):
+        for at, size in row_chunks(rows, 256):
             some = pl.ds(at, size)
             term = None
             for c in range(cores):
@@ -652,7 +652,7 @@
     return found[0], (found[1],)
 
 
-def restack(groups, reads=(), after=()):
+def restack(groups, reads=(), after=(), fixed=False):
     cuts = [cut for _, each in groups for cut in each]
     if any(last is not None and (first % ROW_TILE or last % ROW_TILE) for first, last, _ in cuts):
         return [
@@ -697,7 +697,7 @@
         compiler_params=pltpu.CompilerParams(vmem_limit_bytes=10 * MIB),
         cost_estimate=cost(1.5),
         name="restack",
-    )(*flat, *reads, *after)
+    )(*([in_hbm(each) for each in flat] if fixed else flat), *reads, *after)
     return [
         each.reshape((each.shape[0],) + shape) for each, (_, _, shape) in zip(found, cuts)
     ], (found[-1],)
@@ -1645,13 +1645,19 @@
     codes = to_rows(targets + masked * head_weight.shape[1])
     codes = jnp.broadcast_to(codes[:, None], (rows, 128))
 
+    reaches = [taps // 2 * step for step in steps]
+    rim_reaches = [reach if seq.size == 2 and reach <= rows else 0 for reach in reaches]
+
     tap_parts = tap.gather(bundle(0))
     behind = bundle(1)
-    (conv_part, ffn_part), last = restack([(tap_parts, cuts)], reads=[conv_input, behind])
+    found = rims(conv_input, reaches[0], seq)
+    (conv_part, ffn_part), last = restack(
+        [(tap_parts, cuts)], reads=[behind] + [found if rim_reaches[0] else conv_input]
+    )
+    (behind,), last = hold([behind], last)
     split = (tap.size + 1) // 2
-    (behind,), last = hold([behind], last)
     late_parts = tap.gather(behind)
-    extended, last = extend(conv_input, rims(conv_input, taps // 2 * steps[0], seq), seq, last)
+    extended, last = extend(conv_input, found, seq, last)
     extended_parts = [extended] + [core.shifted(extended, -c) for c in range(1, core.size)]
     conv_parts, ffn_parts = across.gather(conv_part), seq.gather(ffn_part)
     (conv_part, ffn_part), last = restack(
@@ -1669,7 +1675,7 @@
     )
     conv_slots += [core.gather(each) for each in held[: seq.size - 1]]
     ffn_slots += [core.gather(each) for each in held[seq.size - 1 :]]
-    (late_conv, late_ffn), last = restack([(late_parts, cuts)], after=last)
+    (late_conv, late_ffn), last = restack([(late_parts, cuts)], after=last, fixed=True)
     late_conv_parts, late_ffn_parts = across.gather(late_conv), seq.gather(late_ffn)
 
     def turned(slots):
@@ -1679,14 +1685,6 @@
     conv_full[0], last = place_conv(
         turned(conv_slots), places, sizes, last, [part for each in ffn_slots for part in each[1:]]
     )
-    (late_conv, late_ffn), last = restack(
-        [straight(late_conv_parts), straight(late_ffn_parts)], after=last
-    )
-    late_conv_parts, late_ffn_parts = seq.gather(late_conv), across.gather(late_ffn)
-    late_conv_slots = [core.gather(late_conv)]
-    late_ffn_slots = [core.gather(late_ffn)]
-    reaches = [taps // 2 * step for step in steps]
-    rim_reaches = [reach if seq.size == 2 and reach <= rows else 0 for reach in reaches]
     saved = []
     reads = []
     rim = None
@@ -1713,6 +1711,12 @@
         )
         reads = extended_parts[1:]
         if b == 0:
+            (late_conv, late_ffn), last = restack(
+                [straight(late_conv_parts), straight(late_ffn_parts)], after=last
+            )
+            late_conv_parts, late_ffn_parts = seq.gather(late_conv), across.gather(late_ffn)
+            late_conv_slots = [core.gather(late_conv)]
+            late_ffn_slots = [core.gather(late_ffn)]
             in_full[0], out_full[0], last = place_ffn(turned(ffn_slots), sizes, last)
             reads = reads + late_conv_slots[0][1:] + late_ffn_slots[0][1:]
         active, hidden_slopes, (normed_ffn, scale_ffn, stream, conv_input), packets, rim, last = (
@@ -1746,7 +1750,6 @@
             )
         )
 
-    final_state = from_rows(conv_input, windows)
     (stream_grad, head_grad, loss_rows), last = head_and_loss(stream, head_weight, codes, last)
 
     ffn_rows_of_sums = [None, None]
@@ -1859,6 +1862,8 @@
 
     row_groups = [(each, 3) for each in conv_rows_of_sums + ffn_rows_of_sums]
     row_groups.append((head_grad, head_weight.shape[1]))
+    (conv_input,), last = hold([conv_input], last)
+    final_state = from_rows(conv_input, windows)
     packed, last = pack_small(row_groups, in_bias_grads, loss_rows, places, sizes, ffn_rows, last)
 
     conv_rows = taps * slab

time: 383 us -> 377 us (0.984)
  local copies, waits for them, and re-layouts: 38.2 us -> 27.9 us
  Pallas kernels: 187 us -> 194 us
  waiting for transfers between devices: 95.1 us -> 90.1 us
    unnamed x101 -> x131, local copies, waits for them, and re-layouts: 17.3 us -> 10.4 us
    pallas_call x8, Pallas kernels: 2.43 us -> 7.59 us  [add_slots(): pl.pallas_call(kernel, grid=(rows // block,), in_specs=[pl.BlockSpec((slo...]
  transfers between devices with their start and end apart: 63 -> 63, of which waited for: 20 -> 24; matrix products, arithmetic and copies ran while one was open for 5% -> 3% of each run, Pallas kernels for 43% -> 46%
where the time goes in v1:
time: 377 us; the launch traced here: 372 us
  Pallas kernels  194 us (51%)
  waiting for transfers between devices  90.1 us (24%)
  starting transfers between devices  56.5 us (15%)
  local copies, waits for them, and re-layouts  27.9 us (7%)
    ppermute x60, waiting for transfers between devices, shifted(): lax.ppermute(value, self.axis, self.pairs(lambda i: (i + by) % self.size))  89.8 us
    ppermute x60, starting transfers between devices, shifted(): lax.ppermute(value, self.axis, self.pairs(lambda i: (i + by) % self.size))  53 us
    pallas_call x2, Pallas kernels, ffn_forward(): pl.pallas_call(kernel, grid=(steps,), in_specs=[SCALARS, whole, whole, ro...  28.5 us
    pallas_call x2, Pallas kernels, ffn_back_hidden(): pl.pallas_call(kernel, grid=(units // block,), in_specs=[whole, whole, pl...  26.9 us
    pallas_call x2, Pallas kernels, conv_forward(): pl.pallas_call(kernel, grid=(steps,), in_specs=[pl.BlockSpec(extended.sha...  23.7 us
    pallas_call x2, Pallas kernels, conv_weight_grad(): pl.pallas_call(kernel, grid_spec=pltpu.PrefetchScalarGridSpec(num_scalar_...  19.5 us
    pallas_call x2, Pallas kernels, ffn_weight_grad(): pl.pallas_call(kernel, grid=(acrosses * seqs,), in_specs=([left_spec, rig...  16.6 us
    pallas_call x2, Pallas kernels, conv_data_grad(): pl.pallas_call(kernel, grid=(steps,), in_specs=[pl.BlockSpec(extended.sha...  15.2 us
  transfers between devices with their start and end apart: 63, of which 24 were waited for; matrix products, arithmetic and copies ran while one was open for 3% of the time, Pallas kernels for 46%

profile of v1, /device:TPU:0, one launch (start us, length us, event | category | flops | bytes accessed | tf_op | source)
XLA Modules:
  0.0 372.3 jit_solution(10422638381599247087)
XLA Ops:
  7.9 5.1 %collective-permute-start.3 = (bf16[544,256]{1,0:T(8,128)(2,1)S(1)}, bf16[544,256]{1,0:T(8,128)(2,1)S(1)}, u32[]{:S(2)}, u32[]{:S(2)}) collective-permute-start(bf16[544,256]{1,0:T(8,128)(2,1)S(1)} %pad_maximum_fusion.1.refs_0_), channel_id=1, source_target_pairs={{0,3},{1,0},{2,1},{3,2},{4,7},{5,4},{6,5},{7,6},{8,11},{9,8},{10,9... | collective-permute-start | bytes 835592 | tf_op jit(solution)/shard_map/ppermute | solution.py:1428
  20.1 16.6 %collective-permute-done.2.refs_2_ = bf16[544,256]{1,0:T(8,128)(2,1)S(1)} collective-permute-done((bf16[544,256]{1,0:T(8,128)(2,1)S(1)}, bf16[544,256]{1,0:T(8,128)(2,1)S(1)}, u32[]{:S(2)}, u32[]{:S(2)}) %collective-permute-start.2) | collective-permute-done | bytes 278560 | tf_op jit(solution)/shard_map/ppermute | solution.py:1428
  44.4 4.0 %collective-permute-done.7.refs_5_.refs_6_.refs_3_ = bf16[544,256]{1,0:T(8,128)(2,1)S(1)} collective-permute-done((bf16[544,256]{1,0:T(8,128)(2,1)S(1)}, bf16[544,256]{1,0:T(8,128)(2,1)S(1)}, u32[]{:S(2)}, u32[]{:S(2)}) %collective-permute-start.7) | collective-permute-done | bytes 278560 | tf_op jit(solution)/shard_map/ppermute | solution.py:1428
  48.4 8.3 %collective-permute-done.6.refs_4_.refs_1_ = bf16[544,256]{1,0:T(8,128)(2,1)S(1)} collective-permute-done((bf16[544,256]{1,0:T(8,128)(2,1)S(1)}, bf16[544,256]{1,0:T(8,128)(2,1)S(1)}, u32[]{:S(2)}, u32[]{:S(2)}) %collective-permute-start.6) | collective-permute-done | bytes 278560 | tf_op jit(solution)/shard_map/ppermute | solution.py:1428
  59.2 13.0 %collective-permute-done.12.refs_5_.refs_2_ = bf16[544,256]{1,0:T(8,128)(2,1)S(1)} collective-permute-done((bf16[544,256]{1,0:T(8,128)(2,1)S(1)}, bf16[544,256]{1,0:T(8,128)(2,1)S(1)}, u32[]{:S(2)}, u32[]{:S(2)}) %collective-permute-start.12) | collective-permute-done | bytes 278560 | tf_op jit(solution)/shard_map/ppermute | solution.py:1428
  72.2 11.1 %collective-permute-done.9.refs_1_ = bf16[2,4,4,64,256]{4,3,2,1,0:T(8,128)(2,1)S(1)} collective-permute-done((bf16[2,4,4,64,256]{4,3,2,1,0:T(8,128)(2,1)S(1)}, bf16[2,4,4,64,256]{4,3,2,1,0:T(8,128)(2,1)S(1)}, u32[]{:S(2)}, u32[]{:S(2)}) %collective-permute-start.9) | collective-permute-done | bytes 1048608 | tf_op jit(solution)/shard_map/ppermute | solution.py:1428
  91.3 4.7 %place_conv.2 = (bf16[9,512,512]{2,1,0:T(8,128)(2,1)}, f32[8,128]{1,0:T(8,128)S(1)}) custom-call(s32[4]{0:T(128)S(1)} %pad_add_fusion.place_ref, bf16[2,4,9,32,256]{4,3,2,1,0:T(8,128)(2,1)S(1)} %copy-done.15, bf16[2,4,9,32,256]{4,3,2,1,0:T(8,128)(2,1)S(1)} %get-tuple-element.208.refs_1_, bf16[2,4,9,32,256]{4,3,2,1,0:T(8,128)(2,1)S(1)} %collective-permute-done.10.refs_2_, ...), custom_call_target="tpu_custom_call" | custom-call | flops 3300000000 | bytes 10500000 | tf_op jit(solution)/shard_map/place_conv/pallas_call | solution.py:1361
  96.0 11.1 %conv_forward.2 = (bf16[1024,512]{1,0:T(8,128)(2,1)}, bf16[1024,512]{1,0:T(8,128)(2,1)}, f32[1024,512]{1,0:T(8,128)}, bf16[1024,512]{1,0:T(8,128)(2,1)S(1)}, f32[8,128]{1,0:T(8,128)S(1)}) custom-call(bf16[1152,512]{1,0:T(8,128)(2,1)S(1)} %copy-done.12, bf16[9,512,512]{2,1,0:T(8,128)(2,1)} %get-tuple-element.212.weight_ref, ...), custom_call_target="tpu_custom_call" | custom-call | flops 9900000256 | bytes 31500000 | tf_op jit(solution)/shard_map/conv_forward/pallas_call | solution.py:124
  112.7 3.7 place_ffn.2
  116.4 15.2 %ffn_forward.2 = (bf16[1024,1024]{1,0:T(8,128)(2,1)}, bf16[1024,1024]{1,0:T(8,128)(2,1)}, bf16[1024,1024]{1,0:T(8,128)(2,1)}, bf16[1024,512]{1,0:T(8,128)(2,1)},...) custom-call(s32[1]{0:T(128)} %bitcast.place_ref, ...), custom_call_target="tpu_custom_call" | custom-call | flops 12099999744 | bytes 38500000 | tf_op jit(solution)/shard_map/ffn_forward/pallas_call | solution.py:232
  140.7 4.6 %place_conv.3 = (bf16[9,512,512]{2,1,0:T(8,128)(2,1)}, f32[8,128]{1,0:T(8,128)S(1)}) custom-call(s32[4]{0:T(128)S(1)} %pad_add_fusion.place_ref, bf16[2,4,9,32,256]{4,3,2,1,0:T(8,128)(2,1)S(1)} %get-tuple-element.225.refs_0_, bf16[2,4,9,32,256]{4,3,2,1,0:T(8,128)(2,1)S(1)} %get-tuple-element.231.refs_1_, ...), custom_call_target="tpu_custom_call" | custom-call | flops 3300000000 | bytes 10500000 | tf_op jit(solution)/shard_map/place_conv/pallas_call | solution.py:1361
  145.3 3.6 place_ffn.3
  149.0 3.2 collective-permute-done.20.found_ref
  154.5 12.6 %conv_forward.3 = (bf16[1024,512]{1,0:T(8,128)(2,1)}, bf16[1024,512]{1,0:T(8,128)(2,1)}, f32[1024,512]{1,0:T(8,128)}, bf16[1024,512]{1,0:T(8,128)(2,1)S(1)}, f32[8,128]{1,0:T(8,128)S(1)}) custom-call(bf16[2048,512]{1,0:T(8,128)(2,1)} %get-tuple-element.235.extended_ref.refs_0_, bf16[9,512,512]{2,1,0:T(8,128)(2,1)} %get-tuple-element.236.weight_ref, ...), custom_call_target="tpu_custom_call" | custom-call | flops 9900000256 | bytes 31500000 | tf_op jit(solution)/shard_map/conv_forward/pallas_call | solution.py:124
  167.1 13.3 %ffn_forward.3 = (bf16[1024,1024]{1,0:T(8,128)(2,1)}, bf16[1024,1024]{1,0:T(8,128)(2,1)}, bf16[1024,1024]{1,0:T(8,128)(2,1)}, bf16[1024,512]{1,0:T(8,128)(2,1)},...) custom-call(s32[1]{0:T(128)} %bitcast.place_ref, ...), custom_call_target="tpu_custom_call" | custom-call | flops 12099999744 | bytes 38500000 | tf_op jit(solution)/shard_map/ffn_forward/pallas_call | solution.py:232
  181.1 6.0 %head_and_loss.1 = (f32[1024,512]{1,0:T(8,128)S(1)}, f32[8,512]{1,0:T(8,128)S(1)}, f32[8,128]{1,0:T(8,128)S(1)}, f32[8,128]{1,0:T(8,128)S(1)}) custom-call(f32[1024,512]{1,0:T(8,128)S(1)} %get-tuple-element.248.stream_ref, f32[512,128]{1,0:T(8,128)S(1)} %pad.4.head_ref, s32[1024,128]{1,0:T(8,128)S(1)} %broadcast_in_dim.8.code_ref, ...), custom_call_target="tpu_custom_call" | custom-call | flops 6600000000 | bytes 21000000 | tf_op jit(solution)/shard_map/head_and_loss/pallas_call | solution.py:331
  187.2 18.8 %ffn_back_hidden.2 = (bf16[1024,512]{1,0:T(8,128)(2,1)S(1)}, bf16[1024,1024]{1,0:T(8,128)(2,1)}, f32[1,1024]{1,0:T(1,128)S(1)}, f32[1,1024]{1,0:T(1,128)S(1)}, b...) custom-call(f32[1024,512]{1,0:T(8,128)S(1)} %get-tuple-element.250.upstream_ref, ...), custom_call_target="tpu_custom_call" | custom-call | flops 6600000000 | bytes 21000000 | tf_op jit(solution)/shard_map/ffn_back_hidden/pallas_call | solution.py:397
  206.2 7.5 %ffn_back_stream.2 = (f32[1024,512]{1,0:T(8,128)S(1)}, bf16[1024,512]{1,0:T(8,128)(2,1)S(1)}, bf16[1024,256]{1,0:T(8,128)(2,1)S(1)}, bf16[512,512]{1,0:T(8,128)(...) custom-call(s32[2]{0:T(128)S(1)} %pad_add_fusion.1.core_ref, f32[1024,512]{1,0:T(8,128)S(1)} %get-tuple-element.250.upstream_ref, ...), custom_call_target="tpu_custom_call" | custom-call | flops 5500000256 | bytes 17500000 | tf_op jit(solution)/shard_map/ffn_back_stream/pallas_call | solution.py:505
  215.4 7.6 %ffn_weight_grad.2 = (bf16[2,2,2,64,512]{4,3,2,1,0:T(8,128)(2,1)S(1)}, bf16[2,2,2,64,512]{4,3,2,1,0:T(8,128)(2,1)S(1)}, bf16[2,2,2,64,512]{4,3,2,1,0:T(8,128)(2,...) custom-call(bf16[1024,1024]{1,0:T(8,128)(2,1)} %get-tuple-element.258.refs_0_, ...), custom_call_target="tpu_custom_call" | custom-call | flops 8800000000 | bytes 28000000 | tf_op jit(solution)/shard_map/ffn_weight_grad/pallas_call | solution.py:873
  225.2 3.3 collective-permute-done.28.found_ref
  228.7 10.2 %conv_weight_grad.2 = (bf16[2,2,9,32,256]{4,3,2,1,0:T(8,128)(2,1)S(1)}, bf16[2,2,9,32,256]{4,3,2,1,0:T(8,128)(2,1)S(1)}, bf16[2,2,9,32,256]{4,3,2,1,0:T(8,128)(2...) custom-call(s32[4]{0:T(128)S(1)} %pad_add_fusion.place_ref, ...), custom_call_target="tpu_custom_call" | custom-call | flops 9900000256 | bytes 31500000 | tf_op jit(solution)/shard_map/conv_weight_grad/pallas_call | solution.py:765
  241.0 7.6 %conv_data_grad.2 = (f32[1024,512]{1,0:T(8,128)S(1)}, f32[8,128]{1,0:T(8,128)S(1)}) custom-call(bf16[2048,512]{1,0:T(8,128)(2,1)S(1)} %get-tuple-element.268.extended_ref, bf16[9,512,512]{2,1,0:T(8,128)(2,1)} %get-tuple-element.236.weight_ref, f32[1024,512]{1,0:T(8,128)S(1)} %get-tuple-element.269.upstream_ref, f32[8,128]{1,0:T(8,128)S(1)} %get-tuple-element.272.refs_0_), custom_call_target="tpu_custom_call" | custom-call | flops 6600000000 | bytes 21000000 | tf_op jit(solution)/shard_map/conv_data_grad/pallas_call | solution.py:593
  248.6 8.1 %ffn_back_hidden.3 = (bf16[1024,512]{1,0:T(8,128)(2,1)S(1)}, bf16[1024,1024]{1,0:T(8,128)(2,1)}, f32[1,1024]{1,0:T(1,128)S(1)}, f32[1,1024]{1,0:T(1,128)S(1)}, b...) custom-call(f32[1024,512]{1,0:T(8,128)S(1)} %get-tuple-element.273.upstream_ref, ...), custom_call_target="tpu_custom_call" | custom-call | flops 6600000000 | bytes 21000000 | tf_op jit(solution)/shard_map/ffn_back_hidden/pallas_call | solution.py:397
  263.0 7.7 %ffn_back_stream.3 = (f32[1024,512]{1,0:T(8,128)S(1)}, bf16[1024,512]{1,0:T(8,128)(2,1)S(1)}, bf16[1024,256]{1,0:T(8,128)(2,1)S(1)}, bf16[1024,1536]{1,0:T(8,128...) custom-call(s32[2]{0:T(128)S(1)} %pad_add_fusion.1.core_ref, ...), custom_call_target="tpu_custom_call" | custom-call | flops 5500000256 | bytes 17500000 | tf_op jit(solution)/shard_map/ffn_back_stream/pallas_call | solution.py:505
  274.1 5.3 %collective-permute-done.40.refs_3_ = bf16[1024,256]{1,0:T(8,128)(2,1)S(1)} collective-permute-done((bf16[1024,256]{1,0:T(8,128)(2,1)S(1)}, bf16[1024,256]{1,0:T(8,128)(2,1)S(1)}, u32[]{:S(2)}, u32[]{:S(2)}) %collective-permute-start.40) | collective-permute-done | bytes 524320 | tf_op jit(solution)/shard_map/ppermute | solution.py:1428
  279.4 9.2 %conv_weight_grad.3 = (bf16[2,2,9,32,256]{4,3,2,1,0:T(8,128)(2,1)S(1)}, bf16[2,2,9,32,256]{4,3,2,1,0:T(8,128)(2,1)S(1)}, bf16[2,2,9,32,256]{4,3,2,1,0:T(8,128)(2...) custom-call(s32[4]{0:T(128)S(1)} %pad_add_fusion.place_ref, bf16[1152,512]{1,0:T(8,128)(2,1)S(1)} %copy-done.13, ...), custom_call_target="tpu_custom_call" | custom-call | flops 9900000256 | bytes 31500000 | tf_op jit(solution)/shard_map/conv_weight_grad/pallas_call | solution.py:765
  292.1 9.0 %ffn_weight_grad.3 = (bf16[2,2,2,64,512]{4,3,2,1,0:T(8,128)(2,1)S(1)}, bf16[2,2,2,64,512]{4,3,2,1,0:T(8,128)(2,1)}, bf16[2,2,2,64,512]{4,3,2,1,0:T(8,128)(2,1)S(...) custom-call(bf16[1024,1024]{1,0:T(8,128)(2,1)} %get-tuple-element.281.refs_0_, bf16[1024,512]{1,0:T(8,128)(2,1)S(1)} %copy-done.44, ...), custom_call_target="tpu_custom_call" | custom-call | flops 8800000000 | bytes 28000000 | tf_op jit(solution)/shard_map/ffn_weight_grad/pallas_call | solution.py:873
  310.1 7.6 %conv_data_grad.3 = (bf16[1024,512]{1,0:T(8,128)(2,1)S(1)}, f32[8,128]{1,0:T(8,128)S(1)}) custom-call(bf16[1152,512]{1,0:T(8,128)(2,1)S(1)} %get-tuple-element.315.extended_ref, bf16[9,512,512]{2,1,0:T(8,128)(2,1)} %get-tuple-element.212.weight_ref, f32[1024,512]{1,0:T(8,128)S(1)} %get-tuple-element.316.upstream_ref, f32[8,128]{1,0:T(8,128)S(1)} %get-tuple-element.329.refs_0_), custom_call_target="tpu_custom_call" | custom-call | flops 6600000000 | bytes 21000000 | tf_op jit(solution)/shard_map/conv_data_grad/pallas_call | solution.py:593
  326.8 3.6 collective-permute-start.49
  331.0 3.2 add_slots.14
  345.6 3.3 collective-permute-start.59
  367.1 5.0 %place_conv_grads.1 = f32[2,9,128,512]{3,2,1,0:T(8,128)} custom-call(s32[3]{0:T(128)S(1)} %pad_add_fusion.2.place_ref, bf16[4,20,32,256]{3,2,1,0:T(8,128)(2,1)S(1)} %bitcast.125, bf16[4,20,32,256]{3,2,1,0:T(8,128)(2,1)S(1)} %bitcast.126, bf16[4,20,32,256]{3,2,1,0:T(8,128)(2,1)S(1)} %bitcast.127, bf16[4,20,32,256]{3,2,1,0:T(8,128)(2,1)S(1)} %bitcast.128), custom_call_target="tpu_custom_call" | custom-call | flops 5500000256 | bytes 17500000 | tf_op jit(solution)/shard_map/place_conv_grads/pallas_call | solution.py:1297
  (324 shorter events, 117.0 us)
Async XLA Ops:
  13.0 23.7 %collective-permute-start.2 = (bf16[544,256]{1,0:T(8,128)(2,1)S(1)}, bf16[544,256]{1,0:T(8,128)(2,1)S(1)}, u32[]{:S(2)}, u32[]{:S(2)}) collective-permute-start(bf16[544,256]{1,0:T(8,128)(2,1)S(1)} %pad_maximum_fusion.1.refs_0_), channel_id=1, source_target_pairs={{0,2},{1,3},{2,0},{3,1},{4,6},{5,7},{6,4},{7,5},{8,10},{9,11},{10,... | collective-permute-start | bytes 835592 | tf_op jit(solution)/shard_map/ppermute | solution.py:1428
  13.0 23.7 %collective-permute-start.1 = (bf16[544,256]{1,0:T(8,128)(2,1)S(1)}, bf16[544,256]{1,0:T(8,128)(2,1)S(1)}, u32[]{:S(2)}, u32[]{:S(2)}) collective-permute-start(bf16[544,256]{1,0:T(8,128)(2,1)S(1)} %pad_maximum_fusion.1.refs_0_), channel_id=1, source_target_pairs={{0,1},{1,2},{2,3},{3,0},{4,5},{5,6},{6,7},{7,4},{8,9},{9,10},{10,1... | collective-permute-start | bytes 835592 | tf_op jit(solution)/shard_map/ppermute | solution.py:1428
  38.2 18.5 %collective-permute-start.4 = (bf16[4,9,32,256]{3,2,1,0:T(8,128)(2,1)S(1)}, bf16[4,9,32,256]{3,2,1,0:T(8,128)(2,1)S(1)}, u32[]{:S(2)}, u32[]{:S(2)}) collective-permute-start(bf16[4,9,32,256]{3,2,1,0:T(8,128)(2,1)S(1)} %bitcast.138), channel_id=1, source_target_pairs={{0,16},{8,24},{16,0},{24,8},{1,17},{9,25},{17,1},{25,9},{2,18},{10... | collective-permute-start | bytes 1769480 | tf_op jit(solution)/shard_map/ppermute | solution.py:1428
  39.8 17.0 %collective-permute-start.5 = (bf16[4,4,64,256]{3,2,1,0:T(8,128)(2,1)S(1)}, bf16[4,4,64,256]{3,2,1,0:T(8,128)(2,1)S(1)}, u32[]{:S(2)}, u32[]{:S(2)}) collective-permute-start(bf16[4,4,64,256]{3,2,1,0:T(8,128)(2,1)S(1)} %bitcast.149), channel_id=1, source_target_pairs={{0,4},{4,0},{1,5},{5,1},{2,6},{6,2},{3,7},{7,3},{8,12},{12,8},{9,1... | collective-permute-start | bytes 1572872 | tf_op jit(solution)/shard_map/ppermute | solution.py:1428
  41.3 15.4 %collective-permute-start.6 = (bf16[544,256]{1,0:T(8,128)(2,1)S(1)}, bf16[544,256]{1,0:T(8,128)(2,1)S(1)}, u32[]{:S(2)}, u32[]{:S(2)}) collective-permute-start(bf16[544,256]{1,0:T(8,128)(2,1)S(1)} %get-tuple-element.203.refs_0_), channel_id=1, source_target_pairs={{0,1},{1,2},{2,3},{3,0},{4,5},{5,6},{6,7},{7,4},{8,9},{9,10},{10,1... | collective-permute-start | bytes 835592 | tf_op jit(solution)/shard_map/ppermute | solution.py:1428
  57.1 26.2 %collective-permute-start.10 = (bf16[2,4,9,32,256]{4,3,2,1,0:T(8,128)(2,1)S(1)}, bf16[2,4,9,32,256]{4,3,2,1,0:T(8,128)(2,1)S(1)}, u32[]{:S(2)}, u32[]{:S(2)}) collective-permute-start(bf16[2,4,9,32,256]{4,3,2,1,0:T(8,128)(2,1)S(1)} %get-tuple-element.205.refs_0_), channel_id=1, source_target_pairs={{0,8},{8,0},{16,24},{24,16},{1,9},{9,1},{17,25},{25,17},{2,10},{10... | collective-permute-start | bytes 3538952 | tf_op jit(solution)/shard_map/ppermute | solution.py:1428
  57.2 28.4 %collective-permute-start.8 = (bf16[2,4,9,32,256]{4,3,2,1,0:T(8,128)(2,1)S(1)}, bf16[2,4,9,32,256]{4,3,2,1,0:T(8,128)(2,1)S(1)}, u32[]{:S(2)}, u32[]{:S(2)}) collective-permute-start(bf16[2,4,9,32,256]{4,3,2,1,0:T(8,128)(2,1)S(1)} %get-tuple-element.205.refs_0_), channel_id=1, source_target_pairs={{0,4},{4,0},{1,5},{5,1},{2,6},{6,2},{3,7},{7,3},{8,12},{12,8},{9,1... | collective-permute-start | bytes 3538952 | tf_op jit(solution)/shard_map/ppermute | solution.py:1428
  57.8 14.5 %collective-permute-start.11 = (bf16[2,4,4,64,256]{4,3,2,1,0:T(8,128)(2,1)S(1)}, bf16[2,4,4,64,256]{4,3,2,1,0:T(8,128)(2,1)S(1)}, u32[]{:S(2)}, u32[]{:S(2)}) collective-permute-start(bf16[2,4,4,64,256]{4,3,2,1,0:T(8,128)(2,1)S(1)} %get-tuple-element.206.refs_0_), channel_id=1, source_target_pairs={{0,8},{8,0},{16,24},{24,16},{1,9},{9,1},{17,25},{25,17},{2,10},{10... | collective-permute-start | bytes 3145736 | tf_op jit(solution)/shard_map/ppermute | solution.py:1428
  57.9 25.4 %collective-permute-start.9 = (bf16[2,4,4,64,256]{4,3,2,1,0:T(8,128)(2,1)S(1)}, bf16[2,4,4,64,256]{4,3,2,1,0:T(8,128)(2,1)S(1)}, u32[]{:S(2)}, u32[]{:S(2)}) collective-permute-start(bf16[2,4,4,64,256]{4,3,2,1,0:T(8,128)(2,1)S(1)} %get-tuple-element.206.refs_0_), channel_id=1, source_target_pairs={{0,16},{8,24},{16,0},{24,8},{1,17},{9,25},{17,1},{25,9},{2,18},{10... | collective-permute-start | bytes 3145736 | tf_op jit(solution)/shard_map/ppermute | solution.py:1428
  87.5 28.9 %collective-permute-start.17 = (bf16[1152,512]{1,0:T(8,128)(2,1)}, bf16[1152,512]{1,0:T(8,128)(2,1)}, u32[]{:S(2)}, u32[]{:S(2)}) collective-permute-start(bf16[1152,512]{1,0:T(8,128)(2,1)} %copy-done.11), channel_id=1, source_target_pairs={{0,8},{8,0},{16,24},{24,16},{1,9},{9,1},{17,25},{25,17},{2,10},{10... | collective-permute-start | bytes 3538952 | tf_op jit(solution)/shard_map/ppermute | solution.py:1428
  89.1 18.0 %collective-permute-start.16 = (bf16[4,4,64,256]{3,2,1,0:T(8,128)(2,1)S(1)}, bf16[4,4,64,256]{3,2,1,0:T(8,128)(2,1)S(1)}, u32[]{:S(2)}, u32[]{:S(2)}) collective-permute-start(bf16[4,4,64,256]{3,2,1,0:T(8,128)(2,1)S(1)} %bitcast.147), channel_id=1, source_target_pairs={{0,4},{4,0},{1,5},{5,1},{2,6},{6,2},{3,7},{7,3},{8,12},{12,8},{9,1... | collective-permute-start | bytes 1572872 | tf_op jit(solution)/shard_map/ppermute | solution.py:1428
  89.7 17.4 %collective-permute-start.15 = (bf16[4,9,32,256]{3,2,1,0:T(8,128)(2,1)S(1)}, bf16[4,9,32,256]{3,2,1,0:T(8,128)(2,1)S(1)}, u32[]{:S(2)}, u32[]{:S(2)}) collective-permute-start(bf16[4,9,32,256]{3,2,1,0:T(8,128)(2,1)S(1)} %bitcast.136), channel_id=1, source_target_pairs={{0,16},{8,24},{16,0},{24,8},{1,17},{9,25},{17,1},{25,9},{2,18},{10... | collective-permute-start | bytes 1769480 | tf_op jit(solution)/shard_map/ppermute | solution.py:1428
  109.4 25.6 %collective-permute-start.22 = (bf16[2,4,4,64,256]{4,3,2,1,0:T(8,128)(2,1)}, bf16[2,4,4,64,256]{4,3,2,1,0:T(8,128)(2,1)S(1)}, u32[]{:S(2)}, u32[]{:S(2)}) collective-permute-start(bf16[2,4,4,64,256]{4,3,2,1,0:T(8,128)(2,1)} %get-tuple-element.226.refs_0_), channel_id=1, source_target_pairs={{0,16},{8,24},{16,0},{24,8},{1,17},{9,25},{17,1},{25,9},{2,18},{10... | collective-permute-start | bytes 3145736 | tf_op jit(solution)/shard_map/ppermute | solution.py:1428
  110.0 27.8 %collective-permute-start.21 = (bf16[2,4,9,32,256]{4,3,2,1,0:T(8,128)(2,1)S(1)}, bf16[2,4,9,32,256]{4,3,2,1,0:T(8,128)(2,1)S(1)}, u32[]{:S(2)}, u32[]{:S(2)}) collective-permute-start(bf16[2,4,9,32,256]{4,3,2,1,0:T(8,128)(2,1)S(1)} %get-tuple-element.225.refs_0_), channel_id=1, source_target_pairs={{0,4},{4,0},{1,5},{5,1},{2,6},{6,2},{3,7},{7,3},{8,12},{12,8},{9,1... | collective-permute-start | bytes 3538952 | tf_op jit(solution)/shard_map/ppermute | solution.py:1428
  131.7 22.8 %collective-permute-start.25 = (bf16[1024,1536]{1,0:T(8,128)(2,1)}, bf16[1024,1536]{1,0:T(8,128)(2,1)}, u32[]{:S(2)}, u32[]{:S(2)}) collective-permute-start(bf16[1024,1536]{1,0:T(8,128)(2,1)} %get-tuple-element.239), channel_id=1, source_target_pairs={{0,8},{8,0},{16,24},{24,16},{1,9},{9,1},{17,25},{25,17},{2,10},{10... | collective-permute-start | bytes 9437192 | tf_op jit(solution)/shard_map/ppermute | solution.py:1428
  180.4 25.8 %collective-permute-start.27 = (bf16[1024,1536]{1,0:T(8,128)(2,1)S(1)}, bf16[1024,1536]{1,0:T(8,128)(2,1)S(1)}, u32[]{:S(2)}, u32[]{:S(2)}) collective-permute-start(bf16[1024,1536]{1,0:T(8,128)(2,1)S(1)} %get-tuple-element.261), channel_id=1, source_target_pairs={{0,8},{8,0},{16,24},{24,16},{1,9},{9,1},{17,25},{25,17},{2,10},{10... | collective-permute-start | bytes 9437192 | tf_op jit(solution)/shard_map/ppermute | solution.py:1428
  213.7 14.8 %collective-permute-start.28 = (bf16[512,512]{1,0:T(8,128)(2,1)S(1)}, bf16[512,512]{1,0:T(8,128)(2,1)S(1)}, u32[]{:S(2)}, u32[]{:S(2)}) collective-permute-start(bf16[512,512]{1,0:T(8,128)(2,1)S(1)} %get-tuple-element.262), channel_id=1, source_target_pairs={{0,4},{4,0},{1,5},{5,1},{2,6},{6,2},{3,7},{7,3},{8,12},{12,8},{9,1... | collective-permute-start | bytes 1572872 | tf_op jit(solution)/shard_map/ppermute | solution.py:1428
  223.0 34.9 %collective-permute-start.33 = (bf16[512,512]{1,0:T(8,128)(2,1)S(1)}, bf16[512,512]{1,0:T(8,128)(2,1)S(1)}, u32[]{:S(2)}, u32[]{:S(2)}) collective-permute-start(bf16[512,512]{1,0:T(8,128)(2,1)S(1)} %bitcast.143), channel_id=1, source_target_pairs={{0,4},{4,0},{1,5},{5,1},{2,6},{6,2},{3,7},{7,3},{8,12},{12,8},{9,1... | collective-permute-start | bytes 1572872 | tf_op jit(solution)/shard_map/ppermute | solution.py:1428
  223.7 33.6 %collective-permute-start.34 = (bf16[512,512]{1,0:T(8,128)(2,1)S(1)}, bf16[512,512]{1,0:T(8,128)(2,1)S(1)}, u32[]{:S(2)}, u32[]{:S(2)}) collective-permute-start(bf16[512,512]{1,0:T(8,128)(2,1)S(1)} %bitcast.145), channel_id=1, source_target_pairs={{0,16},{8,24},{16,0},{24,8},{1,17},{9,25},{17,1},{25,9},{2,18},{10... | collective-permute-start | bytes 1572872 | tf_op jit(solution)/shard_map/ppermute | solution.py:1428
  238.9 21.7 %collective-permute-start.31 = (bf16[1152,256]{1,0:T(8,128)(2,1)S(1)}, bf16[1152,256]{1,0:T(8,128)(2,1)S(1)}, u32[]{:S(2)}, u32[]{:S(2)}) collective-permute-start(bf16[1152,256]{1,0:T(8,128)(2,1)S(1)} %bitcast.129), channel_id=1, source_target_pairs={{0,16},{8,24},{16,0},{24,8},{1,17},{9,25},{17,1},{25,9},{2,18},{10... | collective-permute-start | bytes 1769480 | tf_op jit(solution)/shard_map/ppermute | solution.py:1428
  240.5 19.8 %collective-permute-start.32 = (bf16[1152,256]{1,0:T(8,128)(2,1)S(1)}, bf16[1152,256]{1,0:T(8,128)(2,1)S(1)}, u32[]{:S(2)}, u32[]{:S(2)}) collective-permute-start(bf16[1152,256]{1,0:T(8,128)(2,1)S(1)} %bitcast.131), channel_id=1, source_target_pairs={{0,4},{4,0},{1,5},{5,1},{2,6},{6,2},{3,7},{7,3},{8,12},{12,8},{9,1... | collective-permute-start | bytes 1769480 | tf_op jit(solution)/shard_map/ppermute | solution.py:1428
  273.4 15.8 %collective-permute-start.39 = (bf16[64,512]{1,0:T(8,128)(2,1)S(1)}, bf16[64,512]{1,0:T(8,128)(2,1)S(1)}, u32[]{:S(2)}, u32[]{:S(2)}) collective-permute-start(bf16[64,512]{1,0:T(8,128)(2,1)S(1)} %get-tuple-element.309), channel_id=1, source_target_pairs={{0,4},{4,0},{1,5},{5,1},{2,6},{6,2},{3,7},{7,3},{8,12},{12,8},{9,1... | collective-permute-start | bytes 196616 | tf_op jit(solution)/shard_map/ppermute | solution.py:1428
  274.1 27.0 %collective-permute-start.44 = (bf16[544,256]{1,0:T(8,128)(2,1)S(1)}, bf16[544,256]{1,0:T(8,128)(2,1)S(1)}, u32[]{:S(2)}, u32[]{:S(2)}) collective-permute-start(bf16[544,256]{1,0:T(8,128)(2,1)S(1)} %get-tuple-element.325), channel_id=1, source_target_pairs={{0,3},{1,0},{2,1},{3,2},{4,7},{5,4},{6,5},{7,6},{8,11},{9,8},{10,9... | collective-permute-start | bytes 835592 | tf_op jit(solution)/shard_map/ppermute | solution.py:1428
  274.1 27.6 %collective-permute-start.45 = (bf16[544,256]{1,0:T(8,128)(2,1)S(1)}, bf16[544,256]{1,0:T(8,128)(2,1)S(1)}, u32[]{:S(2)}, u32[]{:S(2)}) collective-permute-start(bf16[544,256]{1,0:T(8,128)(2,1)S(1)} %get-tuple-element.326), channel_id=1, source_target_pairs={{0,2},{1,3},{2,0},{3,1},{4,6},{5,7},{6,4},{7,5},{8,10},{9,11},{10,... | collective-permute-start | bytes 835592 | tf_op jit(solution)/shard_map/ppermute | solution.py:1428
  279.3 23.7 %collective-permute-start.46 = (bf16[544,256]{1,0:T(8,128)(2,1)S(1)}, bf16[544,256]{1,0:T(8,128)(2,1)S(1)}, u32[]{:S(2)}, u32[]{:S(2)}) collective-permute-start(bf16[544,256]{1,0:T(8,128)(2,1)S(1)} %get-tuple-element.327), channel_id=1, source_target_pairs={{0,1},{1,2},{2,3},{3,0},{4,5},{5,6},{6,7},{7,4},{8,9},{9,10},{10,1... | collective-permute-start | bytes 835592 | tf_op jit(solution)/shard_map/ppermute | solution.py:1428
  288.6 17.1 %collective-permute-start.42 = (bf16[1152,256]{1,0:T(8,128)(2,1)S(1)}, bf16[1152,256]{1,0:T(8,128)(2,1)S(1)}, u32[]{:S(2)}, u32[]{:S(2)}) collective-permute-start(bf16[1152,256]{1,0:T(8,128)(2,1)S(1)} %bitcast.132), channel_id=1, source_target_pairs={{0,16},{8,24},{16,0},{24,8},{1,17},{9,25},{17,1},{25,9},{2,18},{10... | collective-permute-start | bytes 1769480 | tf_op jit(solution)/shard_map/ppermute | solution.py:1428
  289.3 16.1 %collective-permute-start.43 = (bf16[1152,256]{1,0:T(8,128)(2,1)S(1)}, bf16[1152,256]{1,0:T(8,128)(2,1)S(1)}, u32[]{:S(2)}, u32[]{:S(2)}) collective-permute-start(bf16[1152,256]{1,0:T(8,128)(2,1)S(1)} %bitcast.135), channel_id=1, source_target_pairs={{0,4},{4,0},{1,5},{5,1},{2,6},{6,2},{3,7},{7,3},{8,12},{12,8},{9,1... | collective-permute-start | bytes 1769480 | tf_op jit(solution)/shard_map/ppermute | solution.py:1428
  301.1 33.8 %collective-permute-start.52 = (bf16[512,512]{1,0:T(8,128)(2,1)S(1)}, bf16[512,512]{1,0:T(8,128)(2,1)S(1)}, u32[]{:S(2)}, u32[]{:S(2)}) collective-permute-start(bf16[512,512]{1,0:T(8,128)(2,1)S(1)} %bitcast.141), channel_id=1, source_target_pairs={{0,4},{4,0},{1,5},{5,1},{2,6},{6,2},{3,7},{7,3},{8,12},{12,8},{9,1... | collective-permute-start | bytes 1572872 | tf_op jit(solution)/shard_map/ppermute | solution.py:1428
  301.6 29.3 %collective-permute-start.53 = (bf16[512,512]{1,0:T(8,128)(2,1)}, bf16[512,512]{1,0:T(8,128)(2,1)}, u32[]{:S(2)}, u32[]{:S(2)}) collective-permute-start(bf16[512,512]{1,0:T(8,128)(2,1)} %bitcast.78), channel_id=1, source_target_pairs={{0,16},{8,24},{16,0},{24,8},{1,17},{9,25},{17,1},{25,9},{2,18},{10... | collective-permute-start | bytes 1572872 | tf_op jit(solution)/shard_map/ppermute | solution.py:1428
  307.9 15.8 %collective-permute-start.48 = (bf16[576,256]{1,0:T(8,128)(2,1)}, bf16[576,256]{1,0:T(8,128)(2,1)}, u32[]{:S(2)}, u32[]{:S(2)}) collective-permute-start(bf16[576,256]{1,0:T(8,128)(2,1)} %get-tuple-element.336), channel_id=1, source_target_pairs={{0,4},{4,0},{1,5},{5,1},{2,6},{6,2},{3,7},{7,3},{8,12},{12,8},{9,1... | collective-permute-start | bytes 884744 | tf_op jit(solution)/shard_map/ppermute | solution.py:1428
  309.6 14.2 %collective-permute-start.47 = (bf16[576,256]{1,0:T(8,128)(2,1)S(1)}, bf16[576,256]{1,0:T(8,128)(2,1)}, u32[]{:S(2)}, u32[]{:S(2)}) collective-permute-start(bf16[576,256]{1,0:T(8,128)(2,1)S(1)} %get-tuple-element.334), channel_id=1, source_target_pairs={{0,16},{8,24},{16,0},{24,8},{1,17},{9,25},{17,1},{25,9},{2,18},{10... | collective-permute-start | bytes 884744 | tf_op jit(solution)/shard_map/ppermute | solution.py:1428
  326.8 15.1 %collective-permute-start.49 = (bf16[352,256]{1,0:T(8,128)(2,1)}, bf16[352,256]{1,0:T(8,128)(2,1)}, u32[]{:S(2)}, u32[]{:S(2)}) collective-permute-start(bf16[352,256]{1,0:T(8,128)(2,1)} %get-tuple-element.351), channel_id=1, source_target_pairs={{0,3},{1,0},{2,1},{3,2},{4,7},{5,4},{6,5},{7,6},{8,11},{9,8},{10,9... | collective-permute-start | bytes 540680 | tf_op jit(solution)/shard_map/ppermute | solution.py:1428
  (94 other events, 659.4 us)

commit v2 on v1

--- a/solution.py
+++ b/solution.py
@@ -189,7 +189,7 @@
             for packet_ref in packet_refs:
                 packet_ref[:, :width] = lowered_ref[...]
 
-        for at, size in row_chunks(rows, 256):
+        for at, size in row_chunks(rows, 512):
             some = pl.ds(at, size)
             term = None
             for c in range(cores):
@@ -974,7 +974,7 @@
     return found[:slots], (found[slots],)
 
 
-def pack_small(row_groups, biases, losses, places, sizes, ffn_rows, after=()):
+def pack_small(row_groups, biases, losses, places, sizes, ffn_rows, after=(), reads=()):
     cores, seqs, acrosses, tap_peers = sizes
     width = row_groups[0][0].shape[1]
     head_rows = sum(count for _, count in row_groups)
@@ -1047,14 +1047,14 @@
     flat = [array for array, _ in row_groups] + [each for some in biases for each in some]
     found = pl.pallas_call(
         kernel,
-        in_specs=[SCALARS] + [WHOLE] * (len(flat) + 1 + len(after)),
+        in_specs=[SCALARS] + [WHOLE] * (len(flat) + 1 + len(after)) + [ANYWHERE] * len(reads),
         out_specs=[WHOLE] * 2,
         out_shape=[jax.ShapeDtypeStruct((2 * rows, lanes), jnp.bfloat16), TOKEN],
         scratch_shapes=[pltpu.VMEM((rows, width), jnp.float32)],
         compiler_params=pltpu.CompilerParams(vmem_limit_bytes=8 * MIB),
         cost_estimate=cost(2),
         name="pack_small",
-    )(jnp.stack(places).astype(jnp.int32), *flat, losses, *after)
+    )(jnp.stack(places).astype(jnp.int32), *flat, losses, *after, *reads)
     return found[0], (found[1],)
 
 
@@ -1619,7 +1619,7 @@
     def cut_ffn(piece):
         return piece.reshape(ffn_rows, core.size, lanes).swapaxes(0, 1).reshape(-1, lanes)
 
-    def bundle(b):
+    def bundle(b, ready=None):
         conv_piece = lax.dynamic_slice(
             conv_weight[b],
             (0, (seq.index * across.size + across.index) * slab, core.index * lanes),
@@ -1630,6 +1630,8 @@
             cut_ffn(in_weight[b].T),
             cut_ffn(out_weight[b]),
         ]
+        if ready is not None:
+            pieces = [piece + ready for piece in pieces]
         return jnp.concatenate(pieces)
 
     cuts = (
@@ -1649,8 +1651,8 @@
     rim_reaches = [reach if seq.size == 2 and reach <= rows else 0 for reach in reaches]
 
     tap_parts = tap.gather(bundle(0))
-    behind = bundle(1)
     found = rims(conv_input, reaches[0], seq)
+    behind = bundle(1, tap_parts[-1][0, 0] * 0)
     (conv_part, ffn_part), last = restack(
         [(tap_parts, cuts)], reads=[behind] + [found if rim_reaches[0] else conv_input]
     )
@@ -1662,7 +1664,7 @@
     conv_parts, ffn_parts = across.gather(conv_part), seq.gather(ffn_part)
     (conv_part, ffn_part), last = restack(
         [straight(conv_parts), straight(ffn_parts)],
-        reads=[late_parts[by] for by in range(1, tap.size) if by != split],
+        reads=late_parts[1:split],
         after=last,
     )
     conv_parts, ffn_parts = seq.gather(conv_part), across.gather(ffn_part)
@@ -1849,31 +1851,29 @@
             ffn_sums[0], last = ffn_grads(last)
             for each in conv_sums[0]:
                 last = each.step(1, last, merged[1][1:])
-        stream_grad, last = conv_data_grad(
-            extended_grad,
-            conv_full[b],
-            stream_grad,
-            steps[b],
-            jnp.float32 if b == 1 else jnp.bfloat16,
-            last,
-        )
-
-    grad_inputs = from_rows(stream_grad, windows)
+        if b == 1:
+            stream_grad, last = conv_data_grad(
+                extended_grad, conv_full[1], stream_grad, steps[1], jnp.float32, last
+            )
 
     row_groups = [(each, 3) for each in conv_rows_of_sums + ffn_rows_of_sums]
     row_groups.append((head_grad, head_weight.shape[1]))
     (conv_input,), last = hold([conv_input], last)
     final_state = from_rows(conv_input, windows)
-    packed, last = pack_small(row_groups, in_bias_grads, loss_rows, places, sizes, ffn_rows, last)
+    packed, last = pack_small(row_groups, in_bias_grads, loss_rows, places, sizes, ffn_rows, last, [final_state])
 
     conv_rows = taps * slab
-    merged[0], last = append_slots(groups(conv_sums[0]), [packed], last, [final_state])
+    merged[0], last = append_slots(groups(conv_sums[0]), [packed], last)
     merged[0] = tap.swap(merged[0])
+    stream_grad, last = conv_data_grad(
+        extended_grad, conv_full[0], stream_grad, steps[0], jnp.bfloat16, last
+    )
     for each in ffn_sums[0]:
         last = each.step(1, last)
     shards, last = finish_conv([merged[0], merged[1]], conv_rows, packed.shape[0], last)
-    ffn_late, last = append_slots(groups(ffn_sums[0]), [], last, [grad_inputs])
+    ffn_late, last = append_slots(groups(ffn_sums[0]), [], last)
     ffn_late = tap.swap(ffn_late)
+    grad_inputs = from_rows(stream_grad, windows)
     copies = [each for row in shared_copies(shards, across, seq) for each in row]
     grad_in, grad_out, last = finish_ffn(merged[1], ffn_late, conv_rows, ffn_rows, last)
     (stack,), last = restack([straight(copies)], after=last)

time: 377 us -> 361 us (0.958)
  Pallas kernels: 194 us -> 178 us
  starting transfers between devices: 56.5 us -> 67.1 us
  waiting for transfers between devices: 90.1 us -> 82.8 us
    ppermute x60, starting transfers between devices: 53 us -> 63.6 us  [shifted(): lax.ppermute(value, self.axis, self.pairs(lambda i: (i + by) % self.size))]
    pallas_call x2, Pallas kernels: 26.9 us -> 16.3 us  [ffn_back_hidden(): pl.pallas_call(kernel, grid=(units // block,), in_specs=[whole, whole, pl...]
    ppermute x60, waiting for transfers between devices: 89.8 us -> 82.8 us  [shifted(): lax.ppermute(value, self.axis, self.pairs(lambda i: (i + by) % self.size))]
    pallas_call x8, Pallas kernels: 7.59 us -> 3.59 us  [add_slots(): pl.pallas_call(kernel, grid=(rows // block,), in_specs=[pl.BlockSpec((slo...]
    unnamed x131 -> x123, local copies, waits for them, and re-layouts: 10.4 us -> 9.04 us
  transfers between devices with their start and end apart: 63 -> 63, of which waited for: 24 -> 23; matrix products, arithmetic and copies ran while one was open for 3% -> 4% of each run, Pallas kernels for 46% -> 43%
where the time goes in v2:
time: 361 us; the launch traced here: 358 us
  Pallas kernels  178 us (49%)
  waiting for transfers between devices  82.8 us (23%)
  starting transfers between devices  67.1 us (19%)
  local copies, waits for them, and re-layouts  25.4 us (7%)
    ppermute x60, waiting for transfers between devices, shifted(): lax.ppermute(value, self.axis, self.pairs(lambda i: (i + by) % self.size))  82.8 us
    ppermute x60, starting transfers between devices, shifted(): lax.ppermute(value, self.axis, self.pairs(lambda i: (i + by) % self.size))  63.6 us
    pallas_call x2, Pallas kernels, ffn_forward(): pl.pallas_call(kernel, grid=(steps,), in_specs=[SCALARS, whole, whole, ro...  26.1 us
    pallas_call x2, Pallas kernels, conv_forward(): pl.pallas_call(kernel, grid=(steps,), in_specs=[pl.BlockSpec(extended.sha...  23.9 us
    pallas_call x2, Pallas kernels, conv_weight_grad(): pl.pallas_call(kernel, grid_spec=pltpu.PrefetchScalarGridSpec(num_scalar_...  19.4 us
    pallas_call x2, Pallas kernels, ffn_back_hidden(): pl.pallas_call(kernel, grid=(units // block,), in_specs=[whole, whole, pl...  16.3 us
    pallas_call x2, Pallas kernels, ffn_weight_grad(): pl.pallas_call(kernel, grid=(acrosses * seqs,), in_specs=([left_spec, rig...  15.9 us
    pallas_call x2, Pallas kernels, conv_data_grad(): pl.pallas_call(kernel, grid=(steps,), in_specs=[pl.BlockSpec(extended.sha...  15.4 us
  transfers between devices with their start and end apart: 63, of which 23 were waited for; matrix products, arithmetic and copies ran while one was open for 4% of the time, Pallas kernels for 43%

profile of v2, /device:TPU:0, one launch (start us, length us, event | category | flops | bytes accessed | tf_op | source)
XLA Modules:
  0.0 357.7 jit_solution(10527211392057525509)
XLA Ops:
  5.4 5.1 %collective-permute-start.1 = (bf16[544,256]{1,0:T(8,128)(2,1)S(1)}, bf16[544,256]{1,0:T(8,128)(2,1)S(1)}, u32[]{:S(2)}, u32[]{:S(2)}) collective-permute-start(bf16[544,256]{1,0:T(8,128)(2,1)S(1)} %pad_maximum_fusion.refs_0_), channel_id=1, source_target_pairs={{0,3},{1,0},{2,1},{3,2},{4,7},{5,4},{6,5},{7,6},{8,11},{9,8},{10,9... | collective-permute-start | bytes 835592 | tf_op jit(solution)/shard_map/ppermute | solution.py:1428
  14.3 3.3 collective-permute-done.1.refs_3_
  19.9 14.3 %collective-permute-done.3.refs_2_ = bf16[544,256]{1,0:T(8,128)(2,1)S(1)} collective-permute-done((bf16[544,256]{1,0:T(8,128)(2,1)S(1)}, bf16[544,256]{1,0:T(8,128)(2,1)S(1)}, u32[]{:S(2)}, u32[]{:S(2)}) %collective-permute-start.3) | collective-permute-done | bytes 278560 | tf_op jit(solution)/shard_map/ppermute | solution.py:1428
  40.8 6.8 %collective-permute-done.6.refs_4_.refs_1_ = bf16[544,256]{1,0:T(8,128)(2,1)S(1)} collective-permute-done((bf16[544,256]{1,0:T(8,128)(2,1)S(1)}, bf16[544,256]{1,0:T(8,128)(2,1)S(1)}, u32[]{:S(2)}, u32[]{:S(2)}) %collective-permute-start.6) | collective-permute-done | bytes 278560 | tf_op jit(solution)/shard_map/ppermute | solution.py:1428
  53.9 8.6 %collective-permute-done.12.refs_6_.refs_3_ = bf16[544,256]{1,0:T(8,128)(2,1)S(1)} collective-permute-done((bf16[544,256]{1,0:T(8,128)(2,1)S(1)}, bf16[544,256]{1,0:T(8,128)(2,1)S(1)}, u32[]{:S(2)}, u32[]{:S(2)}) %collective-permute-start.12) | collective-permute-done | bytes 278560 | tf_op jit(solution)/shard_map/ppermute | solution.py:1428
  65.6 12.0 %collective-permute-done.11.refs_5_.refs_2_ = bf16[544,256]{1,0:T(8,128)(2,1)S(1)} collective-permute-done((bf16[544,256]{1,0:T(8,128)(2,1)S(1)}, bf16[544,256]{1,0:T(8,128)(2,1)S(1)}, u32[]{:S(2)}, u32[]{:S(2)}) %collective-permute-start.11) | collective-permute-done | bytes 278560 | tf_op jit(solution)/shard_map/ppermute | solution.py:1428
  85.5 4.7 %place_conv.2 = (bf16[9,512,512]{2,1,0:T(8,128)(2,1)}, f32[8,128]{1,0:T(8,128)S(1)}) custom-call(s32[4]{0:T(128)S(1)} %pad_add_fusion.place_ref, bf16[2,4,9,32,256]{4,3,2,1,0:T(8,128)(2,1)S(1)} %copy-done.14, bf16[2,4,9,32,256]{4,3,2,1,0:T(8,128)(2,1)S(1)} %get-tuple-element.208.refs_1_, bf16[2,4,9,32,256]{4,3,2,1,0:T(8,128)(2,1)S(1)} %collective-permute-done.9.refs_2_, ...), custom_call_target="tpu_custom_call" | custom-call | flops 3300000000 | bytes 10500000 | tf_op jit(solution)/shard_map/place_conv/pallas_call | solution.py:1361
  90.3 11.0 %conv_forward.2 = (bf16[1024,512]{1,0:T(8,128)(2,1)}, bf16[1024,512]{1,0:T(8,128)(2,1)}, f32[1024,512]{1,0:T(8,128)}, bf16[1024,512]{1,0:T(8,128)(2,1)S(1)}, f32[8,128]{1,0:T(8,128)S(1)}) custom-call(bf16[1152,512]{1,0:T(8,128)(2,1)S(1)} %copy-done.11, bf16[9,512,512]{2,1,0:T(8,128)(2,1)} %get-tuple-element.212.weight_ref, ...), custom_call_target="tpu_custom_call" | custom-call | flops 9900000256 | bytes 31500000 | tf_op jit(solution)/shard_map/conv_forward/pallas_call | solution.py:124
  107.0 3.7 %place_ffn.2 = (bf16[2,2,4,64,512]{4,3,2,1,0:T(8,128)(2,1)}, bf16[2,2,4,64,512]{4,3,2,1,0:T(8,128)(2,1)}, bf16[2,2,4,64,512]{4,3,2,1,0:T(8,128)(2,1)}, bf16[2,2,4,64,512]{4,3,2,1,0:T(8,128)(2,1)}, f32[8,128]{1,0:T(8,128)S(1)}) custom-call(bf16[2,4,4,64,256]{4,3,2,1,0:T(8,128)(2,1)S(1)} %copy-done.16, bf16[2,4,4,64,256]{4,3,2,1,0:T(8,128)(2,1)S(1)} %copy-done.5, ...), custom_call_target="tpu_custom_call" | custom-call | flops 2200000000 | bytes 7000000 | tf_op jit(solution)/shard_map/place_ffn/pallas_call | solution.py:1408
  110.7 13.9 %ffn_forward.2 = (bf16[1024,1024]{1,0:T(8,128)(2,1)}, bf16[1024,1024]{1,0:T(8,128)(2,1)}, bf16[1024,1024]{1,0:T(8,128)(2,1)}, bf16[1024,512]{1,0:T(8,128)(2,1)},...) custom-call(s32[1]{0:T(128)} %bitcast.place_ref, ...), custom_call_target="tpu_custom_call" | custom-call | flops 12099999744 | bytes 38500000 | tf_op jit(solution)/shard_map/ffn_forward/pallas_call | solution.py:232
  124.7 4.4 %collective-permute-done.22.refs_1_ = bf16[2,4,4,64,256]{4,3,2,1,0:T(8,128)(2,1)S(1)} collective-permute-done((bf16[2,4,4,64,256]{4,3,2,1,0:T(8,128)(2,1)}, bf16[2,4,4,64,256]{4,3,2,1,0:T(8,128)(2,1)S(1)}, u32[]{:S(2)}, u32[]{:S(2)}) %collective-permute-start.22) | collective-permute-done | bytes 1048608 | tf_op jit(solution)/shard_map/ppermute | solution.py:1428
  134.9 4.6 %place_conv.3 = (bf16[9,512,512]{2,1,0:T(8,128)(2,1)}, f32[8,128]{1,0:T(8,128)S(1)}) custom-call(s32[4]{0:T(128)S(1)} %pad_add_fusion.place_ref, bf16[2,4,9,32,256]{4,3,2,1,0:T(8,128)(2,1)S(1)} %get-tuple-element.225.refs_0_, bf16[2,4,9,32,256]{4,3,2,1,0:T(8,128)(2,1)S(1)} %get-tuple-element.231.refs_1_, ...), custom_call_target="tpu_custom_call" | custom-call | flops 3300000000 | bytes 10500000 | tf_op jit(solution)/shard_map/place_conv/pallas_call | solution.py:1361
  139.6 3.6 %place_ffn.3 = (bf16[2,2,4,64,512]{4,3,2,1,0:T(8,128)(2,1)}, bf16[2,2,4,64,512]{4,3,2,1,0:T(8,128)(2,1)}, bf16[2,2,4,64,512]{4,3,2,1,0:T(8,128)(2,1)}, bf16[2,2,4,64,512]{4,3,2,1,0:T(8,128)(2,1)}, f32[8,128]{1,0:T(8,128)S(1)}) custom-call(bf16[2,4,4,64,256]{4,3,2,1,0:T(8,128)(2,1)} %get-tuple-element.226.refs_0_, ...), custom_call_target="tpu_custom_call" | custom-call | flops 2200000000 | bytes 7000000 | tf_op jit(solution)/shard_map/place_ffn/pallas_call | solution.py:1408
  143.2 3.2 collective-permute-done.20.found_ref
  148.7 12.8 %conv_forward.3 = (bf16[1024,512]{1,0:T(8,128)(2,1)}, bf16[1024,512]{1,0:T(8,128)(2,1)}, f32[1024,512]{1,0:T(8,128)}, bf16[1024,512]{1,0:T(8,128)(2,1)S(1)}, f32[8,128]{1,0:T(8,128)S(1)}) custom-call(bf16[2048,512]{1,0:T(8,128)(2,1)} %get-tuple-element.235.extended_ref.refs_0_, bf16[9,512,512]{2,1,0:T(8,128)(2,1)} %get-tuple-element.236.weight_ref, ...), custom_call_target="tpu_custom_call" | custom-call | flops 9900000256 | bytes 31500000 | tf_op jit(solution)/shard_map/conv_forward/pallas_call | solution.py:124
  161.6 12.2 %ffn_forward.3 = (bf16[1024,1024]{1,0:T(8,128)(2,1)}, bf16[1024,1024]{1,0:T(8,128)(2,1)}, bf16[1024,1024]{1,0:T(8,128)(2,1)}, bf16[1024,512]{1,0:T(8,128)(2,1)},...) custom-call(s32[1]{0:T(128)} %bitcast.place_ref, ...), custom_call_target="tpu_custom_call" | custom-call | flops 12099999744 | bytes 38500000 | tf_op jit(solution)/shard_map/ffn_forward/pallas_call | solution.py:232
  174.5 6.0 %head_and_loss.1 = (f32[1024,512]{1,0:T(8,128)S(1)}, f32[8,512]{1,0:T(8,128)S(1)}, f32[8,128]{1,0:T(8,128)S(1)}, f32[8,128]{1,0:T(8,128)S(1)}) custom-call(f32[1024,512]{1,0:T(8,128)S(1)} %get-tuple-element.248.stream_ref, f32[512,128]{1,0:T(8,128)S(1)} %pad.4.head_ref, s32[1024,128]{1,0:T(8,128)S(1)} %broadcast_in_dim.8.code_ref, ...), custom_call_target="tpu_custom_call" | custom-call | flops 6600000000 | bytes 21000000 | tf_op jit(solution)/shard_map/head_and_loss/pallas_call | solution.py:331
  180.6 8.3 %ffn_back_hidden.2 = (bf16[1024,512]{1,0:T(8,128)(2,1)S(1)}, bf16[1024,1024]{1,0:T(8,128)(2,1)}, f32[1,1024]{1,0:T(1,128)S(1)}, f32[1,1024]{1,0:T(1,128)S(1)}, b...) custom-call(f32[1024,512]{1,0:T(8,128)S(1)} %get-tuple-element.250.upstream_ref, ...), custom_call_target="tpu_custom_call" | custom-call | flops 6600000000 | bytes 21000000 | tf_op jit(solution)/shard_map/ffn_back_hidden/pallas_call | solution.py:397
  189.0 7.5 %ffn_back_stream.2 = (f32[1024,512]{1,0:T(8,128)S(1)}, bf16[1024,512]{1,0:T(8,128)(2,1)S(1)}, bf16[1024,256]{1,0:T(8,128)(2,1)S(1)}, bf16[512,512]{1,0:T(8,128)(...) custom-call(s32[2]{0:T(128)S(1)} %pad_add_fusion.1.core_ref, f32[1024,512]{1,0:T(8,128)S(1)} %get-tuple-element.250.upstream_ref, ...), custom_call_target="tpu_custom_call" | custom-call | flops 5500000256 | bytes 17500000 | tf_op jit(solution)/shard_map/ffn_back_stream/pallas_call | solution.py:505
  198.4 7.6 %ffn_weight_grad.2 = (bf16[2,2,2,64,512]{4,3,2,1,0:T(8,128)(2,1)S(1)}, bf16[2,2,2,64,512]{4,3,2,1,0:T(8,128)(2,1)S(1)}, bf16[2,2,2,64,512]{4,3,2,1,0:T(8,128)(2,...) custom-call(bf16[1024,1024]{1,0:T(8,128)(2,1)} %get-tuple-element.258.refs_0_, ...), custom_call_target="tpu_custom_call" | custom-call | flops 8800000000 | bytes 28000000 | tf_op jit(solution)/shard_map/ffn_weight_grad/pallas_call | solution.py:873
  208.0 3.4 collective-permute-done.28.found_ref
  211.5 10.2 %conv_weight_grad.2 = (bf16[2,2,9,32,256]{4,3,2,1,0:T(8,128)(2,1)S(1)}, bf16[2,2,9,32,256]{4,3,2,1,0:T(8,128)(2,1)S(1)}, bf16[2,2,9,32,256]{4,3,2,1,0:T(8,128)(2...) custom-call(s32[4]{0:T(128)S(1)} %pad_add_fusion.place_ref, ...), custom_call_target="tpu_custom_call" | custom-call | flops 9900000256 | bytes 31500000 | tf_op jit(solution)/shard_map/conv_weight_grad/pallas_call | solution.py:765
  223.9 7.7 %conv_data_grad.2 = (f32[1024,512]{1,0:T(8,128)S(1)}, f32[8,128]{1,0:T(8,128)S(1)}) custom-call(bf16[2048,512]{1,0:T(8,128)(2,1)S(1)} %get-tuple-element.268.extended_ref, bf16[9,512,512]{2,1,0:T(8,128)(2,1)} %get-tuple-element.236.weight_ref, f32[1024,512]{1,0:T(8,128)S(1)} %get-tuple-element.269.upstream_ref, f32[8,128]{1,0:T(8,128)S(1)} %get-tuple-element.272.refs_0_), custom_call_target="tpu_custom_call" | custom-call | flops 6600000000 | bytes 21000000 | tf_op jit(solution)/shard_map/conv_data_grad/pallas_call | solution.py:593
  231.7 8.1 %ffn_back_hidden.3 = (bf16[1024,512]{1,0:T(8,128)(2,1)S(1)}, bf16[1024,1024]{1,0:T(8,128)(2,1)}, f32[1,1024]{1,0:T(1,128)S(1)}, f32[1,1024]{1,0:T(1,128)S(1)}, b...) custom-call(f32[1024,512]{1,0:T(8,128)S(1)} %get-tuple-element.273.upstream_ref, ...), custom_call_target="tpu_custom_call" | custom-call | flops 6600000000 | bytes 21000000 | tf_op jit(solution)/shard_map/ffn_back_hidden/pallas_call | solution.py:397
  245.5 7.7 %ffn_back_stream.3 = (f32[1024,512]{1,0:T(8,128)S(1)}, bf16[1024,512]{1,0:T(8,128)(2,1)S(1)}, bf16[1024,256]{1,0:T(8,128)(2,1)S(1)}, bf16[1024,1536]{1,0:T(8,128...) custom-call(s32[2]{0:T(128)S(1)} %pad_add_fusion.1.core_ref, ...), custom_call_target="tpu_custom_call" | custom-call | flops 5500000256 | bytes 17500000 | tf_op jit(solution)/shard_map/ffn_back_stream/pallas_call | solution.py:505
  263.0 9.2 %conv_weight_grad.3 = (bf16[2,2,9,32,256]{4,3,2,1,0:T(8,128)(2,1)S(1)}, bf16[2,2,9,32,256]{4,3,2,1,0:T(8,128)(2,1)S(1)}, bf16[2,2,9,32,256]{4,3,2,1,0:T(8,128)(2...) custom-call(s32[4]{0:T(128)S(1)} %pad_add_fusion.place_ref, bf16[1152,512]{1,0:T(8,128)(2,1)S(1)} %copy-done.12, ...), custom_call_target="tpu_custom_call" | custom-call | flops 9900000256 | bytes 31500000 | tf_op jit(solution)/shard_map/conv_weight_grad/pallas_call | solution.py:765
  276.0 8.3 %ffn_weight_grad.3 = (bf16[2,2,2,64,512]{4,3,2,1,0:T(8,128)(2,1)S(1)}, bf16[2,2,2,64,512]{4,3,2,1,0:T(8,128)(2,1)S(1)}, bf16[2,2,2,64,512]{4,3,2,1,0:T(8,128)(2,...) custom-call(bf16[1024,1024]{1,0:T(8,128)(2,1)} %get-tuple-element.281.refs_0_, ...), custom_call_target="tpu_custom_call" | custom-call | flops 8800000000 | bytes 28000000 | tf_op jit(solution)/shard_map/ffn_weight_grad/pallas_call | solution.py:873
  284.4 3.6 %collective-permute-done.42 = bf16[1152,256]{1,0:T(8,128)(2,1)S(1)} collective-permute-done((bf16[1152,256]{1,0:T(8,128)(2,1)S(1)}, bf16[1152,256]{1,0:T(8,128)(2,1)S(1)}, u32[]{:S(2)}, u32[]{:S(2)}) %collective-permute-start.42) | collective-permute-done | bytes 589856 | tf_op jit(solution)/shard_map/ppermute | solution.py:1428
  306.6 7.7 %conv_data_grad.3 = (bf16[1024,512]{1,0:T(8,128)(2,1)S(1)}, f32[8,128]{1,0:T(8,128)S(1)}) custom-call(bf16[1152,512]{1,0:T(8,128)(2,1)S(1)} %copy-done.34, bf16[9,512,512]{2,1,0:T(8,128)(2,1)} %get-tuple-element.212.weight_ref, f32[1024,512]{1,0:T(8,128)S(1)} %copy-done.32, f32[8,128]{1,0:T(8,128)S(1)} %get-tuple-element.348.refs_0_), custom_call_target="tpu_custom_call" | custom-call | flops 6600000000 | bytes 21000000 | tf_op jit(solution)/shard_map/conv_data_grad/pallas_call | solution.py:593
  323.3 7.4 %collective-permute-start.59 = (bf16[128,512]{1,0:T(8,128)(2,1)S(1)}, bf16[128,512]{1,0:T(8,128)(2,1)S(1)}, u32[]{:S(2)}, u32[]{:S(2)}) collective-permute-start(bf16[128,512]{1,0:T(8,128)(2,1)S(1)} %get-tuple-element.369), channel_id=1, source_target_pairs={{0,3},{1,0},{2,1},{3,2},{4,7},{5,4},{6,5},{7,6},{8,11},{9,8},{10,9... | collective-permute-start | bytes 393224 | tf_op jit(solution)/shard_map/ppermute | solution.py:1428
  334.8 6.6 %collective-permute-done.60.refs_6_ = bf16[128,512]{1,0:T(8,128)(2,1)S(1)} collective-permute-done((bf16[128,512]{1,0:T(8,128)(2,1)S(1)}, bf16[128,512]{1,0:T(8,128)(2,1)S(1)}, u32[]{:S(2)}, u32[]{:S(2)}) %collective-permute-start.60) | collective-permute-done | bytes 131104 | tf_op jit(solution)/shard_map/ppermute | solution.py:1428
  350.6 6.9 %place_conv_grads.1 = f32[2,9,128,512]{3,2,1,0:T(8,128)} custom-call(s32[3]{0:T(128)S(1)} %pad_add_fusion.2.place_ref, bf16[4,20,32,256]{3,2,1,0:T(8,128)(2,1)S(1)} %bitcast.124, bf16[4,20,32,256]{3,2,1,0:T(8,128)(2,1)S(1)} %bitcast.125, bf16[4,20,32,256]{3,2,1,0:T(8,128)(2,1)} %bitcast.86.refs_2_.refs_3_, bf16[4,20,32,256]{3,2,1,0:T(8,128)(2,1)} %bitcast.86.refs_2_.refs_3_), custom_call_target="tpu_custom_call" | custom-call | flops 5500000256 | bytes 17500000 | tf_op jit(solution)/shard_map/place_conv_grads/pallas_call | solution.py:1297
  (320 shorter events, 114.2 us)
Async XLA Ops:
  10.5 23.7 %collective-permute-start.3 = (bf16[544,256]{1,0:T(8,128)(2,1)S(1)}, bf16[544,256]{1,0:T(8,128)(2,1)S(1)}, u32[]{:S(2)}, u32[]{:S(2)}) collective-permute-start(bf16[544,256]{1,0:T(8,128)(2,1)S(1)} %pad_maximum_fusion.refs_0_), channel_id=1, source_target_pairs={{0,2},{1,3},{2,0},{3,1},{4,6},{5,7},{6,4},{7,5},{8,10},{9,11},{10,... | collective-permute-start | bytes 835592 | tf_op jit(solution)/shard_map/ppermute | solution.py:1428
  10.5 23.7 %collective-permute-start.2 = (bf16[544,256]{1,0:T(8,128)(2,1)S(1)}, bf16[544,256]{1,0:T(8,128)(2,1)S(1)}, u32[]{:S(2)}, u32[]{:S(2)}) collective-permute-start(bf16[544,256]{1,0:T(8,128)(2,1)S(1)} %pad_maximum_fusion.refs_0_), channel_id=1, source_target_pairs={{0,1},{1,2},{2,3},{3,0},{4,5},{5,6},{6,7},{7,4},{8,9},{9,10},{10,1... | collective-permute-start | bytes 835592 | tf_op jit(solution)/shard_map/ppermute | solution.py:1428
  35.8 14.3 %collective-permute-start.4 = (bf16[4,9,32,256]{3,2,1,0:T(8,128)(2,1)S(1)}, bf16[4,9,32,256]{3,2,1,0:T(8,128)(2,1)S(1)}, u32[]{:S(2)}, u32[]{:S(2)}) collective-permute-start(bf16[4,9,32,256]{3,2,1,0:T(8,128)(2,1)S(1)} %bitcast.135), channel_id=1, source_target_pairs={{0,16},{8,24},{16,0},{24,8},{1,17},{9,25},{17,1},{25,9},{2,18},{10... | collective-permute-start | bytes 1769480 | tf_op jit(solution)/shard_map/ppermute | solution.py:1428
  50.4 27.2 %collective-permute-start.9 = (bf16[2,4,9,32,256]{4,3,2,1,0:T(8,128)(2,1)S(1)}, bf16[2,4,9,32,256]{4,3,2,1,0:T(8,128)(2,1)S(1)}, u32[]{:S(2)}, u32[]{:S(2)}) collective-permute-start(bf16[2,4,9,32,256]{4,3,2,1,0:T(8,128)(2,1)S(1)} %get-tuple-element.205.refs_0_), channel_id=1, source_target_pairs={{0,8},{8,0},{16,24},{24,16},{1,9},{9,1},{17,25},{25,17},{2,10},{10... | collective-permute-start | bytes 3538952 | tf_op jit(solution)/shard_map/ppermute | solution.py:1428
  50.5 28.4 %collective-permute-start.7 = (bf16[2,4,9,32,256]{4,3,2,1,0:T(8,128)(2,1)S(1)}, bf16[2,4,9,32,256]{4,3,2,1,0:T(8,128)(2,1)S(1)}, u32[]{:S(2)}, u32[]{:S(2)}) collective-permute-start(bf16[2,4,9,32,256]{4,3,2,1,0:T(8,128)(2,1)S(1)} %get-tuple-element.205.refs_0_), channel_id=1, source_target_pairs={{0,4},{4,0},{1,5},{5,1},{2,6},{6,2},{3,7},{7,3},{8,12},{12,8},{9,1... | collective-permute-start | bytes 3538952 | tf_op jit(solution)/shard_map/ppermute | solution.py:1428
  52.1 25.6 %collective-permute-start.10 = (bf16[2,4,4,64,256]{4,3,2,1,0:T(8,128)(2,1)S(1)}, bf16[2,4,4,64,256]{4,3,2,1,0:T(8,128)(2,1)S(1)}, u32[]{:S(2)}, u32[]{:S(2)}) collective-permute-start(bf16[2,4,4,64,256]{4,3,2,1,0:T(8,128)(2,1)S(1)} %get-tuple-element.206.refs_0_), channel_id=1, source_target_pairs={{0,8},{8,0},{16,24},{24,16},{1,9},{9,1},{17,25},{25,17},{2,10},{10... | collective-permute-start | bytes 3145736 | tf_op jit(solution)/shard_map/ppermute | solution.py:1428
  52.2 25.4 %collective-permute-start.8 = (bf16[2,4,4,64,256]{4,3,2,1,0:T(8,128)(2,1)S(1)}, bf16[2,4,4,64,256]{4,3,2,1,0:T(8,128)(2,1)S(1)}, u32[]{:S(2)}, u32[]{:S(2)}) collective-permute-start(bf16[2,4,4,64,256]{4,3,2,1,0:T(8,128)(2,1)S(1)} %get-tuple-element.206.refs_0_), channel_id=1, source_target_pairs={{0,16},{8,24},{16,0},{24,8},{1,17},{9,25},{17,1},{25,9},{2,18},{10... | collective-permute-start | bytes 3145736 | tf_op jit(solution)/shard_map/ppermute | solution.py:1428
  62.6 15.1 %collective-permute-start.11 = (bf16[544,256]{1,0:T(8,128)(2,1)S(1)}, bf16[544,256]{1,0:T(8,128)(2,1)S(1)}, u32[]{:S(2)}, u32[]{:S(2)}) collective-permute-start(bf16[544,256]{1,0:T(8,128)(2,1)S(1)} %get-tuple-element.203.refs_0_), channel_id=1, source_target_pairs={{0,2},{1,3},{2,0},{3,1},{4,6},{5,7},{6,4},{7,5},{8,10},{9,11},{10,... | collective-permute-start | bytes 835592 | tf_op jit(solution)/shard_map/ppermute | solution.py:1428
  80.8 29.9 %collective-permute-start.17 = (bf16[1152,512]{1,0:T(8,128)(2,1)}, bf16[1152,512]{1,0:T(8,128)(2,1)}, u32[]{:S(2)}, u32[]{:S(2)}) collective-permute-start(bf16[1152,512]{1,0:T(8,128)(2,1)} %copy-done.10), channel_id=1, source_target_pairs={{0,8},{8,0},{16,24},{24,16},{1,9},{9,1},{17,25},{25,17},{2,10},{10... | collective-permute-start | bytes 3538952 | tf_op jit(solution)/shard_map/ppermute | solution.py:1428
  82.4 18.9 %collective-permute-start.16 = (bf16[4,4,64,256]{3,2,1,0:T(8,128)(2,1)S(1)}, bf16[4,4,64,256]{3,2,1,0:T(8,128)(2,1)S(1)}, u32[]{:S(2)}, u32[]{:S(2)}) collective-permute-start(bf16[4,4,64,256]{3,2,1,0:T(8,128)(2,1)S(1)} %bitcast.146), channel_id=1, source_target_pairs={{0,4},{4,0},{1,5},{5,1},{2,6},{6,2},{3,7},{7,3},{8,12},{12,8},{9,1... | collective-permute-start | bytes 1572872 | tf_op jit(solution)/shard_map/ppermute | solution.py:1428
  84.0 17.3 %collective-permute-start.15 = (bf16[4,9,32,256]{3,2,1,0:T(8,128)(2,1)S(1)}, bf16[4,9,32,256]{3,2,1,0:T(8,128)(2,1)S(1)}, u32[]{:S(2)}, u32[]{:S(2)}) collective-permute-start(bf16[4,9,32,256]{3,2,1,0:T(8,128)(2,1)S(1)} %bitcast.133), channel_id=1, source_target_pairs={{0,16},{8,24},{16,0},{24,8},{1,17},{9,25},{17,1},{25,9},{2,18},{10... | collective-permute-start | bytes 1769480 | tf_op jit(solution)/shard_map/ppermute | solution.py:1428
  103.7 25.5 %collective-permute-start.22 = (bf16[2,4,4,64,256]{4,3,2,1,0:T(8,128)(2,1)}, bf16[2,4,4,64,256]{4,3,2,1,0:T(8,128)(2,1)S(1)}, u32[]{:S(2)}, u32[]{:S(2)}) collective-permute-start(bf16[2,4,4,64,256]{4,3,2,1,0:T(8,128)(2,1)} %get-tuple-element.226.refs_0_), channel_id=1, source_target_pairs={{0,16},{8,24},{16,0},{24,8},{1,17},{9,25},{17,1},{25,9},{2,18},{10... | collective-permute-start | bytes 3145736 | tf_op jit(solution)/shard_map/ppermute | solution.py:1428
  104.3 27.8 %collective-permute-start.21 = (bf16[2,4,9,32,256]{4,3,2,1,0:T(8,128)(2,1)S(1)}, bf16[2,4,9,32,256]{4,3,2,1,0:T(8,128)(2,1)S(1)}, u32[]{:S(2)}, u32[]{:S(2)}) collective-permute-start(bf16[2,4,9,32,256]{4,3,2,1,0:T(8,128)(2,1)S(1)} %get-tuple-element.225.refs_0_), channel_id=1, source_target_pairs={{0,4},{4,0},{1,5},{5,1},{2,6},{6,2},{3,7},{7,3},{8,12},{12,8},{9,1... | collective-permute-start | bytes 3538952 | tf_op jit(solution)/shard_map/ppermute | solution.py:1428
  124.7 24.1 %collective-permute-start.25 = (bf16[1024,1536]{1,0:T(8,128)(2,1)}, bf16[1024,1536]{1,0:T(8,128)(2,1)}, u32[]{:S(2)}, u32[]{:S(2)}) collective-permute-start(bf16[1024,1536]{1,0:T(8,128)(2,1)} %get-tuple-element.239), channel_id=1, source_target_pairs={{0,8},{8,0},{16,24},{24,16},{1,9},{9,1},{17,25},{25,17},{2,10},{10... | collective-permute-start | bytes 9437192 | tf_op jit(solution)/shard_map/ppermute | solution.py:1428
  132.6 13.8 %collective-permute-start.20 = (bf16[512,512]{1,0:T(8,128)(2,1)S(1)}, bf16[512,512]{1,0:T(8,128)(2,1)S(1)}, u32[]{:S(2)}, u32[]{:S(2)}) collective-permute-start(bf16[512,512]{1,0:T(8,128)(2,1)S(1)} %get-tuple-element.227), channel_id=1, source_target_pairs={{0,4},{4,0},{1,5},{5,1},{2,6},{6,2},{3,7},{7,3},{8,12},{12,8},{9,1... | collective-permute-start | bytes 1572872 | tf_op jit(solution)/shard_map/ppermute | solution.py:1428
  173.8 15.2 %collective-permute-start.27 = (bf16[1024,1536]{1,0:T(8,128)(2,1)S(1)}, bf16[1024,1536]{1,0:T(8,128)(2,1)S(1)}, u32[]{:S(2)}, u32[]{:S(2)}) collective-permute-start(bf16[1024,1536]{1,0:T(8,128)(2,1)S(1)} %get-tuple-element.261), channel_id=1, source_target_pairs={{0,8},{8,0},{16,24},{24,16},{1,9},{9,1},{17,25},{25,17},{2,10},{10... | collective-permute-start | bytes 9437192 | tf_op jit(solution)/shard_map/ppermute | solution.py:1428
  196.6 14.8 %collective-permute-start.28 = (bf16[512,512]{1,0:T(8,128)(2,1)S(1)}, bf16[512,512]{1,0:T(8,128)(2,1)S(1)}, u32[]{:S(2)}, u32[]{:S(2)}) collective-permute-start(bf16[512,512]{1,0:T(8,128)(2,1)S(1)} %get-tuple-element.262), channel_id=1, source_target_pairs={{0,4},{4,0},{1,5},{5,1},{2,6},{6,2},{3,7},{7,3},{8,12},{12,8},{9,1... | collective-permute-start | bytes 1572872 | tf_op jit(solution)/shard_map/ppermute | solution.py:1428
  206.0 34.3 %collective-permute-start.33 = (bf16[512,512]{1,0:T(8,128)(2,1)S(1)}, bf16[512,512]{1,0:T(8,128)(2,1)S(1)}, u32[]{:S(2)}, u32[]{:S(2)}) collective-permute-start(bf16[512,512]{1,0:T(8,128)(2,1)S(1)} %bitcast.141), channel_id=1, source_target_pairs={{0,4},{4,0},{1,5},{5,1},{2,6},{6,2},{3,7},{7,3},{8,12},{12,8},{9,1... | collective-permute-start | bytes 1572872 | tf_op jit(solution)/shard_map/ppermute | solution.py:1428
  206.6 33.2 %collective-permute-start.34 = (bf16[512,512]{1,0:T(8,128)(2,1)S(1)}, bf16[512,512]{1,0:T(8,128)(2,1)S(1)}, u32[]{:S(2)}, u32[]{:S(2)}) collective-permute-start(bf16[512,512]{1,0:T(8,128)(2,1)S(1)} %bitcast.144), channel_id=1, source_target_pairs={{0,16},{8,24},{16,0},{24,8},{1,17},{9,25},{17,1},{25,9},{2,18},{10... | collective-permute-start | bytes 1572872 | tf_op jit(solution)/shard_map/ppermute | solution.py:1428
  221.8 21.2 %collective-permute-start.31 = (bf16[1152,256]{1,0:T(8,128)(2,1)S(1)}, bf16[1152,256]{1,0:T(8,128)(2,1)S(1)}, u32[]{:S(2)}, u32[]{:S(2)}) collective-permute-start(bf16[1152,256]{1,0:T(8,128)(2,1)S(1)} %bitcast.126), channel_id=1, source_target_pairs={{0,16},{8,24},{16,0},{24,8},{1,17},{9,25},{17,1},{25,9},{2,18},{10... | collective-permute-start | bytes 1769480 | tf_op jit(solution)/shard_map/ppermute | solution.py:1428
  223.3 19.4 %collective-permute-start.32 = (bf16[1152,256]{1,0:T(8,128)(2,1)S(1)}, bf16[1152,256]{1,0:T(8,128)(2,1)S(1)}, u32[]{:S(2)}, u32[]{:S(2)}) collective-permute-start(bf16[1152,256]{1,0:T(8,128)(2,1)S(1)} %bitcast.128), channel_id=1, source_target_pairs={{0,4},{4,0},{1,5},{5,1},{2,6},{6,2},{3,7},{7,3},{8,12},{12,8},{9,1... | collective-permute-start | bytes 1769480 | tf_op jit(solution)/shard_map/ppermute | solution.py:1428
  240.6 13.9 %collective-permute-start.38 = (bf16[256,512]{1,0:T(8,128)(2,1)S(1)}, bf16[256,512]{1,0:T(8,128)(2,1)S(1)}, u32[]{:S(2)}, u32[]{:S(2)}) collective-permute-start(bf16[256,512]{1,0:T(8,128)(2,1)S(1)} %get-tuple-element.307), channel_id=1, source_target_pairs={{0,16},{8,24},{16,0},{24,8},{1,17},{9,25},{17,1},{25,9},{2,18},{10... | collective-permute-start | bytes 786440 | tf_op jit(solution)/shard_map/ppermute | solution.py:1428
  256.0 17.2 %collective-permute-start.43 = (bf16[64,512]{1,0:T(8,128)(2,1)S(1)}, bf16[64,512]{1,0:T(8,128)(2,1)S(1)}, u32[]{:S(2)}, u32[]{:S(2)}) collective-permute-start(bf16[64,512]{1,0:T(8,128)(2,1)S(1)} %get-tuple-element.319), channel_id=1, source_target_pairs={{0,4},{4,0},{1,5},{5,1},{2,6},{6,2},{3,7},{7,3},{8,12},{12,8},{9,1... | collective-permute-start | bytes 196616 | tf_op jit(solution)/shard_map/ppermute | solution.py:1428
  256.8 27.5 %collective-permute-start.44 = (bf16[544,256]{1,0:T(8,128)(2,1)S(1)}, bf16[544,256]{1,0:T(8,128)(2,1)S(1)}, u32[]{:S(2)}, u32[]{:S(2)}) collective-permute-start(bf16[544,256]{1,0:T(8,128)(2,1)S(1)} %get-tuple-element.323), channel_id=1, source_target_pairs={{0,3},{1,0},{2,1},{3,2},{4,7},{5,4},{6,5},{7,6},{8,11},{9,8},{10,9... | collective-permute-start | bytes 835592 | tf_op jit(solution)/shard_map/ppermute | solution.py:1428
  257.6 26.8 %collective-permute-start.45 = (bf16[544,256]{1,0:T(8,128)(2,1)S(1)}, bf16[544,256]{1,0:T(8,128)(2,1)S(1)}, u32[]{:S(2)}, u32[]{:S(2)}) collective-permute-start(bf16[544,256]{1,0:T(8,128)(2,1)S(1)} %get-tuple-element.324), channel_id=1, source_target_pairs={{0,2},{1,3},{2,0},{3,1},{4,6},{5,7},{6,4},{7,5},{8,10},{9,11},{10,... | collective-permute-start | bytes 835592 | tf_op jit(solution)/shard_map/ppermute | solution.py:1428
  261.9 22.5 %collective-permute-start.46 = (bf16[544,256]{1,0:T(8,128)(2,1)S(1)}, bf16[544,256]{1,0:T(8,128)(2,1)S(1)}, u32[]{:S(2)}, u32[]{:S(2)}) collective-permute-start(bf16[544,256]{1,0:T(8,128)(2,1)S(1)} %get-tuple-element.325), channel_id=1, source_target_pairs={{0,1},{1,2},{2,3},{3,0},{4,5},{5,6},{6,7},{7,4},{8,9},{9,10},{10,1... | collective-permute-start | bytes 835592 | tf_op jit(solution)/shard_map/ppermute | solution.py:1428
  272.3 16.1 %collective-permute-start.41 = (bf16[1152,256]{1,0:T(8,128)(2,1)S(1)}, bf16[1152,256]{1,0:T(8,128)(2,1)S(1)}, u32[]{:S(2)}, u32[]{:S(2)}) collective-permute-start(bf16[1152,256]{1,0:T(8,128)(2,1)S(1)} %bitcast.130), channel_id=1, source_target_pairs={{0,16},{8,24},{16,0},{24,8},{1,17},{9,25},{17,1},{25,9},{2,18},{10... | collective-permute-start | bytes 1769480 | tf_op jit(solution)/shard_map/ppermute | solution.py:1428
  273.2 14.8 %collective-permute-start.42 = (bf16[1152,256]{1,0:T(8,128)(2,1)S(1)}, bf16[1152,256]{1,0:T(8,128)(2,1)S(1)}, u32[]{:S(2)}, u32[]{:S(2)}) collective-permute-start(bf16[1152,256]{1,0:T(8,128)(2,1)S(1)} %bitcast.132), channel_id=1, source_target_pairs={{0,4},{4,0},{1,5},{5,1},{2,6},{6,2},{3,7},{7,3},{8,12},{12,8},{9,1... | collective-permute-start | bytes 1769480 | tf_op jit(solution)/shard_map/ppermute | solution.py:1428
  291.8 22.7 %collective-permute-start.52 = (bf16[512,512]{1,0:T(8,128)(2,1)S(1)}, bf16[512,512]{1,0:T(8,128)(2,1)S(1)}, u32[]{:S(2)}, u32[]{:S(2)}) collective-permute-start(bf16[512,512]{1,0:T(8,128)(2,1)S(1)} %bitcast.138), channel_id=1, source_target_pairs={{0,4},{4,0},{1,5},{5,1},{2,6},{6,2},{3,7},{7,3},{8,12},{12,8},{9,1... | collective-permute-start | bytes 1572872 | tf_op jit(solution)/shard_map/ppermute | solution.py:1428
  293.1 21.2 %collective-permute-start.53 = (bf16[512,512]{1,0:T(8,128)(2,1)S(1)}, bf16[512,512]{1,0:T(8,128)(2,1)S(1)}, u32[]{:S(2)}, u32[]{:S(2)}) collective-permute-start(bf16[512,512]{1,0:T(8,128)(2,1)S(1)} %bitcast.139), channel_id=1, source_target_pairs={{0,16},{8,24},{16,0},{24,8},{1,17},{9,25},{17,1},{25,9},{2,18},{10... | collective-permute-start | bytes 1572872 | tf_op jit(solution)/shard_map/ppermute | solution.py:1428
  302.3 15.4 %collective-permute-start.49 = (bf16[352,256]{1,0:T(8,128)(2,1)S(1)}, bf16[352,256]{1,0:T(8,128)(2,1)S(1)}, u32[]{:S(2)}, u32[]{:S(2)}) collective-permute-start(bf16[352,256]{1,0:T(8,128)(2,1)S(1)} %get-tuple-element.351), channel_id=1, source_target_pairs={{0,3},{1,0},{2,1},{3,2},{4,7},{5,4},{6,5},{7,6},{8,11},{9,8},{10,9... | collective-permute-start | bytes 540680 | tf_op jit(solution)/shard_map/ppermute | solution.py:1428
  305.0 14.4 %collective-permute-start.50 = (bf16[352,256]{1,0:T(8,128)(2,1)S(1)}, bf16[352,256]{1,0:T(8,128)(2,1)S(1)}, u32[]{:S(2)}, u32[]{:S(2)}) collective-permute-start(bf16[352,256]{1,0:T(8,128)(2,1)S(1)} %get-tuple-element.352), channel_id=1, source_target_pairs={{0,2},{1,3},{2,0},{3,1},{4,6},{5,7},{6,4},{7,5},{8,10},{9,11},{10,... | collective-permute-start | bytes 540680 | tf_op jit(solution)/shard_map/ppermute | solution.py:1428
  (90 other events, 610.4 us)

commit v3 on v2

--- a/solution.py
+++ b/solution.py
@@ -1875,9 +1875,9 @@
     ffn_late = tap.swap(ffn_late)
     grad_inputs = from_rows(stream_grad, windows)
     copies = [each for row in shared_copies(shards, across, seq) for each in row]
+    (stack,), last = restack([straight(copies)], reads=[grad_inputs] + ffn_late[1:], after=last)
+    stacks = core.gather(stack)
     grad_in, grad_out, last = finish_ffn(merged[1], ffn_late, conv_rows, ffn_rows, last)
-    (stack,), last = restack([straight(copies)], after=last)
-    stacks = core.gather(stack)
     (
         grad_conv_bias,
         grad_gains,

time: 361 us -> 365 us (1.011)
    unnamed x123 -> x149, local copies, waits for them, and re-layouts: 9.04 us -> 12.2 us
  transfers between devices with their start and end apart: 63 -> 63, of which waited for: 23 -> 24; matrix products, arithmetic and copies ran while one was open for 4% -> 4% of each run, Pallas kernels for 43% -> 42%
where the time goes in v3:
time: 365 us; the launch traced here: 362 us
  Pallas kernels  179 us (49%)
  waiting for transfers between devices  86.2 us (24%)
  starting transfers between devices  64.2 us (18%)
  local copies, waits for them, and re-layouts  27.8 us (8%)
    ppermute x60, waiting for transfers between devices, shifted(): lax.ppermute(value, self.axis, self.pairs(lambda i: (i + by) % self.size))  86.2 us
    ppermute x60, starting transfers between devices, shifted(): lax.ppermute(value, self.axis, self.pairs(lambda i: (i + by) % self.size))  60.6 us
    pallas_call x2, Pallas kernels, ffn_forward(): pl.pallas_call(kernel, grid=(steps,), in_specs=[SCALARS, whole, whole, ro...  26.2 us
    pallas_call x2, Pallas kernels, conv_forward(): pl.pallas_call(kernel, grid=(steps,), in_specs=[pl.BlockSpec(extended.sha...  23.8 us
    pallas_call x2, Pallas kernels, conv_weight_grad(): pl.pallas_call(kernel, grid_spec=pltpu.PrefetchScalarGridSpec(num_scalar_...  19.4 us
    pallas_call x2, Pallas kernels, ffn_back_hidden(): pl.pallas_call(kernel, grid=(units // block,), in_specs=[whole, whole, pl...  16.3 us
    pallas_call x2, Pallas kernels, ffn_weight_grad(): pl.pallas_call(kernel, grid=(acrosses * seqs,), in_specs=([left_spec, rig...  15.9 us
    pallas_call x2, Pallas kernels, conv_data_grad(): pl.pallas_call(kernel, grid=(steps,), in_specs=[pl.BlockSpec(extended.sha...  15.4 us
  transfers between devices with their start and end apart: 63, of which 24 were waited for; matrix products, arithmetic and copies ran while one was open for 4% of the time, Pallas kernels for 42%

profile of v3, /device:TPU:0, one launch (start us, length us, event | category | flops | bytes accessed | tf_op | source)
XLA Modules:
  0.0 361.5 jit_solution(15257806547038995479)
XLA Ops:
  5.4 5.1 %collective-permute-start.1 = (bf16[544,256]{1,0:T(8,128)(2,1)S(1)}, bf16[544,256]{1,0:T(8,128)(2,1)S(1)}, u32[]{:S(2)}, u32[]{:S(2)}) collective-permute-start(bf16[544,256]{1,0:T(8,128)(2,1)S(1)} %pad_maximum_fusion.refs_0_), channel_id=1, source_target_pairs={{0,3},{1,0},{2,1},{3,2},{4,7},{5,4},{6,5},{7,6},{8,11},{9,8},{10,9... | collective-permute-start | bytes 835592 | tf_op jit(solution)/shard_map/ppermute | solution.py:1428
  14.3 3.3 collective-permute-done.1.refs_3_
  19.9 14.3 %collective-permute-done.3.refs_2_ = bf16[544,256]{1,0:T(8,128)(2,1)S(1)} collective-permute-done((bf16[544,256]{1,0:T(8,128)(2,1)S(1)}, bf16[544,256]{1,0:T(8,128)(2,1)S(1)}, u32[]{:S(2)}, u32[]{:S(2)}) %collective-permute-start.3) | collective-permute-done | bytes 278560 | tf_op jit(solution)/shard_map/ppermute | solution.py:1428
  40.8 6.8 %collective-permute-done.6.refs_4_.refs_1_ = bf16[544,256]{1,0:T(8,128)(2,1)S(1)} collective-permute-done((bf16[544,256]{1,0:T(8,128)(2,1)S(1)}, bf16[544,256]{1,0:T(8,128)(2,1)S(1)}, u32[]{:S(2)}, u32[]{:S(2)}) %collective-permute-start.6) | collective-permute-done | bytes 278560 | tf_op jit(solution)/shard_map/ppermute | solution.py:1428
  53.9 8.6 %collective-permute-done.12.refs_6_.refs_3_ = bf16[544,256]{1,0:T(8,128)(2,1)S(1)} collective-permute-done((bf16[544,256]{1,0:T(8,128)(2,1)S(1)}, bf16[544,256]{1,0:T(8,128)(2,1)S(1)}, u32[]{:S(2)}, u32[]{:S(2)}) %collective-permute-start.12) | collective-permute-done | bytes 278560 | tf_op jit(solution)/shard_map/ppermute | solution.py:1428
  62.6 3.1 collective-permute-start.11
  65.6 12.0 %collective-permute-done.11.refs_5_.refs_2_ = bf16[544,256]{1,0:T(8,128)(2,1)S(1)} collective-permute-done((bf16[544,256]{1,0:T(8,128)(2,1)S(1)}, bf16[544,256]{1,0:T(8,128)(2,1)S(1)}, u32[]{:S(2)}, u32[]{:S(2)}) %collective-permute-start.11) | collective-permute-done | bytes 278560 | tf_op jit(solution)/shard_map/ppermute | solution.py:1428
  85.5 4.7 %place_conv.2 = (bf16[9,512,512]{2,1,0:T(8,128)(2,1)}, f32[8,128]{1,0:T(8,128)S(1)}) custom-call(s32[4]{0:T(128)S(1)} %pad_add_fusion.place_ref, bf16[2,4,9,32,256]{4,3,2,1,0:T(8,128)(2,1)S(1)} %copy-done.15, bf16[2,4,9,32,256]{4,3,2,1,0:T(8,128)(2,1)S(1)} %get-tuple-element.208.refs_1_, bf16[2,4,9,32,256]{4,3,2,1,0:T(8,128)(2,1)S(1)} %collective-permute-done.9.refs_2_, ...), custom_call_target="tpu_custom_call" | custom-call | flops 3300000000 | bytes 10500000 | tf_op jit(solution)/shard_map/place_conv/pallas_call | solution.py:1361
  90.3 11.1 %conv_forward.2 = (bf16[1024,512]{1,0:T(8,128)(2,1)}, bf16[1024,512]{1,0:T(8,128)(2,1)}, f32[1024,512]{1,0:T(8,128)}, bf16[1024,512]{1,0:T(8,128)(2,1)S(1)}, f32[8,128]{1,0:T(8,128)S(1)}) custom-call(bf16[1152,512]{1,0:T(8,128)(2,1)S(1)} %copy-done.12, bf16[9,512,512]{2,1,0:T(8,128)(2,1)} %get-tuple-element.212.weight_ref, ...), custom_call_target="tpu_custom_call" | custom-call | flops 9900000256 | bytes 31500000 | tf_op jit(solution)/shard_map/conv_forward/pallas_call | solution.py:124
  107.0 3.7 %place_ffn.2 = (bf16[2,2,4,64,512]{4,3,2,1,0:T(8,128)(2,1)}, bf16[2,2,4,64,512]{4,3,2,1,0:T(8,128)(2,1)}, bf16[2,2,4,64,512]{4,3,2,1,0:T(8,128)(2,1)}, bf16[2,2,4,64,512]{4,3,2,1,0:T(8,128)(2,1)}, f32[8,128]{1,0:T(8,128)S(1)}) custom-call(bf16[2,4,4,64,256]{4,3,2,1,0:T(8,128)(2,1)S(1)} %copy-done.17, bf16[2,4,4,64,256]{4,3,2,1,0:T(8,128)(2,1)S(1)} %copy-done.6, ...), custom_call_target="tpu_custom_call" | custom-call | flops 2200000000 | bytes 7000000 | tf_op jit(solution)/shard_map/place_ffn/pallas_call | solution.py:1408
  110.7 14.0 %ffn_forward.2 = (bf16[1024,1024]{1,0:T(8,128)(2,1)}, bf16[1024,1024]{1,0:T(8,128)(2,1)}, bf16[1024,1024]{1,0:T(8,128)(2,1)}, bf16[1024,512]{1,0:T(8,128)(2,1)},...) custom-call(s32[1]{0:T(128)} %bitcast.place_ref, ...), custom_call_target="tpu_custom_call" | custom-call | flops 12099999744 | bytes 38500000 | tf_op jit(solution)/shard_map/ffn_forward/pallas_call | solution.py:232
  124.8 4.4 %collective-permute-done.22.refs_1_ = bf16[2,4,4,64,256]{4,3,2,1,0:T(8,128)(2,1)S(1)} collective-permute-done((bf16[2,4,4,64,256]{4,3,2,1,0:T(8,128)(2,1)}, bf16[2,4,4,64,256]{4,3,2,1,0:T(8,128)(2,1)S(1)}, u32[]{:S(2)}, u32[]{:S(2)}) %collective-permute-start.22) | collective-permute-done | bytes 1048608 | tf_op jit(solution)/shard_map/ppermute | solution.py:1428
  134.9 4.6 %place_conv.3 = (bf16[9,512,512]{2,1,0:T(8,128)(2,1)}, f32[8,128]{1,0:T(8,128)S(1)}) custom-call(s32[4]{0:T(128)S(1)} %pad_add_fusion.place_ref, bf16[2,4,9,32,256]{4,3,2,1,0:T(8,128)(2,1)S(1)} %get-tuple-element.225.refs_0_, bf16[2,4,9,32,256]{4,3,2,1,0:T(8,128)(2,1)S(1)} %get-tuple-element.231.refs_1_, ...), custom_call_target="tpu_custom_call" | custom-call | flops 3300000000 | bytes 10500000 | tf_op jit(solution)/shard_map/place_conv/pallas_call | solution.py:1361
  139.6 3.6 %place_ffn.3 = (bf16[2,2,4,64,512]{4,3,2,1,0:T(8,128)(2,1)}, bf16[2,2,4,64,512]{4,3,2,1,0:T(8,128)(2,1)}, bf16[2,2,4,64,512]{4,3,2,1,0:T(8,128)(2,1)}, bf16[2,2,4,64,512]{4,3,2,1,0:T(8,128)(2,1)}, f32[8,128]{1,0:T(8,128)S(1)}) custom-call(bf16[2,4,4,64,256]{4,3,2,1,0:T(8,128)(2,1)} %get-tuple-element.226.refs_0_, ...), custom_call_target="tpu_custom_call" | custom-call | flops 2200000000 | bytes 7000000 | tf_op jit(solution)/shard_map/place_ffn/pallas_call | solution.py:1408
  143.2 3.2 collective-permute-done.20.found_ref
  148.8 12.8 %conv_forward.3 = (bf16[1024,512]{1,0:T(8,128)(2,1)}, bf16[1024,512]{1,0:T(8,128)(2,1)}, f32[1024,512]{1,0:T(8,128)}, bf16[1024,512]{1,0:T(8,128)(2,1)S(1)}, f32[8,128]{1,0:T(8,128)S(1)}) custom-call(bf16[2048,512]{1,0:T(8,128)(2,1)} %get-tuple-element.235.extended_ref.refs_0_, bf16[9,512,512]{2,1,0:T(8,128)(2,1)} %get-tuple-element.236.weight_ref, ...), custom_call_target="tpu_custom_call" | custom-call | flops 9900000256 | bytes 31500000 | tf_op jit(solution)/shard_map/conv_forward/pallas_call | solution.py:124
  161.6 12.2 %ffn_forward.3 = (bf16[1024,1024]{1,0:T(8,128)(2,1)}, bf16[1024,1024]{1,0:T(8,128)(2,1)}, bf16[1024,1024]{1,0:T(8,128)(2,1)}, bf16[1024,512]{1,0:T(8,128)(2,1)},...) custom-call(s32[1]{0:T(128)} %bitcast.place_ref, ...), custom_call_target="tpu_custom_call" | custom-call | flops 12099999744 | bytes 38500000 | tf_op jit(solution)/shard_map/ffn_forward/pallas_call | solution.py:232
  174.6 6.0 %head_and_loss.1 = (f32[1024,512]{1,0:T(8,128)S(1)}, f32[8,512]{1,0:T(8,128)S(1)}, f32[8,128]{1,0:T(8,128)S(1)}, f32[8,128]{1,0:T(8,128)S(1)}) custom-call(f32[1024,512]{1,0:T(8,128)S(1)} %get-tuple-element.248.stream_ref, f32[512,128]{1,0:T(8,128)S(1)} %pad.4.head_ref, s32[1024,128]{1,0:T(8,128)S(1)} %broadcast_in_dim.8.code_ref, ...), custom_call_target="tpu_custom_call" | custom-call | flops 6600000000 | bytes 21000000 | tf_op jit(solution)/shard_map/head_and_loss/pallas_call | solution.py:331
  180.6 8.3 %ffn_back_hidden.2 = (bf16[1024,512]{1,0:T(8,128)(2,1)S(1)}, bf16[1024,1024]{1,0:T(8,128)(2,1)}, f32[1,1024]{1,0:T(1,128)S(1)}, f32[1,1024]{1,0:T(1,128)S(1)}, b...) custom-call(f32[1024,512]{1,0:T(8,128)S(1)} %get-tuple-element.250.upstream_ref, ...), custom_call_target="tpu_custom_call" | custom-call | flops 6600000000 | bytes 21000000 | tf_op jit(solution)/shard_map/ffn_back_hidden/pallas_call | solution.py:397
  189.0 7.5 %ffn_back_stream.2 = (f32[1024,512]{1,0:T(8,128)S(1)}, bf16[1024,512]{1,0:T(8,128)(2,1)S(1)}, bf16[1024,256]{1,0:T(8,128)(2,1)S(1)}, bf16[512,512]{1,0:T(8,128)(...) custom-call(s32[2]{0:T(128)S(1)} %pad_add_fusion.1.core_ref, f32[1024,512]{1,0:T(8,128)S(1)} %get-tuple-element.250.upstream_ref, ...), custom_call_target="tpu_custom_call" | custom-call | flops 5500000256 | bytes 17500000 | tf_op jit(solution)/shard_map/ffn_back_stream/pallas_call | solution.py:505
  198.4 7.6 %ffn_weight_grad.2 = (bf16[2,2,2,64,512]{4,3,2,1,0:T(8,128)(2,1)S(1)}, bf16[2,2,2,64,512]{4,3,2,1,0:T(8,128)(2,1)S(1)}, bf16[2,2,2,64,512]{4,3,2,1,0:T(8,128)(2,...) custom-call(bf16[1024,1024]{1,0:T(8,128)(2,1)} %get-tuple-element.258.refs_0_, ...), custom_call_target="tpu_custom_call" | custom-call | flops 8800000000 | bytes 28000000 | tf_op jit(solution)/shard_map/ffn_weight_grad/pallas_call | solution.py:873
  208.0 3.4 collective-permute-done.28.found_ref
  211.6 10.2 %conv_weight_grad.2 = (bf16[2,2,9,32,256]{4,3,2,1,0:T(8,128)(2,1)S(1)}, bf16[2,2,9,32,256]{4,3,2,1,0:T(8,128)(2,1)S(1)}, bf16[2,2,9,32,256]{4,3,2,1,0:T(8,128)(2...) custom-call(s32[4]{0:T(128)S(1)} %pad_add_fusion.place_ref, ...), custom_call_target="tpu_custom_call" | custom-call | flops 9900000256 | bytes 31500000 | tf_op jit(solution)/shard_map/conv_weight_grad/pallas_call | solution.py:765
  224.0 7.7 %conv_data_grad.2 = (f32[1024,512]{1,0:T(8,128)S(1)}, f32[8,128]{1,0:T(8,128)S(1)}) custom-call(bf16[2048,512]{1,0:T(8,128)(2,1)S(1)} %get-tuple-element.268.extended_ref, bf16[9,512,512]{2,1,0:T(8,128)(2,1)} %get-tuple-element.236.weight_ref, f32[1024,512]{1,0:T(8,128)S(1)} %get-tuple-element.269.upstream_ref, f32[8,128]{1,0:T(8,128)S(1)} %get-tuple-element.272.refs_0_), custom_call_target="tpu_custom_call" | custom-call | flops 6600000000 | bytes 21000000 | tf_op jit(solution)/shard_map/conv_data_grad/pallas_call | solution.py:593
  231.7 8.1 %ffn_back_hidden.3 = (bf16[1024,512]{1,0:T(8,128)(2,1)S(1)}, bf16[1024,1024]{1,0:T(8,128)(2,1)}, f32[1,1024]{1,0:T(1,128)S(1)}, f32[1,1024]{1,0:T(1,128)S(1)}, b...) custom-call(f32[1024,512]{1,0:T(8,128)S(1)} %get-tuple-element.273.upstream_ref, ...), custom_call_target="tpu_custom_call" | custom-call | flops 6600000000 | bytes 21000000 | tf_op jit(solution)/shard_map/ffn_back_hidden/pallas_call | solution.py:397
  245.5 7.7 %ffn_back_stream.3 = (f32[1024,512]{1,0:T(8,128)S(1)}, bf16[1024,512]{1,0:T(8,128)(2,1)S(1)}, bf16[1024,256]{1,0:T(8,128)(2,1)S(1)}, bf16[1024,1536]{1,0:T(8,128...) custom-call(s32[2]{0:T(128)S(1)} %pad_add_fusion.1.core_ref, ...), custom_call_target="tpu_custom_call" | custom-call | flops 5500000256 | bytes 17500000 | tf_op jit(solution)/shard_map/ffn_back_stream/pallas_call | solution.py:505
  263.1 9.2 %conv_weight_grad.3 = (bf16[2,2,9,32,256]{4,3,2,1,0:T(8,128)(2,1)S(1)}, bf16[2,2,9,32,256]{4,3,2,1,0:T(8,128)(2,1)S(1)}, bf16[2,2,9,32,256]{4,3,2,1,0:T(8,128)(2...) custom-call(s32[4]{0:T(128)S(1)} %pad_add_fusion.place_ref, bf16[1152,512]{1,0:T(8,128)(2,1)S(1)} %copy-done.13, ...), custom_call_target="tpu_custom_call" | custom-call | flops 9900000256 | bytes 31500000 | tf_op jit(solution)/shard_map/conv_weight_grad/pallas_call | solution.py:765
  276.0 8.3 %ffn_weight_grad.3 = (bf16[2,2,2,64,512]{4,3,2,1,0:T(8,128)(2,1)S(1)}, bf16[2,2,2,64,512]{4,3,2,1,0:T(8,128)(2,1)S(1)}, bf16[2,2,2,64,512]{4,3,2,1,0:T(8,128)(2,...) custom-call(bf16[1024,1024]{1,0:T(8,128)(2,1)} %get-tuple-element.281.refs_0_, ...), custom_call_target="tpu_custom_call" | custom-call | flops 8800000000 | bytes 28000000 | tf_op jit(solution)/shard_map/ffn_weight_grad/pallas_call | solution.py:873
  284.4 3.6 %collective-permute-done.42 = bf16[1152,256]{1,0:T(8,128)(2,1)S(1)} collective-permute-done((bf16[1152,256]{1,0:T(8,128)(2,1)S(1)}, bf16[1152,256]{1,0:T(8,128)(2,1)S(1)}, u32[]{:S(2)}, u32[]{:S(2)}) %collective-permute-start.42) | collective-permute-done | bytes 589856 | tf_op jit(solution)/shard_map/ppermute | solution.py:1428
  306.6 7.7 %conv_data_grad.3 = (bf16[1024,512]{1,0:T(8,128)(2,1)S(1)}, f32[8,128]{1,0:T(8,128)S(1)}) custom-call(bf16[1152,512]{1,0:T(8,128)(2,1)S(1)} %copy-done.44, bf16[9,512,512]{2,1,0:T(8,128)(2,1)} %get-tuple-element.212.weight_ref, f32[1024,512]{1,0:T(8,128)S(1)} %copy-done.42, f32[8,128]{1,0:T(8,128)S(1)} %get-tuple-element.348.refs_0_), custom_call_target="tpu_custom_call" | custom-call | flops 6600000000 | bytes 21000000 | tf_op jit(solution)/shard_map/conv_data_grad/pallas_call | solution.py:593
  323.5 8.9 %collective-permute-done.57 = bf16[256,512]{1,0:T(8,128)(2,1)S(1)} collective-permute-done((bf16[256,512]{1,0:T(8,128)(2,1)S(1)}, bf16[256,512]{1,0:T(8,128)(2,1)S(1)}, u32[]{:S(2)}, u32[]{:S(2)}) %collective-permute-start.57) | collective-permute-done | bytes 262176 | tf_op jit(solution)/shard_map/ppermute | solution.py:1428
  354.4 6.9 %place_conv_grads.1 = f32[2,9,128,512]{3,2,1,0:T(8,128)} custom-call(s32[3]{0:T(128)S(1)} %pad_add_fusion.2.place_ref, bf16[4,20,32,256]{3,2,1,0:T(8,128)(2,1)S(1)} %bitcast.126, bf16[4,20,32,256]{3,2,1,0:T(8,128)(2,1)S(1)} %bitcast.127, bf16[4,20,32,256]{3,2,1,0:T(8,128)(2,1)} %bitcast.86.refs_2_.refs_3_, bf16[4,20,32,256]{3,2,1,0:T(8,128)(2,1)} %bitcast.86.refs_2_.refs_3_), custom_call_target="tpu_custom_call" | custom-call | flops 5500000256 | bytes 17500000 | tf_op jit(solution)/shard_map/place_conv_grads/pallas_call | solution.py:1297
  (346 shorter events, 120.0 us)
Async XLA Ops:
  10.5 23.7 %collective-permute-start.3 = (bf16[544,256]{1,0:T(8,128)(2,1)S(1)}, bf16[544,256]{1,0:T(8,128)(2,1)S(1)}, u32[]{:S(2)}, u32[]{:S(2)}) collective-permute-start(bf16[544,256]{1,0:T(8,128)(2,1)S(1)} %pad_maximum_fusion.refs_0_), channel_id=1, source_target_pairs={{0,2},{1,3},{2,0},{3,1},{4,6},{5,7},{6,4},{7,5},{8,10},{9,11},{10,... | collective-permute-start | bytes 835592 | tf_op jit(solution)/shard_map/ppermute | solution.py:1428
  10.5 23.7 %collective-permute-start.2 = (bf16[544,256]{1,0:T(8,128)(2,1)S(1)}, bf16[544,256]{1,0:T(8,128)(2,1)S(1)}, u32[]{:S(2)}, u32[]{:S(2)}) collective-permute-start(bf16[544,256]{1,0:T(8,128)(2,1)S(1)} %pad_maximum_fusion.refs_0_), channel_id=1, source_target_pairs={{0,1},{1,2},{2,3},{3,0},{4,5},{5,6},{6,7},{7,4},{8,9},{9,10},{10,1... | collective-permute-start | bytes 835592 | tf_op jit(solution)/shard_map/ppermute | solution.py:1428
  50.4 27.2 %collective-permute-start.9 = (bf16[2,4,9,32,256]{4,3,2,1,0:T(8,128)(2,1)S(1)}, bf16[2,4,9,32,256]{4,3,2,1,0:T(8,128)(2,1)S(1)}, u32[]{:S(2)}, u32[]{:S(2)}) collective-permute-start(bf16[2,4,9,32,256]{4,3,2,1,0:T(8,128)(2,1)S(1)} %get-tuple-element.205.refs_0_), channel_id=1, source_target_pairs={{0,8},{8,0},{16,24},{24,16},{1,9},{9,1},{17,25},{25,17},{2,10},{10... | collective-permute-start | bytes 3538952 | tf_op jit(solution)/shard_map/ppermute | solution.py:1428
  50.5 28.4 %collective-permute-start.7 = (bf16[2,4,9,32,256]{4,3,2,1,0:T(8,128)(2,1)S(1)}, bf16[2,4,9,32,256]{4,3,2,1,0:T(8,128)(2,1)S(1)}, u32[]{:S(2)}, u32[]{:S(2)}) collective-permute-start(bf16[2,4,9,32,256]{4,3,2,1,0:T(8,128)(2,1)S(1)} %get-tuple-element.205.refs_0_), channel_id=1, source_target_pairs={{0,4},{4,0},{1,5},{5,1},{2,6},{6,2},{3,7},{7,3},{8,12},{12,8},{9,1... | collective-permute-start | bytes 3538952 | tf_op jit(solution)/shard_map/ppermute | solution.py:1428
  52.1 25.6 %collective-permute-start.10 = (bf16[2,4,4,64,256]{4,3,2,1,0:T(8,128)(2,1)S(1)}, bf16[2,4,4,64,256]{4,3,2,1,0:T(8,128)(2,1)S(1)}, u32[]{:S(2)}, u32[]{:S(2)}) collective-permute-start(bf16[2,4,4,64,256]{4,3,2,1,0:T(8,128)(2,1)S(1)} %get-tuple-element.206.refs_0_), channel_id=1, source_target_pairs={{0,8},{8,0},{16,24},{24,16},{1,9},{9,1},{17,25},{25,17},{2,10},{10... | collective-permute-start | bytes 3145736 | tf_op jit(solution)/shard_map/ppermute | solution.py:1428
  52.2 25.4 %collective-permute-start.8 = (bf16[2,4,4,64,256]{4,3,2,1,0:T(8,128)(2,1)S(1)}, bf16[2,4,4,64,256]{4,3,2,1,0:T(8,128)(2,1)S(1)}, u32[]{:S(2)}, u32[]{:S(2)}) collective-permute-start(bf16[2,4,4,64,256]{4,3,2,1,0:T(8,128)(2,1)S(1)} %get-tuple-element.206.refs_0_), channel_id=1, source_target_pairs={{0,16},{8,24},{16,0},{24,8},{1,17},{9,25},{17,1},{25,9},{2,18},{10... | collective-permute-start | bytes 3145736 | tf_op jit(solution)/shard_map/ppermute | solution.py:1428
  62.6 15.1 %collective-permute-start.11 = (bf16[544,256]{1,0:T(8,128)(2,1)S(1)}, bf16[544,256]{1,0:T(8,128)(2,1)S(1)}, u32[]{:S(2)}, u32[]{:S(2)}) collective-permute-start(bf16[544,256]{1,0:T(8,128)(2,1)S(1)} %get-tuple-element.203.refs_0_), channel_id=1, source_target_pairs={{0,2},{1,3},{2,0},{3,1},{4,6},{5,7},{6,4},{7,5},{8,10},{9,11},{10,... | collective-permute-start | bytes 835592 | tf_op jit(solution)/shard_map/ppermute | solution.py:1428
  80.8 29.9 %collective-permute-start.17 = (bf16[1152,512]{1,0:T(8,128)(2,1)}, bf16[1152,512]{1,0:T(8,128)(2,1)}, u32[]{:S(2)}, u32[]{:S(2)}) collective-permute-start(bf16[1152,512]{1,0:T(8,128)(2,1)} %copy-done.11), channel_id=1, source_target_pairs={{0,8},{8,0},{16,24},{24,16},{1,9},{9,1},{17,25},{25,17},{2,10},{10... | collective-permute-start | bytes 3538952 | tf_op jit(solution)/shard_map/ppermute | solution.py:1428
  82.4 18.9 %collective-permute-start.16 = (bf16[4,4,64,256]{3,2,1,0:T(8,128)(2,1)S(1)}, bf16[4,4,64,256]{3,2,1,0:T(8,128)(2,1)S(1)}, u32[]{:S(2)}, u32[]{:S(2)}) collective-permute-start(bf16[4,4,64,256]{3,2,1,0:T(8,128)(2,1)S(1)} %bitcast.148), channel_id=1, source_target_pairs={{0,4},{4,0},{1,5},{5,1},{2,6},{6,2},{3,7},{7,3},{8,12},{12,8},{9,1... | collective-permute-start | bytes 1572872 | tf_op jit(solution)/shard_map/ppermute | solution.py:1428
  84.0 17.4 %collective-permute-start.15 = (bf16[4,9,32,256]{3,2,1,0:T(8,128)(2,1)S(1)}, bf16[4,9,32,256]{3,2,1,0:T(8,128)(2,1)S(1)}, u32[]{:S(2)}, u32[]{:S(2)}) collective-permute-start(bf16[4,9,32,256]{3,2,1,0:T(8,128)(2,1)S(1)} %bitcast.135), channel_id=1, source_target_pairs={{0,16},{8,24},{16,0},{24,8},{1,17},{9,25},{17,1},{25,9},{2,18},{10... | collective-permute-start | bytes 1769480 | tf_op jit(solution)/shard_map/ppermute | solution.py:1428
  103.7 25.5 %collective-permute-start.22 = (bf16[2,4,4,64,256]{4,3,2,1,0:T(8,128)(2,1)}, bf16[2,4,4,64,256]{4,3,2,1,0:T(8,128)(2,1)S(1)}, u32[]{:S(2)}, u32[]{:S(2)}) collective-permute-start(bf16[2,4,4,64,256]{4,3,2,1,0:T(8,128)(2,1)} %get-tuple-element.226.refs_0_), channel_id=1, source_target_pairs={{0,16},{8,24},{16,0},{24,8},{1,17},{9,25},{17,1},{25,9},{2,18},{10... | collective-permute-start | bytes 3145736 | tf_op jit(solution)/shard_map/ppermute | solution.py:1428
  104.3 27.8 %collective-permute-start.21 = (bf16[2,4,9,32,256]{4,3,2,1,0:T(8,128)(2,1)S(1)}, bf16[2,4,9,32,256]{4,3,2,1,0:T(8,128)(2,1)S(1)}, u32[]{:S(2)}, u32[]{:S(2)}) collective-permute-start(bf16[2,4,9,32,256]{4,3,2,1,0:T(8,128)(2,1)S(1)} %get-tuple-element.225.refs_0_), channel_id=1, source_target_pairs={{0,4},{4,0},{1,5},{5,1},{2,6},{6,2},{3,7},{7,3},{8,12},{12,8},{9,1... | collective-permute-start | bytes 3538952 | tf_op jit(solution)/shard_map/ppermute | solution.py:1428
  124.7 24.0 %collective-permute-start.25 = (bf16[1024,1536]{1,0:T(8,128)(2,1)}, bf16[1024,1536]{1,0:T(8,128)(2,1)}, u32[]{:S(2)}, u32[]{:S(2)}) collective-permute-start(bf16[1024,1536]{1,0:T(8,128)(2,1)} %get-tuple-element.239), channel_id=1, source_target_pairs={{0,8},{8,0},{16,24},{24,16},{1,9},{9,1},{17,25},{25,17},{2,10},{10... | collective-permute-start | bytes 9437192 | tf_op jit(solution)/shard_map/ppermute | solution.py:1428
  173.8 15.2 %collective-permute-start.27 = (bf16[1024,1536]{1,0:T(8,128)(2,1)S(1)}, bf16[1024,1536]{1,0:T(8,128)(2,1)S(1)}, u32[]{:S(2)}, u32[]{:S(2)}) collective-permute-start(bf16[1024,1536]{1,0:T(8,128)(2,1)S(1)} %get-tuple-element.261), channel_id=1, source_target_pairs={{0,8},{8,0},{16,24},{24,16},{1,9},{9,1},{17,25},{25,17},{2,10},{10... | collective-permute-start | bytes 9437192 | tf_op jit(solution)/shard_map/ppermute | solution.py:1428
  196.6 14.8 %collective-permute-start.28 = (bf16[512,512]{1,0:T(8,128)(2,1)S(1)}, bf16[512,512]{1,0:T(8,128)(2,1)S(1)}, u32[]{:S(2)}, u32[]{:S(2)}) collective-permute-start(bf16[512,512]{1,0:T(8,128)(2,1)S(1)} %get-tuple-element.262), channel_id=1, source_target_pairs={{0,4},{4,0},{1,5},{5,1},{2,6},{6,2},{3,7},{7,3},{8,12},{12,8},{9,1... | collective-permute-start | bytes 1572872 | tf_op jit(solution)/shard_map/ppermute | solution.py:1428
  206.0 34.4 %collective-permute-start.33 = (bf16[512,512]{1,0:T(8,128)(2,1)S(1)}, bf16[512,512]{1,0:T(8,128)(2,1)S(1)}, u32[]{:S(2)}, u32[]{:S(2)}) collective-permute-start(bf16[512,512]{1,0:T(8,128)(2,1)S(1)} %bitcast.143), channel_id=1, source_target_pairs={{0,4},{4,0},{1,5},{5,1},{2,6},{6,2},{3,7},{7,3},{8,12},{12,8},{9,1... | collective-permute-start | bytes 1572872 | tf_op jit(solution)/shard_map/ppermute | solution.py:1428
  206.6 33.2 %collective-permute-start.34 = (bf16[512,512]{1,0:T(8,128)(2,1)S(1)}, bf16[512,512]{1,0:T(8,128)(2,1)S(1)}, u32[]{:S(2)}, u32[]{:S(2)}) collective-permute-start(bf16[512,512]{1,0:T(8,128)(2,1)S(1)} %bitcast.146), channel_id=1, source_target_pairs={{0,16},{8,24},{16,0},{24,8},{1,17},{9,25},{17,1},{25,9},{2,18},{10... | collective-permute-start | bytes 1572872 | tf_op jit(solution)/shard_map/ppermute | solution.py:1428
  221.8 21.2 %collective-permute-start.31 = (bf16[1152,256]{1,0:T(8,128)(2,1)S(1)}, bf16[1152,256]{1,0:T(8,128)(2,1)S(1)}, u32[]{:S(2)}, u32[]{:S(2)}) collective-permute-start(bf16[1152,256]{1,0:T(8,128)(2,1)S(1)} %bitcast.128), channel_id=1, source_target_pairs={{0,16},{8,24},{16,0},{24,8},{1,17},{9,25},{17,1},{25,9},{2,18},{10... | collective-permute-start | bytes 1769480 | tf_op jit(solution)/shard_map/ppermute | solution.py:1428
  223.3 19.4 %collective-permute-start.32 = (bf16[1152,256]{1,0:T(8,128)(2,1)S(1)}, bf16[1152,256]{1,0:T(8,128)(2,1)S(1)}, u32[]{:S(2)}, u32[]{:S(2)}) collective-permute-start(bf16[1152,256]{1,0:T(8,128)(2,1)S(1)} %bitcast.130), channel_id=1, source_target_pairs={{0,4},{4,0},{1,5},{5,1},{2,6},{6,2},{3,7},{7,3},{8,12},{12,8},{9,1... | collective-permute-start | bytes 1769480 | tf_op jit(solution)/shard_map/ppermute | solution.py:1428
  256.0 17.2 %collective-permute-start.43 = (bf16[64,512]{1,0:T(8,128)(2,1)S(1)}, bf16[64,512]{1,0:T(8,128)(2,1)S(1)}, u32[]{:S(2)}, u32[]{:S(2)}) collective-permute-start(bf16[64,512]{1,0:T(8,128)(2,1)S(1)} %get-tuple-element.319), channel_id=1, source_target_pairs={{0,4},{4,0},{1,5},{5,1},{2,6},{6,2},{3,7},{7,3},{8,12},{12,8},{9,1... | collective-permute-start | bytes 196616 | tf_op jit(solution)/shard_map/ppermute | solution.py:1428
  256.8 27.6 %collective-permute-start.44 = (bf16[544,256]{1,0:T(8,128)(2,1)S(1)}, bf16[544,256]{1,0:T(8,128)(2,1)S(1)}, u32[]{:S(2)}, u32[]{:S(2)}) collective-permute-start(bf16[544,256]{1,0:T(8,128)(2,1)S(1)} %get-tuple-element.323), channel_id=1, source_target_pairs={{0,3},{1,0},{2,1},{3,2},{4,7},{5,4},{6,5},{7,6},{8,11},{9,8},{10,9... | collective-permute-start | bytes 835592 | tf_op jit(solution)/shard_map/ppermute | solution.py:1428
  257.6 26.8 %collective-permute-start.45 = (bf16[544,256]{1,0:T(8,128)(2,1)S(1)}, bf16[544,256]{1,0:T(8,128)(2,1)S(1)}, u32[]{:S(2)}, u32[]{:S(2)}) collective-permute-start(bf16[544,256]{1,0:T(8,128)(2,1)S(1)} %get-tuple-element.324), channel_id=1, source_target_pairs={{0,2},{1,3},{2,0},{3,1},{4,6},{5,7},{6,4},{7,5},{8,10},{9,11},{10,... | collective-permute-start | bytes 835592 | tf_op jit(solution)/shard_map/ppermute | solution.py:1428
  261.9 22.5 %collective-permute-start.46 = (bf16[544,256]{1,0:T(8,128)(2,1)S(1)}, bf16[544,256]{1,0:T(8,128)(2,1)S(1)}, u32[]{:S(2)}, u32[]{:S(2)}) collective-permute-start(bf16[544,256]{1,0:T(8,128)(2,1)S(1)} %get-tuple-element.325), channel_id=1, source_target_pairs={{0,1},{1,2},{2,3},{3,0},{4,5},{5,6},{6,7},{7,4},{8,9},{9,10},{10,1... | collective-permute-start | bytes 835592 | tf_op jit(solution)/shard_map/ppermute | solution.py:1428
  272.3 16.1 %collective-permute-start.41 = (bf16[1152,256]{1,0:T(8,128)(2,1)S(1)}, bf16[1152,256]{1,0:T(8,128)(2,1)S(1)}, u32[]{:S(2)}, u32[]{:S(2)}) collective-permute-start(bf16[1152,256]{1,0:T(8,128)(2,1)S(1)} %bitcast.132), channel_id=1, source_target_pairs={{0,16},{8,24},{16,0},{24,8},{1,17},{9,25},{17,1},{25,9},{2,18},{10... | collective-permute-start | bytes 1769480 | tf_op jit(solution)/shard_map/ppermute | solution.py:1428
  273.2 14.8 %collective-permute-start.42 = (bf16[1152,256]{1,0:T(8,128)(2,1)S(1)}, bf16[1152,256]{1,0:T(8,128)(2,1)S(1)}, u32[]{:S(2)}, u32[]{:S(2)}) collective-permute-start(bf16[1152,256]{1,0:T(8,128)(2,1)S(1)} %bitcast.134), channel_id=1, source_target_pairs={{0,4},{4,0},{1,5},{5,1},{2,6},{6,2},{3,7},{7,3},{8,12},{12,8},{9,1... | collective-permute-start | bytes 1769480 | tf_op jit(solution)/shard_map/ppermute | solution.py:1428
  291.8 22.7 %collective-permute-start.52 = (bf16[512,512]{1,0:T(8,128)(2,1)S(1)}, bf16[512,512]{1,0:T(8,128)(2,1)S(1)}, u32[]{:S(2)}, u32[]{:S(2)}) collective-permute-start(bf16[512,512]{1,0:T(8,128)(2,1)S(1)} %bitcast.140), channel_id=1, source_target_pairs={{0,4},{4,0},{1,5},{5,1},{2,6},{6,2},{3,7},{7,3},{8,12},{12,8},{9,1... | collective-permute-start | bytes 1572872 | tf_op jit(solution)/shard_map/ppermute | solution.py:1428
  293.1 21.2 %collective-permute-start.53 = (bf16[512,512]{1,0:T(8,128)(2,1)S(1)}, bf16[512,512]{1,0:T(8,128)(2,1)S(1)}, u32[]{:S(2)}, u32[]{:S(2)}) collective-permute-start(bf16[512,512]{1,0:T(8,128)(2,1)S(1)} %bitcast.141), channel_id=1, source_target_pairs={{0,16},{8,24},{16,0},{24,8},{1,17},{9,25},{17,1},{25,9},{2,18},{10... | collective-permute-start | bytes 1572872 | tf_op jit(solution)/shard_map/ppermute | solution.py:1428
  302.3 15.5 %collective-permute-start.49 = (bf16[352,256]{1,0:T(8,128)(2,1)S(1)}, bf16[352,256]{1,0:T(8,128)(2,1)S(1)}, u32[]{:S(2)}, u32[]{:S(2)}) collective-permute-start(bf16[352,256]{1,0:T(8,128)(2,1)S(1)} %get-tuple-element.351), channel_id=1, source_target_pairs={{0,3},{1,0},{2,1},{3,2},{4,7},{5,4},{6,5},{7,6},{8,11},{9,8},{10,9... | collective-permute-start | bytes 540680 | tf_op jit(solution)/shard_map/ppermute | solution.py:1428
  316.8 15.6 %collective-permute-start.57 = (bf16[256,512]{1,0:T(8,128)(2,1)S(1)}, bf16[256,512]{1,0:T(8,128)(2,1)S(1)}, u32[]{:S(2)}, u32[]{:S(2)}) collective-permute-start(bf16[256,512]{1,0:T(8,128)(2,1)S(1)} %get-tuple-element.364), channel_id=1, source_target_pairs={{0,4},{4,0},{1,5},{5,1},{2,6},{6,2},{3,7},{7,3},{8,12},{12,8},{9,1... | collective-permute-start | bytes 786440 | tf_op jit(solution)/shard_map/ppermute | solution.py:1428
  319.6 26.1 %collective-permute-start.56 = (bf16[640,256]{1,0:T(8,128)(2,1)S(1)}, bf16[640,256]{1,0:T(8,128)(2,1)S(1)}, u32[]{:S(2)}, u32[]{:S(2)}) collective-permute-start(bf16[640,256]{1,0:T(8,128)(2,1)S(1)} %get-tuple-element.362.refs_0_), channel_id=1, source_target_pairs={{0,20},{4,16},{8,28},{12,24},{16,4},{20,0},{24,12},{28,8},{1,21},{... | collective-permute-start | bytes 983048 | tf_op jit(solution)/shard_map/ppermute | solution.py:1504
  321.1 24.7 %collective-permute-start.55 = (bf16[640,256]{1,0:T(8,128)(2,1)S(1)}, bf16[640,256]{1,0:T(8,128)(2,1)S(1)}, u32[]{:S(2)}, u32[]{:S(2)}) collective-permute-start(bf16[640,256]{1,0:T(8,128)(2,1)S(1)} %get-tuple-element.362.refs_0_), channel_id=1, source_target_pairs={{0,4},{4,0},{8,12},{12,8},{16,20},{20,16},{24,28},{28,24},{1,5},{5... | collective-permute-start | bytes 983048 | tf_op jit(solution)/shard_map/ppermute | solution.py:1504
  322.3 23.4 %collective-permute-start.54 = (bf16[640,256]{1,0:T(8,128)(2,1)S(1)}, bf16[640,256]{1,0:T(8,128)(2,1)}, u32[]{:S(2)}, u32[]{:S(2)}) collective-permute-start(bf16[640,256]{1,0:T(8,128)(2,1)S(1)} %get-tuple-element.362.refs_0_), channel_id=1, source_target_pairs={{0,16},{4,20},{8,24},{12,28},{16,0},{20,4},{24,8},{28,12},{1,17},{... | collective-permute-start | bytes 983048 | tf_op jit(solution)/shard_map/ppermute | solution.py:1504
  (103 other events, 652.4 us)

commit v4 on v3

--- a/solution.py
+++ b/solution.py
@@ -1875,7 +1875,7 @@
     ffn_late = tap.swap(ffn_late)
     grad_inputs = from_rows(stream_grad, windows)
     copies = [each for row in shared_copies(shards, across, seq) for each in row]
-    (stack,), last = restack([straight(copies)], reads=[grad_inputs] + ffn_late[1:], after=last)
+    (stack,), last = restack([straight(copies)], reads=[grad_inputs], after=last)
     stacks = core.gather(stack)
     grad_in, grad_out, last = finish_ffn(merged[1], ffn_late, conv_rows, ffn_rows, last)
     (

time: 365 us -> 370 us (1.014)
  waiting for transfers between devices: 86.2 us -> 91.5 us
    ppermute x3, waiting for transfers between devices: 0.01 us -> 3.77 us  [shared_copies(): lax.ppermute(value, ('dp', 'seq'), [(place, target(place, by_a, by_s)) fo...]
    unnamed x149 -> x141, local copies, waits for them, and re-layouts: 12.2 us -> 9.04 us
  transfers between devices with their start and end apart: 63 -> 63, of which waited for: 24 -> 24; matrix products, arithmetic and copies ran while one was open for 4% -> 4% of each run, Pallas kernels for 42% -> 43%
where the time goes in v4:
time: 370 us; the launch traced here: 366 us
  Pallas kernels  182 us (49%)
  waiting for transfers between devices  91.5 us (25%)
  starting transfers between devices  64.2 us (17%)
  local copies, waits for them, and re-layouts  24.6 us (7%)
    ppermute x60, waiting for transfers between devices, shifted(): lax.ppermute(value, self.axis, self.pairs(lambda i: (i + by) % self.size))  87.7 us
    ppermute x60, starting transfers between devices, shifted(): lax.ppermute(value, self.axis, self.pairs(lambda i: (i + by) % self.size))  60.7 us
    pallas_call x2, Pallas kernels, ffn_forward(): pl.pallas_call(kernel, grid=(steps,), in_specs=[SCALARS, whole, whole, ro...  26.1 us
    pallas_call x2, Pallas kernels, conv_forward(): pl.pallas_call(kernel, grid=(steps,), in_specs=[pl.BlockSpec(extended.sha...  23.9 us
    pallas_call x2, Pallas kernels, conv_weight_grad(): pl.pallas_call(kernel, grid_spec=pltpu.PrefetchScalarGridSpec(num_scalar_...  19.4 us
    pallas_call x2, Pallas kernels, ffn_back_hidden(): pl.pallas_call(kernel, grid=(units // block,), in_specs=[whole, whole, pl...  16.3 us
    pallas_call x2, Pallas kernels, ffn_weight_grad(): pl.pallas_call(kernel, grid=(acrosses * seqs,), in_specs=([left_spec, rig...  15.9 us
    pallas_call x2, Pallas kernels, conv_data_grad(): pl.pallas_call(kernel, grid=(steps,), in_specs=[pl.BlockSpec(extended.sha...  15.4 us
  transfers between devices with their start and end apart: 63, of which 24 were waited for; matrix products, arithmetic and copies ran while one was open for 4% of the time, Pallas kernels for 43%

profile of v4, /device:TPU:0, one launch (start us, length us, event | category | flops | bytes accessed | tf_op | source)
XLA Modules:
  0.0 366.2 jit_solution(14724436467013483080)
XLA Ops:
  5.4 5.1 %collective-permute-start.1 = (bf16[544,256]{1,0:T(8,128)(2,1)S(1)}, bf16[544,256]{1,0:T(8,128)(2,1)S(1)}, u32[]{:S(2)}, u32[]{:S(2)}) collective-permute-start(bf16[544,256]{1,0:T(8,128)(2,1)S(1)} %pad_maximum_fusion.refs_0_), channel_id=1, source_target_pairs={{0,3},{1,0},{2,1},{3,2},{4,7},{5,4},{6,5},{7,6},{8,11},{9,8},{10,9... | collective-permute-start | bytes 835592 | tf_op jit(solution)/shard_map/ppermute | solution.py:1428
  14.3 3.3 collective-permute-done.1.refs_3_
  19.9 14.3 %collective-permute-done.3.refs_2_ = bf16[544,256]{1,0:T(8,128)(2,1)S(1)} collective-permute-done((bf16[544,256]{1,0:T(8,128)(2,1)S(1)}, bf16[544,256]{1,0:T(8,128)(2,1)S(1)}, u32[]{:S(2)}, u32[]{:S(2)}) %collective-permute-start.3) | collective-permute-done | bytes 278560 | tf_op jit(solution)/shard_map/ppermute | solution.py:1428
  40.8 6.8 %collective-permute-done.6.refs_4_.refs_1_ = bf16[544,256]{1,0:T(8,128)(2,1)S(1)} collective-permute-done((bf16[544,256]{1,0:T(8,128)(2,1)S(1)}, bf16[544,256]{1,0:T(8,128)(2,1)S(1)}, u32[]{:S(2)}, u32[]{:S(2)}) %collective-permute-start.6) | collective-permute-done | bytes 278560 | tf_op jit(solution)/shard_map/ppermute | solution.py:1428
  53.9 8.6 %collective-permute-done.12.refs_6_.refs_3_ = bf16[544,256]{1,0:T(8,128)(2,1)S(1)} collective-permute-done((bf16[544,256]{1,0:T(8,128)(2,1)S(1)}, bf16[544,256]{1,0:T(8,128)(2,1)S(1)}, u32[]{:S(2)}, u32[]{:S(2)}) %collective-permute-start.12) | collective-permute-done | bytes 278560 | tf_op jit(solution)/shard_map/ppermute | solution.py:1428
  65.6 12.0 %collective-permute-done.11.refs_5_.refs_2_ = bf16[544,256]{1,0:T(8,128)(2,1)S(1)} collective-permute-done((bf16[544,256]{1,0:T(8,128)(2,1)S(1)}, bf16[544,256]{1,0:T(8,128)(2,1)S(1)}, u32[]{:S(2)}, u32[]{:S(2)}) %collective-permute-start.11) | collective-permute-done | bytes 278560 | tf_op jit(solution)/shard_map/ppermute | solution.py:1428
  85.5 4.7 %place_conv.2 = (bf16[9,512,512]{2,1,0:T(8,128)(2,1)}, f32[8,128]{1,0:T(8,128)S(1)}) custom-call(s32[4]{0:T(128)S(1)} %pad_add_fusion.place_ref, bf16[2,4,9,32,256]{4,3,2,1,0:T(8,128)(2,1)S(1)} %copy-done.15, bf16[2,4,9,32,256]{4,3,2,1,0:T(8,128)(2,1)S(1)} %get-tuple-element.208.refs_1_, bf16[2,4,9,32,256]{4,3,2,1,0:T(8,128)(2,1)S(1)} %collective-permute-done.9.refs_2_, ...), custom_call_target="tpu_custom_call" | custom-call | flops 3300000000 | bytes 10500000 | tf_op jit(solution)/shard_map/place_conv/pallas_call | solution.py:1361
  90.3 11.1 %conv_forward.2 = (bf16[1024,512]{1,0:T(8,128)(2,1)}, bf16[1024,512]{1,0:T(8,128)(2,1)}, f32[1024,512]{1,0:T(8,128)}, bf16[1024,512]{1,0:T(8,128)(2,1)S(1)}, f32[8,128]{1,0:T(8,128)S(1)}) custom-call(bf16[1152,512]{1,0:T(8,128)(2,1)S(1)} %copy-done.12, bf16[9,512,512]{2,1,0:T(8,128)(2,1)} %get-tuple-element.212.weight_ref, ...), custom_call_target="tpu_custom_call" | custom-call | flops 9900000256 | bytes 31500000 | tf_op jit(solution)/shard_map/conv_forward/pallas_call | solution.py:124
  107.0 3.7 place_ffn.2
  110.7 13.9 %ffn_forward.2 = (bf16[1024,1024]{1,0:T(8,128)(2,1)}, bf16[1024,1024]{1,0:T(8,128)(2,1)}, bf16[1024,1024]{1,0:T(8,128)(2,1)}, bf16[1024,512]{1,0:T(8,128)(2,1)},...) custom-call(s32[1]{0:T(128)} %bitcast.place_ref, ...), custom_call_target="tpu_custom_call" | custom-call | flops 12099999744 | bytes 38500000 | tf_op jit(solution)/shard_map/ffn_forward/pallas_call | solution.py:232
  124.7 4.4 %collective-permute-done.22.refs_1_ = bf16[2,4,4,64,256]{4,3,2,1,0:T(8,128)(2,1)S(1)} collective-permute-done((bf16[2,4,4,64,256]{4,3,2,1,0:T(8,128)(2,1)}, bf16[2,4,4,64,256]{4,3,2,1,0:T(8,128)(2,1)S(1)}, u32[]{:S(2)}, u32[]{:S(2)}) %collective-permute-start.22) | collective-permute-done | bytes 1048608 | tf_op jit(solution)/shard_map/ppermute | solution.py:1428
  135.0 4.6 %place_conv.3 = (bf16[9,512,512]{2,1,0:T(8,128)(2,1)}, f32[8,128]{1,0:T(8,128)S(1)}) custom-call(s32[4]{0:T(128)S(1)} %pad_add_fusion.place_ref, bf16[2,4,9,32,256]{4,3,2,1,0:T(8,128)(2,1)S(1)} %get-tuple-element.225.refs_0_, bf16[2,4,9,32,256]{4,3,2,1,0:T(8,128)(2,1)S(1)} %get-tuple-element.231.refs_1_, ...), custom_call_target="tpu_custom_call" | custom-call | flops 3300000000 | bytes 10500000 | tf_op jit(solution)/shard_map/place_conv/pallas_call | solution.py:1361
  139.6 3.7 place_ffn.3
  148.8 12.8 %conv_forward.3 = (bf16[1024,512]{1,0:T(8,128)(2,1)}, bf16[1024,512]{1,0:T(8,128)(2,1)}, f32[1024,512]{1,0:T(8,128)}, bf16[1024,512]{1,0:T(8,128)(2,1)S(1)}, f32[8,128]{1,0:T(8,128)S(1)}) custom-call(bf16[2048,512]{1,0:T(8,128)(2,1)} %get-tuple-element.235.extended_ref.refs_0_, bf16[9,512,512]{2,1,0:T(8,128)(2,1)} %get-tuple-element.236.weight_ref, ...), custom_call_target="tpu_custom_call" | custom-call | flops 9900000256 | bytes 31500000 | tf_op jit(solution)/shard_map/conv_forward/pallas_call | solution.py:124
  161.6 12.2 %ffn_forward.3 = (bf16[1024,1024]{1,0:T(8,128)(2,1)}, bf16[1024,1024]{1,0:T(8,128)(2,1)}, bf16[1024,1024]{1,0:T(8,128)(2,1)}, bf16[1024,512]{1,0:T(8,128)(2,1)},...) custom-call(s32[1]{0:T(128)} %bitcast.place_ref, ...), custom_call_target="tpu_custom_call" | custom-call | flops 12099999744 | bytes 38500000 | tf_op jit(solution)/shard_map/ffn_forward/pallas_call | solution.py:232
  174.5 6.0 %head_and_loss.1 = (f32[1024,512]{1,0:T(8,128)S(1)}, f32[8,512]{1,0:T(8,128)S(1)}, f32[8,128]{1,0:T(8,128)S(1)}, f32[8,128]{1,0:T(8,128)S(1)}) custom-call(f32[1024,512]{1,0:T(8,128)S(1)} %get-tuple-element.248.stream_ref, f32[512,128]{1,0:T(8,128)S(1)} %pad.4.head_ref, s32[1024,128]{1,0:T(8,128)S(1)} %broadcast_in_dim.8.code_ref, ...), custom_call_target="tpu_custom_call" | custom-call | flops 6600000000 | bytes 21000000 | tf_op jit(solution)/shard_map/head_and_loss/pallas_call | solution.py:331
  180.6 8.3 %ffn_back_hidden.2 = (bf16[1024,512]{1,0:T(8,128)(2,1)S(1)}, bf16[1024,1024]{1,0:T(8,128)(2,1)}, f32[1,1024]{1,0:T(1,128)S(1)}, f32[1,1024]{1,0:T(1,128)S(1)}, b...) custom-call(f32[1024,512]{1,0:T(8,128)S(1)} %get-tuple-element.250.upstream_ref, ...), custom_call_target="tpu_custom_call" | custom-call | flops 6600000000 | bytes 21000000 | tf_op jit(solution)/shard_map/ffn_back_hidden/pallas_call | solution.py:397
  189.0 7.5 %ffn_back_stream.2 = (f32[1024,512]{1,0:T(8,128)S(1)}, bf16[1024,512]{1,0:T(8,128)(2,1)S(1)}, bf16[1024,256]{1,0:T(8,128)(2,1)S(1)}, bf16[512,512]{1,0:T(8,128)(...) custom-call(s32[2]{0:T(128)S(1)} %pad_add_fusion.1.core_ref, f32[1024,512]{1,0:T(8,128)S(1)} %get-tuple-element.250.upstream_ref, ...), custom_call_target="tpu_custom_call" | custom-call | flops 5500000256 | bytes 17500000 | tf_op jit(solution)/shard_map/ffn_back_stream/pallas_call | solution.py:505
  198.4 7.6 %ffn_weight_grad.2 = (bf16[2,2,2,64,512]{4,3,2,1,0:T(8,128)(2,1)S(1)}, bf16[2,2,2,64,512]{4,3,2,1,0:T(8,128)(2,1)S(1)}, bf16[2,2,2,64,512]{4,3,2,1,0:T(8,128)(2,...) custom-call(bf16[1024,1024]{1,0:T(8,128)(2,1)} %get-tuple-element.258.refs_0_, ...), custom_call_target="tpu_custom_call" | custom-call | flops 8800000000 | bytes 28000000 | tf_op jit(solution)/shard_map/ffn_weight_grad/pallas_call | solution.py:873
  208.0 3.4 collective-permute-done.28.found_ref
  211.5 10.2 %conv_weight_grad.2 = (bf16[2,2,9,32,256]{4,3,2,1,0:T(8,128)(2,1)S(1)}, bf16[2,2,9,32,256]{4,3,2,1,0:T(8,128)(2,1)S(1)}, bf16[2,2,9,32,256]{4,3,2,1,0:T(8,128)(2...) custom-call(s32[4]{0:T(128)S(1)} %pad_add_fusion.place_ref, ...), custom_call_target="tpu_custom_call" | custom-call | flops 9900000256 | bytes 31500000 | tf_op jit(solution)/shard_map/conv_weight_grad/pallas_call | solution.py:765
  223.9 7.7 %conv_data_grad.2 = (f32[1024,512]{1,0:T(8,128)S(1)}, f32[8,128]{1,0:T(8,128)S(1)}) custom-call(bf16[2048,512]{1,0:T(8,128)(2,1)S(1)} %get-tuple-element.268.extended_ref, bf16[9,512,512]{2,1,0:T(8,128)(2,1)} %get-tuple-element.236.weight_ref, f32[1024,512]{1,0:T(8,128)S(1)} %get-tuple-element.269.upstream_ref, f32[8,128]{1,0:T(8,128)S(1)} %get-tuple-element.272.refs_0_), custom_call_target="tpu_custom_call" | custom-call | flops 6600000000 | bytes 21000000 | tf_op jit(solution)/shard_map/conv_data_grad/pallas_call | solution.py:593
  231.6 8.1 %ffn_back_hidden.3 = (bf16[1024,512]{1,0:T(8,128)(2,1)S(1)}, bf16[1024,1024]{1,0:T(8,128)(2,1)}, f32[1,1024]{1,0:T(1,128)S(1)}, f32[1,1024]{1,0:T(1,128)S(1)}, b...) custom-call(f32[1024,512]{1,0:T(8,128)S(1)} %get-tuple-element.273.upstream_ref, ...), custom_call_target="tpu_custom_call" | custom-call | flops 6600000000 | bytes 21000000 | tf_op jit(solution)/shard_map/ffn_back_hidden/pallas_call | solution.py:397
  245.4 7.7 %ffn_back_stream.3 = (f32[1024,512]{1,0:T(8,128)S(1)}, bf16[1024,512]{1,0:T(8,128)(2,1)S(1)}, bf16[1024,256]{1,0:T(8,128)(2,1)S(1)}, bf16[1024,1536]{1,0:T(8,128...) custom-call(s32[2]{0:T(128)S(1)} %pad_add_fusion.1.core_ref, ...), custom_call_target="tpu_custom_call" | custom-call | flops 5500000256 | bytes 17500000 | tf_op jit(solution)/shard_map/ffn_back_stream/pallas_call | solution.py:505
  263.0 9.2 %conv_weight_grad.3 = (bf16[2,2,9,32,256]{4,3,2,1,0:T(8,128)(2,1)S(1)}, bf16[2,2,9,32,256]{4,3,2,1,0:T(8,128)(2,1)S(1)}, bf16[2,2,9,32,256]{4,3,2,1,0:T(8,128)(2...) custom-call(s32[4]{0:T(128)S(1)} %pad_add_fusion.place_ref, bf16[1152,512]{1,0:T(8,128)(2,1)S(1)} %copy-done.13, ...), custom_call_target="tpu_custom_call" | custom-call | flops 9900000256 | bytes 31500000 | tf_op jit(solution)/shard_map/conv_weight_grad/pallas_call | solution.py:765
  276.0 8.3 %ffn_weight_grad.3 = (bf16[2,2,2,64,512]{4,3,2,1,0:T(8,128)(2,1)S(1)}, bf16[2,2,2,64,512]{4,3,2,1,0:T(8,128)(2,1)S(1)}, bf16[2,2,2,64,512]{4,3,2,1,0:T(8,128)(2,...) custom-call(bf16[1024,1024]{1,0:T(8,128)(2,1)} %get-tuple-element.281.refs_0_, ...), custom_call_target="tpu_custom_call" | custom-call | flops 8800000000 | bytes 28000000 | tf_op jit(solution)/shard_map/ffn_weight_grad/pallas_call | solution.py:873
  284.3 3.6 collective-permute-done.42
  306.5 7.7 %conv_data_grad.3 = (bf16[1024,512]{1,0:T(8,128)(2,1)S(1)}, f32[8,128]{1,0:T(8,128)S(1)}) custom-call(bf16[1152,512]{1,0:T(8,128)(2,1)S(1)} %copy-done.42, bf16[9,512,512]{2,1,0:T(8,128)(2,1)} %get-tuple-element.212.weight_ref, f32[1024,512]{1,0:T(8,128)S(1)} %copy-done.40, f32[8,128]{1,0:T(8,128)S(1)} %get-tuple-element.348.refs_0_), custom_call_target="tpu_custom_call" | custom-call | flops 6600000000 | bytes 21000000 | tf_op jit(solution)/shard_map/conv_data_grad/pallas_call | solution.py:593
  327.3 5.5 %collective-permute-done.57 = bf16[256,512]{1,0:T(8,128)(2,1)} collective-permute-done((bf16[256,512]{1,0:T(8,128)(2,1)}, bf16[256,512]{1,0:T(8,128)(2,1)}, u32[]{:S(2)}, u32[]{:S(2)}) %collective-permute-start.57) | collective-permute-done | bytes 262176 | tf_op jit(solution)/shard_map/ppermute | solution.py:1428
  334.2 3.6 collective-permute-done.55.refs_2_
  346.3 8.6 %collective-permute-done.61.refs_6_ = bf16[128,512]{1,0:T(8,128)(2,1)S(1)} collective-permute-done((bf16[128,512]{1,0:T(8,128)(2,1)S(1)}, bf16[128,512]{1,0:T(8,128)(2,1)S(1)}, u32[]{:S(2)}, u32[]{:S(2)}) %collective-permute-start.61) | collective-permute-done | bytes 131104 | tf_op jit(solution)/shard_map/ppermute | solution.py:1428
  359.1 6.9 %place_conv_grads.1 = f32[2,9,128,512]{3,2,1,0:T(8,128)} custom-call(s32[3]{0:T(128)S(1)} %pad_add_fusion.2.place_ref, bf16[4,20,32,256]{3,2,1,0:T(8,128)(2,1)S(1)} %bitcast.126, bf16[4,20,32,256]{3,2,1,0:T(8,128)(2,1)S(1)} %bitcast.127, bf16[4,20,32,256]{3,2,1,0:T(8,128)(2,1)} %bitcast.86.refs_2_.refs_3_, bf16[4,20,32,256]{3,2,1,0:T(8,128)(2,1)} %bitcast.86.refs_2_.refs_3_), custom_call_target="tpu_custom_call" | custom-call | flops 5500000256 | bytes 17500000 | tf_op jit(solution)/shard_map/place_conv_grads/pallas_call | solution.py:1297
  (338 shorter events, 122.2 us)
Async XLA Ops:
  10.5 23.7 %collective-permute-start.3 = (bf16[544,256]{1,0:T(8,128)(2,1)S(1)}, bf16[544,256]{1,0:T(8,128)(2,1)S(1)}, u32[]{:S(2)}, u32[]{:S(2)}) collective-permute-start(bf16[544,256]{1,0:T(8,128)(2,1)S(1)} %pad_maximum_fusion.refs_0_), channel_id=1, source_target_pairs={{0,2},{1,3},{2,0},{3,1},{4,6},{5,7},{6,4},{7,5},{8,10},{9,11},{10,... | collective-permute-start | bytes 835592 | tf_op jit(solution)/shard_map/ppermute | solution.py:1428
  10.5 23.7 %collective-permute-start.2 = (bf16[544,256]{1,0:T(8,128)(2,1)S(1)}, bf16[544,256]{1,0:T(8,128)(2,1)S(1)}, u32[]{:S(2)}, u32[]{:S(2)}) collective-permute-start(bf16[544,256]{1,0:T(8,128)(2,1)S(1)} %pad_maximum_fusion.refs_0_), channel_id=1, source_target_pairs={{0,1},{1,2},{2,3},{3,0},{4,5},{5,6},{6,7},{7,4},{8,9},{9,10},{10,1... | collective-permute-start | bytes 835592 | tf_op jit(solution)/shard_map/ppermute | solution.py:1428
  50.4 27.2 %collective-permute-start.9 = (bf16[2,4,9,32,256]{4,3,2,1,0:T(8,128)(2,1)S(1)}, bf16[2,4,9,32,256]{4,3,2,1,0:T(8,128)(2,1)S(1)}, u32[]{:S(2)}, u32[]{:S(2)}) collective-permute-start(bf16[2,4,9,32,256]{4,3,2,1,0:T(8,128)(2,1)S(1)} %get-tuple-element.205.refs_0_), channel_id=1, source_target_pairs={{0,8},{8,0},{16,24},{24,16},{1,9},{9,1},{17,25},{25,17},{2,10},{10... | collective-permute-start | bytes 3538952 | tf_op jit(solution)/shard_map/ppermute | solution.py:1428
  50.5 28.4 %collective-permute-start.7 = (bf16[2,4,9,32,256]{4,3,2,1,0:T(8,128)(2,1)S(1)}, bf16[2,4,9,32,256]{4,3,2,1,0:T(8,128)(2,1)S(1)}, u32[]{:S(2)}, u32[]{:S(2)}) collective-permute-start(bf16[2,4,9,32,256]{4,3,2,1,0:T(8,128)(2,1)S(1)} %get-tuple-element.205.refs_0_), channel_id=1, source_target_pairs={{0,4},{4,0},{1,5},{5,1},{2,6},{6,2},{3,7},{7,3},{8,12},{12,8},{9,1... | collective-permute-start | bytes 3538952 | tf_op jit(solution)/shard_map/ppermute | solution.py:1428
  52.1 25.6 %collective-permute-start.10 = (bf16[2,4,4,64,256]{4,3,2,1,0:T(8,128)(2,1)S(1)}, bf16[2,4,4,64,256]{4,3,2,1,0:T(8,128)(2,1)S(1)}, u32[]{:S(2)}, u32[]{:S(2)}) collective-permute-start(bf16[2,4,4,64,256]{4,3,2,1,0:T(8,128)(2,1)S(1)} %get-tuple-element.206.refs_0_), channel_id=1, source_target_pairs={{0,8},{8,0},{16,24},{24,16},{1,9},{9,1},{17,25},{25,17},{2,10},{10... | collective-permute-start | bytes 3145736 | tf_op jit(solution)/shard_map/ppermute | solution.py:1428
  52.2 25.4 %collective-permute-start.8 = (bf16[2,4,4,64,256]{4,3,2,1,0:T(8,128)(2,1)S(1)}, bf16[2,4,4,64,256]{4,3,2,1,0:T(8,128)(2,1)S(1)}, u32[]{:S(2)}, u32[]{:S(2)}) collective-permute-start(bf16[2,4,4,64,256]{4,3,2,1,0:T(8,128)(2,1)S(1)} %get-tuple-element.206.refs_0_), channel_id=1, source_target_pairs={{0,16},{8,24},{16,0},{24,8},{1,17},{9,25},{17,1},{25,9},{2,18},{10... | collective-permute-start | bytes 3145736 | tf_op jit(solution)/shard_map/ppermute | solution.py:1428
  62.6 15.1 %collective-permute-start.11 = (bf16[544,256]{1,0:T(8,128)(2,1)S(1)}, bf16[544,256]{1,0:T(8,128)(2,1)S(1)}, u32[]{:S(2)}, u32[]{:S(2)}) collective-permute-start(bf16[544,256]{1,0:T(8,128)(2,1)S(1)} %get-tuple-element.203.refs_0_), channel_id=1, source_target_pairs={{0,2},{1,3},{2,0},{3,1},{4,6},{5,7},{6,4},{7,5},{8,10},{9,11},{10,... | collective-permute-start | bytes 835592 | tf_op jit(solution)/shard_map/ppermute | solution.py:1428
  80.8 29.9 %collective-permute-start.17 = (bf16[1152,512]{1,0:T(8,128)(2,1)}, bf16[1152,512]{1,0:T(8,128)(2,1)}, u32[]{:S(2)}, u32[]{:S(2)}) collective-permute-start(bf16[1152,512]{1,0:T(8,128)(2,1)} %copy-done.11), channel_id=1, source_target_pairs={{0,8},{8,0},{16,24},{24,16},{1,9},{9,1},{17,25},{25,17},{2,10},{10... | collective-permute-start | bytes 3538952 | tf_op jit(solution)/shard_map/ppermute | solution.py:1428
  82.4 19.0 %collective-permute-start.16 = (bf16[4,4,64,256]{3,2,1,0:T(8,128)(2,1)S(1)}, bf16[4,4,64,256]{3,2,1,0:T(8,128)(2,1)S(1)}, u32[]{:S(2)}, u32[]{:S(2)}) collective-permute-start(bf16[4,4,64,256]{3,2,1,0:T(8,128)(2,1)S(1)} %bitcast.148), channel_id=1, source_target_pairs={{0,4},{4,0},{1,5},{5,1},{2,6},{6,2},{3,7},{7,3},{8,12},{12,8},{9,1... | collective-permute-start | bytes 1572872 | tf_op jit(solution)/shard_map/ppermute | solution.py:1428
  84.0 17.4 %collective-permute-start.15 = (bf16[4,9,32,256]{3,2,1,0:T(8,128)(2,1)S(1)}, bf16[4,9,32,256]{3,2,1,0:T(8,128)(2,1)S(1)}, u32[]{:S(2)}, u32[]{:S(2)}) collective-permute-start(bf16[4,9,32,256]{3,2,1,0:T(8,128)(2,1)S(1)} %bitcast.135), channel_id=1, source_target_pairs={{0,16},{8,24},{16,0},{24,8},{1,17},{9,25},{17,1},{25,9},{2,18},{10... | collective-permute-start | bytes 1769480 | tf_op jit(solution)/shard_map/ppermute | solution.py:1428
  103.7 25.5 %collective-permute-start.22 = (bf16[2,4,4,64,256]{4,3,2,1,0:T(8,128)(2,1)}, bf16[2,4,4,64,256]{4,3,2,1,0:T(8,128)(2,1)S(1)}, u32[]{:S(2)}, u32[]{:S(2)}) collective-permute-start(bf16[2,4,4,64,256]{4,3,2,1,0:T(8,128)(2,1)} %get-tuple-element.226.refs_0_), channel_id=1, source_target_pairs={{0,16},{8,24},{16,0},{24,8},{1,17},{9,25},{17,1},{25,9},{2,18},{10... | collective-permute-start | bytes 3145736 | tf_op jit(solution)/shard_map/ppermute | solution.py:1428
  104.3 27.8 %collective-permute-start.21 = (bf16[2,4,9,32,256]{4,3,2,1,0:T(8,128)(2,1)S(1)}, bf16[2,4,9,32,256]{4,3,2,1,0:T(8,128)(2,1)S(1)}, u32[]{:S(2)}, u32[]{:S(2)}) collective-permute-start(bf16[2,4,9,32,256]{4,3,2,1,0:T(8,128)(2,1)S(1)} %get-tuple-element.225.refs_0_), channel_id=1, source_target_pairs={{0,4},{4,0},{1,5},{5,1},{2,6},{6,2},{3,7},{7,3},{8,12},{12,8},{9,1... | collective-permute-start | bytes 3538952 | tf_op jit(solution)/shard_map/ppermute | solution.py:1428
  124.7 24.1 %collective-permute-start.25 = (bf16[1024,1536]{1,0:T(8,128)(2,1)}, bf16[1024,1536]{1,0:T(8,128)(2,1)}, u32[]{:S(2)}, u32[]{:S(2)}) collective-permute-start(bf16[1024,1536]{1,0:T(8,128)(2,1)} %get-tuple-element.239), channel_id=1, source_target_pairs={{0,8},{8,0},{16,24},{24,16},{1,9},{9,1},{17,25},{25,17},{2,10},{10... | collective-permute-start | bytes 9437192 | tf_op jit(solution)/shard_map/ppermute | solution.py:1428
  173.8 15.2 %collective-permute-start.27 = (bf16[1024,1536]{1,0:T(8,128)(2,1)S(1)}, bf16[1024,1536]{1,0:T(8,128)(2,1)S(1)}, u32[]{:S(2)}, u32[]{:S(2)}) collective-permute-start(bf16[1024,1536]{1,0:T(8,128)(2,1)S(1)} %get-tuple-element.261), channel_id=1, source_target_pairs={{0,8},{8,0},{16,24},{24,16},{1,9},{9,1},{17,25},{25,17},{2,10},{10... | collective-permute-start | bytes 9437192 | tf_op jit(solution)/shard_map/ppermute | solution.py:1428
  196.6 14.8 %collective-permute-start.28 = (bf16[512,512]{1,0:T(8,128)(2,1)S(1)}, bf16[512,512]{1,0:T(8,128)(2,1)S(1)}, u32[]{:S(2)}, u32[]{:S(2)}) collective-permute-start(bf16[512,512]{1,0:T(8,128)(2,1)S(1)} %get-tuple-element.262), channel_id=1, source_target_pairs={{0,4},{4,0},{1,5},{5,1},{2,6},{6,2},{3,7},{7,3},{8,12},{12,8},{9,1... | collective-permute-start | bytes 1572872 | tf_op jit(solution)/shard_map/ppermute | solution.py:1428
  206.0 34.3 %collective-permute-start.33 = (bf16[512,512]{1,0:T(8,128)(2,1)S(1)}, bf16[512,512]{1,0:T(8,128)(2,1)S(1)}, u32[]{:S(2)}, u32[]{:S(2)}) collective-permute-start(bf16[512,512]{1,0:T(8,128)(2,1)S(1)} %bitcast.143), channel_id=1, source_target_pairs={{0,4},{4,0},{1,5},{5,1},{2,6},{6,2},{3,7},{7,3},{8,12},{12,8},{9,1... | collective-permute-start | bytes 1572872 | tf_op jit(solution)/shard_map/ppermute | solution.py:1428
  206.6 33.2 %collective-permute-start.34 = (bf16[512,512]{1,0:T(8,128)(2,1)S(1)}, bf16[512,512]{1,0:T(8,128)(2,1)S(1)}, u32[]{:S(2)}, u32[]{:S(2)}) collective-permute-start(bf16[512,512]{1,0:T(8,128)(2,1)S(1)} %bitcast.146), channel_id=1, source_target_pairs={{0,16},{8,24},{16,0},{24,8},{1,17},{9,25},{17,1},{25,9},{2,18},{10... | collective-permute-start | bytes 1572872 | tf_op jit(solution)/shard_map/ppermute | solution.py:1428
  221.8 21.2 %collective-permute-start.31 = (bf16[1152,256]{1,0:T(8,128)(2,1)S(1)}, bf16[1152,256]{1,0:T(8,128)(2,1)S(1)}, u32[]{:S(2)}, u32[]{:S(2)}) collective-permute-start(bf16[1152,256]{1,0:T(8,128)(2,1)S(1)} %bitcast.128), channel_id=1, source_target_pairs={{0,16},{8,24},{16,0},{24,8},{1,17},{9,25},{17,1},{25,9},{2,18},{10... | collective-permute-start | bytes 1769480 | tf_op jit(solution)/shard_map/ppermute | solution.py:1428
  223.3 19.4 %collective-permute-start.32 = (bf16[1152,256]{1,0:T(8,128)(2,1)S(1)}, bf16[1152,256]{1,0:T(8,128)(2,1)S(1)}, u32[]{:S(2)}, u32[]{:S(2)}) collective-permute-start(bf16[1152,256]{1,0:T(8,128)(2,1)S(1)} %bitcast.130), channel_id=1, source_target_pairs={{0,4},{4,0},{1,5},{5,1},{2,6},{6,2},{3,7},{7,3},{8,12},{12,8},{9,1... | collective-permute-start | bytes 1769480 | tf_op jit(solution)/shard_map/ppermute | solution.py:1428
  256.0 17.1 %collective-permute-start.43 = (bf16[64,512]{1,0:T(8,128)(2,1)S(1)}, bf16[64,512]{1,0:T(8,128)(2,1)S(1)}, u32[]{:S(2)}, u32[]{:S(2)}) collective-permute-start(bf16[64,512]{1,0:T(8,128)(2,1)S(1)} %get-tuple-element.319), channel_id=1, source_target_pairs={{0,4},{4,0},{1,5},{5,1},{2,6},{6,2},{3,7},{7,3},{8,12},{12,8},{9,1... | collective-permute-start | bytes 196616 | tf_op jit(solution)/shard_map/ppermute | solution.py:1428
  256.7 27.6 %collective-permute-start.44 = (bf16[544,256]{1,0:T(8,128)(2,1)S(1)}, bf16[544,256]{1,0:T(8,128)(2,1)S(1)}, u32[]{:S(2)}, u32[]{:S(2)}) collective-permute-start(bf16[544,256]{1,0:T(8,128)(2,1)S(1)} %get-tuple-element.323), channel_id=1, source_target_pairs={{0,3},{1,0},{2,1},{3,2},{4,7},{5,4},{6,5},{7,6},{8,11},{9,8},{10,9... | collective-permute-start | bytes 835592 | tf_op jit(solution)/shard_map/ppermute | solution.py:1428
  257.5 26.8 %collective-permute-start.45 = (bf16[544,256]{1,0:T(8,128)(2,1)S(1)}, bf16[544,256]{1,0:T(8,128)(2,1)S(1)}, u32[]{:S(2)}, u32[]{:S(2)}) collective-permute-start(bf16[544,256]{1,0:T(8,128)(2,1)S(1)} %get-tuple-element.324), channel_id=1, source_target_pairs={{0,2},{1,3},{2,0},{3,1},{4,6},{5,7},{6,4},{7,5},{8,10},{9,11},{10,... | collective-permute-start | bytes 835592 | tf_op jit(solution)/shard_map/ppermute | solution.py:1428
  261.9 22.4 %collective-permute-start.46 = (bf16[544,256]{1,0:T(8,128)(2,1)S(1)}, bf16[544,256]{1,0:T(8,128)(2,1)S(1)}, u32[]{:S(2)}, u32[]{:S(2)}) collective-permute-start(bf16[544,256]{1,0:T(8,128)(2,1)S(1)} %get-tuple-element.325), channel_id=1, source_target_pairs={{0,1},{1,2},{2,3},{3,0},{4,5},{5,6},{6,7},{7,4},{8,9},{9,10},{10,1... | collective-permute-start | bytes 835592 | tf_op jit(solution)/shard_map/ppermute | solution.py:1428
  272.2 16.1 %collective-permute-start.41 = (bf16[1152,256]{1,0:T(8,128)(2,1)S(1)}, bf16[1152,256]{1,0:T(8,128)(2,1)S(1)}, u32[]{:S(2)}, u32[]{:S(2)}) collective-permute-start(bf16[1152,256]{1,0:T(8,128)(2,1)S(1)} %bitcast.132), channel_id=1, source_target_pairs={{0,16},{8,24},{16,0},{24,8},{1,17},{9,25},{17,1},{25,9},{2,18},{10... | collective-permute-start | bytes 1769480 | tf_op jit(solution)/shard_map/ppermute | solution.py:1428
  273.1 14.8 %collective-permute-start.42 = (bf16[1152,256]{1,0:T(8,128)(2,1)S(1)}, bf16[1152,256]{1,0:T(8,128)(2,1)S(1)}, u32[]{:S(2)}, u32[]{:S(2)}) collective-permute-start(bf16[1152,256]{1,0:T(8,128)(2,1)S(1)} %bitcast.134), channel_id=1, source_target_pairs={{0,4},{4,0},{1,5},{5,1},{2,6},{6,2},{3,7},{7,3},{8,12},{12,8},{9,1... | collective-permute-start | bytes 1769480 | tf_op jit(solution)/shard_map/ppermute | solution.py:1428
  291.7 24.6 %collective-permute-start.52 = (bf16[512,512]{1,0:T(8,128)(2,1)S(1)}, bf16[512,512]{1,0:T(8,128)(2,1)S(1)}, u32[]{:S(2)}, u32[]{:S(2)}) collective-permute-start(bf16[512,512]{1,0:T(8,128)(2,1)S(1)} %bitcast.140), channel_id=1, source_target_pairs={{0,4},{4,0},{1,5},{5,1},{2,6},{6,2},{3,7},{7,3},{8,12},{12,8},{9,1... | collective-permute-start | bytes 1572872 | tf_op jit(solution)/shard_map/ppermute | solution.py:1428
  293.0 21.1 %collective-permute-start.53 = (bf16[512,512]{1,0:T(8,128)(2,1)S(1)}, bf16[512,512]{1,0:T(8,128)(2,1)S(1)}, u32[]{:S(2)}, u32[]{:S(2)}) collective-permute-start(bf16[512,512]{1,0:T(8,128)(2,1)S(1)} %bitcast.141), channel_id=1, source_target_pairs={{0,16},{8,24},{16,0},{24,8},{1,17},{9,25},{17,1},{25,9},{2,18},{10... | collective-permute-start | bytes 1572872 | tf_op jit(solution)/shard_map/ppermute | solution.py:1428
  302.3 17.6 %collective-permute-start.49 = (bf16[352,256]{1,0:T(8,128)(2,1)S(1)}, bf16[352,256]{1,0:T(8,128)(2,1)S(1)}, u32[]{:S(2)}, u32[]{:S(2)}) collective-permute-start(bf16[352,256]{1,0:T(8,128)(2,1)S(1)} %get-tuple-element.351), channel_id=1, source_target_pairs={{0,3},{1,0},{2,1},{3,2},{4,7},{5,4},{6,5},{7,6},{8,11},{9,8},{10,9... | collective-permute-start | bytes 540680 | tf_op jit(solution)/shard_map/ppermute | solution.py:1428
  305.0 14.9 %collective-permute-start.50 = (bf16[352,256]{1,0:T(8,128)(2,1)S(1)}, bf16[352,256]{1,0:T(8,128)(2,1)S(1)}, u32[]{:S(2)}, u32[]{:S(2)}) collective-permute-start(bf16[352,256]{1,0:T(8,128)(2,1)S(1)} %get-tuple-element.352), channel_id=1, source_target_pairs={{0,2},{1,3},{2,0},{3,1},{4,6},{5,7},{6,4},{7,5},{8,10},{9,11},{10,... | collective-permute-start | bytes 540680 | tf_op jit(solution)/shard_map/ppermute | solution.py:1428
  321.6 16.2 %collective-permute-start.55 = (bf16[640,256]{1,0:T(8,128)(2,1)S(1)}, bf16[640,256]{1,0:T(8,128)(2,1)S(1)}, u32[]{:S(2)}, u32[]{:S(2)}) collective-permute-start(bf16[640,256]{1,0:T(8,128)(2,1)S(1)} %get-tuple-element.362.refs_0_), channel_id=1, source_target_pairs={{0,4},{4,0},{8,12},{12,8},{16,20},{20,16},{24,28},{28,24},{1,5},{5... | collective-permute-start | bytes 983048 | tf_op jit(solution)/shard_map/ppermute | solution.py:1504
  322.7 15.2 %collective-permute-start.54 = (bf16[640,256]{1,0:T(8,128)(2,1)S(1)}, bf16[640,256]{1,0:T(8,128)(2,1)}, u32[]{:S(2)}, u32[]{:S(2)}) collective-permute-start(bf16[640,256]{1,0:T(8,128)(2,1)S(1)} %get-tuple-element.362.refs_0_), channel_id=1, source_target_pairs={{0,16},{4,20},{8,24},{12,28},{16,0},{20,4},{24,8},{28,12},{1,17},{... | collective-permute-start | bytes 983048 | tf_op jit(solution)/shard_map/ppermute | solution.py:1504
  339.0 17.7 %collective-permute-start.59 = (bf16[4,640,256]{2,1,0:T(8,128)(2,1)S(1)}, bf16[4,640,256]{2,1,0:T(8,128)(2,1)}, u32[]{:S(2)}, u32[]{:S(2)}) collective-permute-start(bf16[4,640,256]{2,1,0:T(8,128)(2,1)S(1)} %get-tuple-element.369.refs_0_), channel_id=1, source_target_pairs={{0,8},{8,0},{16,24},{24,16},{1,9},{9,1},{17,25},{25,17},{2,10},{10... | collective-permute-start | bytes 3932168 | tf_op jit(solution)/shard_map/ppermute | solution.py:1428
  (99 other events, 748.0 us)
